TPU v7x, 32 devices: a whole 2x2x4 slice. The times are simulated.
32 devices in a mesh: section: 2 (over y), mp: 4 (over x, core), dp: 4 (over z).
Axes of the slice: x: 2, y: 2, z: 4, core: 2. Of those that a mesh axis runs over, the one named last changes fastest.
Arguments:
- saved_inputs: bfloat16 [2, 8, 512, 8192], P('section', None, 'dp', 'mp'), may hold values from -40 to 40
- cotangent: bfloat16 [8, 512, 8192], P(None, 'dp', 'mp'), may hold values from -6 to 6
- weight_in: bfloat16 [2, 8192, 512], P('section', 'mp', 'dp'), may hold values from -0.0625 to 0.0625
- weight_out: bfloat16 [2, 8192, 512], P('section', 'mp', 'dp'), may hold values from -0.25 to 0.25
- gain: float32 [2, 8192], P(None, 'mp'), may hold values from 0.1 to 1.9
- plan: int32 [8], replicated, may hold values from 0 to 7, each once
Outputs:
- grad_in: float32 [2, 8192, 512], P('section', 'mp', 'dp')
- grad_out: float32 [2, 8192, 512], P('section', 'mp', 'dp')
- input_grads: bfloat16 [2, 8, 512, 8192], P('section', None, 'dp', 'mp')
All inputs are finite; a program needn't handle non-finite values.
Results may differ from a plain program's by a relative error of at most 0.02.
Values may be sent and summed in bfloat16 or wider, within the bound.
No kernel may reach another device: no remote copies, remote signals or barrier semaphores. Data moves between devices by JAX's collectives and lax.ppermute only.
A program may use at most 128 MiB of HBM per device.

v0:
```python
import jax
import jax.numpy as jnp
from jax import lax
from jax.sharding import PartitionSpec as P

D = 8192


EPS = 1e-05


def from_partner(block, axis, bit):
    count = lax.axis_size(axis)
    route = []
    for low in range(count):
        high = low | 1 << bit
        if high != low and high < count:
            route += [(low, high), (high, low)]
    return lax.ppermute(block, axis, route)


def shifted(array, axis, by):
    count = lax.axis_size(axis)
    pairs = [(i, i + by) for i in range(count) if 0 <= i + by < count]
    return lax.ppermute(array, axis, pairs)


def per_device(saved_inputs, cotangent, weight_in, weight_out, gain, plan):
    section_count = lax.axis_size("section")
    own_section = lax.axis_index("section")
    flip_count = section_count.bit_length() - 1
    slot_count = cotangent.shape[0]
    half_slots = slot_count // 2
    own_weights = jnp.stack((weight_in[0], weight_out[0]))
    mirrored = own_weights
    for bit_index in range(flip_count):
        mirrored = from_partner(mirrored, "section", bit_index)
    gathered = lax.all_gather(jnp.concatenate((own_weights, mirrored), 0), "dp", axis=2, tiled=True)
    in_own, out_own, in_up, out_up = (gathered[0], gathered[1], gathered[2], gathered[3])
    mirror_section = section_count - 1 - own_section
    gain_own = lax.dynamic_index_in_dim(gain, own_section, 0, keepdims=False)
    gain_up = lax.dynamic_index_in_dim(gain, mirror_section, 0, keepdims=False)
    stored = saved_inputs[0]
    stored_wide = stored.astype(jnp.float32)
    feature_count = gain_own.shape[0]
    slot_gains = jnp.concatenate(
        (
            jnp.broadcast_to(gain_own, (half_slots, 1, feature_count)),
            jnp.broadcast_to(gain_up, (slot_count - half_slots, 1, feature_count)),
        ),
        0,
    )
    normed = (stored_wide * slot_gains).astype(jnp.bfloat16)
    part_down = jnp.einsum(
        "krd,de->kre", normed[:half_slots], in_own, preferred_element_type=jnp.float32
    )
    part_up = jnp.einsum(
        "krd,de->kre", normed[half_slots:], in_up, preferred_element_type=jnp.float32
    )
    unit_sums, square_sums = (
        lax.psum(jnp.concatenate((part_down, part_up), 0).astype(jnp.bfloat16), "mp").astype(
            jnp.float32
        ),
        lax.psum(jnp.sum(stored_wide * stored_wide, axis=-1).astype(jnp.bfloat16), "mp").astype(
            jnp.float32
        ),
    )
    inverse_rms = lax.rsqrt(square_sums / D + EPS)[..., None]
    hidden_pre = inverse_rms * unit_sums

    def unit_partial(incoming, out_full, live):
        return lax.cond(
            live,
            lambda: jnp.dot(incoming, out_full, preferred_element_type=jnp.float32),
            lambda: jnp.zeros((incoming.shape[0], out_full.shape[1]), jnp.float32),
        )

    def finish(live, slot, incoming, unit_grads, gain_row, in_full, total_in, total_out):

        def active():
            stored_slot = lax.dynamic_index_in_dim(stored_wide, slot, 0, keepdims=False)
            normed_slot = lax.dynamic_index_in_dim(normed, slot, 0, keepdims=False)
            sums_slot = lax.dynamic_index_in_dim(unit_sums, slot, 0, keepdims=False)
            rms_slot = lax.dynamic_index_in_dim(inverse_rms, slot, 0, keepdims=False)
            pre_slot = lax.dynamic_index_in_dim(hidden_pre, slot, 0, keepdims=False)
            sigma = jax.nn.sigmoid(pre_slot)
            grad_hidden = unit_grads * sigma * (1.0 + pre_slot * (1.0 - sigma))
            scaled_grad = (rms_slot * grad_hidden).astype(jnp.bfloat16)
            activated = jax.nn.silu(pre_slot).astype(jnp.bfloat16)
            back_proj = lax.dot_general(
                scaled_grad, in_full, (((1,), (1,)), ((), ())), preferred_element_type=jnp.float32
            )
            rms_term = jnp.sum(grad_hidden * sums_slot, axis=-1, keepdims=True)
            result = (
                incoming.astype(jnp.float32)
                + gain_row * back_proj
                - rms_slot**3 / D * rms_term * stored_slot
            )
            grad_in_part = lax.dot_general(
                normed_slot,
                scaled_grad,
                (((0,), (0,)), ((), ())),
                preferred_element_type=jnp.float32,
            )
            grad_out_part = lax.dot_general(
                incoming, activated, (((0,), (0,)), ((), ())), preferred_element_type=jnp.float32
            )
            return (result.astype(jnp.bfloat16), total_in + grad_in_part, total_out + grad_out_part)

        def resting():
            return (jnp.zeros_like(incoming), total_in, total_out)

        return lax.cond(live, active, resting)

    step_count = section_count - 1 + half_slots

    def advance(step_index, loop_state):
        (
            from_above,
            from_below,
            in_down_total,
            out_down_total,
            in_up_total,
            out_up_total,
            outputs,
        ) = loop_state
        pos_down = step_index - (section_count - 1 - own_section)
        live_down = (pos_down >= 0) & (pos_down < half_slots)
        slot_down = jnp.clip(pos_down, 0, half_slots - 1)
        pos_up = step_index - own_section
        live_up = (pos_up >= 0) & (pos_up < half_slots)
        slot_up = half_slots + jnp.clip(pos_up, 0, half_slots - 1)
        top_down = lax.dynamic_index_in_dim(cotangent, plan[slot_down], 0, keepdims=False)
        top_up = lax.dynamic_index_in_dim(cotangent, plan[slot_up], 0, keepdims=False)
        grad_down = jnp.where(own_section == section_count - 1, top_down, from_above)
        grad_up = jnp.where(own_section == 0, top_up, from_below)
        units_down, units_up = (
            lax.psum(unit_partial(grad_down, out_own, live_down).astype(jnp.bfloat16), "mp").astype(
                jnp.float32
            ),
            lax.psum(unit_partial(grad_up, out_up, live_up).astype(jnp.bfloat16), "mp").astype(
                jnp.float32
            ),
        )
        result_down, in_down_total, out_down_total = finish(
            live_down,
            slot_down,
            grad_down,
            units_down,
            gain_own,
            in_own,
            in_down_total,
            out_down_total,
        )
        result_up, in_up_total, out_up_total = finish(
            live_up, slot_up, grad_up, units_up, gain_up, in_up, in_up_total, out_up_total
        )
        next_above = shifted(result_down, "section", -1)
        next_below = shifted(result_up, "section", 1)
        outputs = jnp.where(
            live_down, lax.dynamic_update_index_in_dim(outputs, result_down, slot_down, 0), outputs
        )
        outputs = jnp.where(
            live_up, lax.dynamic_update_index_in_dim(outputs, result_up, slot_up, 0), outputs
        )
        return (
            next_above,
            next_below,
            in_down_total,
            out_down_total,
            in_up_total,
            out_up_total,
            outputs,
        )

    zero_grad = jnp.zeros_like(stored[0])
    zero_total = jnp.zeros((in_own.shape[0], in_own.shape[1]), jnp.float32)
    initial = (
        zero_grad,
        zero_grad,
        zero_total,
        zero_total,
        zero_total,
        zero_total,
        jnp.zeros_like(stored),
    )
    final_state = lax.fori_loop(0, step_count, advance, initial)
    in_down_total, out_down_total, in_up_total, out_up_total, outputs = (
        final_state[2],
        final_state[3],
        final_state[4],
        final_state[5],
        final_state[6],
    )
    up_totals = jnp.stack((in_up_total, out_up_total))
    for bit_index in range(flip_count):
        up_totals = from_partner(up_totals.astype(jnp.bfloat16), "section", bit_index).astype(
            up_totals.dtype
        )
    reduced = lax.psum_scatter(
        (jnp.stack((in_down_total, out_down_total)) + up_totals).astype(jnp.bfloat16),
        "dp",
        scatter_dimension=2,
        tiled=True,
    ).astype(jnp.float32)
    return (reduced[0][None], reduced[1][None], outputs[None])


def solution(mesh):
    in_specs = (
        P("section", None, "dp", "mp"),
        P(None, "dp", "mp"),
        P("section", "mp", "dp"),
        P("section", "mp", "dp"),
        P(None, "mp"),
        P(),
    )
    out_specs = (P("section", "mp", "dp"), P("section", "mp", "dp"), P("section", None, "dp", "mp"))
    return jax.shard_map(
        per_device, mesh=mesh, in_specs=in_specs, out_specs=out_specs, check_vma=False
    )
```

profile of v0, /device:TPU:0, one launch (start us, length us, event | category | flops | bytes accessed | tf_op | source)
XLA Modules:
  0.0 881.7 jit_solution(15023520132768106705)
XLA Ops:
  11.6 23.2 %collective-permute-done.2 = bf16[2,2048,128]{2,1,0:T(8,128)(2,1)S(1)} collective-permute-done((bf16[2,2048,128]{2,1,0:T(8,128)(2,1)S(1)}, bf16[2,2048,128]{2,1,0:T(8,128)(2,1)S(1)}, u32[]{:S(2)}, u32[]{:S(2)}) %collective-permute-start.2) | collective-permute-done | bytes 1048608 | tf_op jit(solution)/shard_map/ppermute | solution.py:19
  55.6 132.6 %all-gather.2.cloned.1.call-done = bf16[4,2048,512]{2,1,0:T(8,128)(2,1)} async-done(((bf16[4,2048,128]{2,1,0:T(8,128)(2,1)}), bf16[4,2048,512]{2,1,0:T(8,128)(2,1)}) %all-gather.2.cloned.1.call-update) | async-done | bytes 8388624 | tf_op jit(solution)/shard_map/all_gather | solution.py:38
  201.6 28.7 %all-reduce.6.cloned.1.call-done = bf16[8,128,512]{2,1,0:T(8,128)(2,1)} async-done(((bf16[8,128,512]{2,1,0:T(8,128)(2,1)}), bf16[8,128,512]{2,1,0:T(8,128)(2,1)}) %all-reduce.6.cloned.1.call-update) | async-done | bytes 1048592 | tf_op jit(solution)/shard_map/psum | solution.py:61
  250.1 417.3 %while.27 = (s32[]{:T(128)}, bf16[128,2048]{1,0:T(8,128)(2,1)}, bf16[128,2048]{1,0:T(8,128)(2,1)}, f32[2048,512]{1,0:T(8,128)}, f32[2048,512]{0,1:T(8,128)}, /*i...) while((s32[]{:T(128)}, bf16[128,2048]{1,0:T(8,128)(2,1)}, ...), condition=%wide.region_16.17_spmd, body=%wide.region_3.16_spmd.sunk | while | flops 2160984832 | bytes 209745904 | solution.py:187
  257.3 34.2 %all-reduce.8.cloned.1.call-done = (bf16[128,512]{1,0:T(8,128)(2,1)}, bf16[128,512]{1,0:T(8,128)(2,1)}) async-done(((bf16[128,512]{1,0:T(8,128)(2,1)}, bf16[128,512]{1,0:T(8,128)(2,1)}), (bf16[128,512]{1,0:T(8,128)(2,1)}, bf16[128,512]{1,0:T(8,128)(2,1)})) %all-reduce.8.cloned.1.call-update) | async-done | bytes 262160 | tf_op jit(solution)/shard_map/while/body/eval_jaxpr/psum | solution.py:138
  291.6 13.9 %conditional.11 = (bf16[128,2048]{1,0:T(8,128)(2,1)}, f32[2048,512]{1,0:T(8,128)}, f32[2048,512]{0,1:T(8,128)}, bf16[1,128,2048]{2,1,0:T(8,128)(2,1)}) conditional(s32[]{:T(128)} %convert_element_type.163, (f32[2048,512]{1,0:T(8,128)}, f32[2048,512]{0,1:T(8,128)}) %tuple.102, (bf16[128,2048]{1,0:T(8,128)(2,1)S(1)}, f32[2048]{0:T(1024)S(1)}, ...), branch_computations={%region_13.13_spmd, %region_14.15_spmd} | conditional | flops 811467136 | bytes 92420312 | solution.py:113
  332.7 32.2 %all-reduce.8.cloned.1.call-done = (bf16[128,512]{1,0:T(8,128)(2,1)}, bf16[128,512]{1,0:T(8,128)(2,1)}) async-done(((bf16[128,512]{1,0:T(8,128)(2,1)}, bf16[128,512]{1,0:T(8,128)(2,1)}), (bf16[128,512]{1,0:T(8,128)(2,1)}, bf16[128,512]{1,0:T(8,128)(2,1)})) %all-reduce.8.cloned.1.call-update) | async-done | bytes 262160 | tf_op jit(solution)/shard_map/while/body/eval_jaxpr/psum | solution.py:138
  364.9 13.9 %conditional.11 = (bf16[128,2048]{1,0:T(8,128)(2,1)}, f32[2048,512]{1,0:T(8,128)}, f32[2048,512]{0,1:T(8,128)}, bf16[1,128,2048]{2,1,0:T(8,128)(2,1)}) conditional(s32[]{:T(128)} %convert_element_type.163, (f32[2048,512]{1,0:T(8,128)}, f32[2048,512]{0,1:T(8,128)}) %tuple.102, (bf16[128,2048]{1,0:T(8,128)(2,1)S(1)}, f32[2048]{0:T(1024)S(1)}, ...), branch_computations={%region_13.13_spmd, %region_14.15_spmd} | conditional | flops 811467136 | bytes 92420312 | solution.py:113
  383.0 11.8 %conditional.10 = (bf16[128,2048]{1,0:T(8,128)(2,1)S(1)}, f32[2048,512]{1,0:T(8,128)}, f32[2048,512]{0,1:T(8,128)}, bf16[1,128,2048]{2,1,0:T(8,128)(2,1)}) conditional(s32[]{:T(128)} %convert_element_type.162, (f32[2048,512]{1,0:T(8,128)}, f32[2048,512]{0,1:T(8,128)}) %tuple.96, (bf16[128,2048]{1,0:T(8,128)(2,1)S(1)}, f32[2048]{0:T(1024)S(1)}, ...), branch_computations={%region_7.7_spmd, %region_8.9_spmd} | conditional | flops 811467136 | bytes 96090360 | solution.py:113
  400.3 8.8 collective-permute-done
  419.1 31.8 %all-reduce.8.cloned.1.call-done = (bf16[128,512]{1,0:T(8,128)(2,1)}, bf16[128,512]{1,0:T(8,128)(2,1)}) async-done(((bf16[128,512]{1,0:T(8,128)(2,1)}, bf16[128,512]{1,0:T(8,128)(2,1)}), (bf16[128,512]{1,0:T(8,128)(2,1)}, bf16[128,512]{1,0:T(8,128)(2,1)})) %all-reduce.8.cloned.1.call-update) | async-done | bytes 262160 | tf_op jit(solution)/shard_map/while/body/eval_jaxpr/psum | solution.py:138
  450.9 13.9 %conditional.11 = (bf16[128,2048]{1,0:T(8,128)(2,1)}, f32[2048,512]{1,0:T(8,128)}, f32[2048,512]{0,1:T(8,128)}, bf16[1,128,2048]{2,1,0:T(8,128)(2,1)}) conditional(s32[]{:T(128)} %convert_element_type.163, (f32[2048,512]{1,0:T(8,128)}, f32[2048,512]{0,1:T(8,128)}) %tuple.102, (bf16[128,2048]{1,0:T(8,128)(2,1)S(1)}, f32[2048]{0:T(1024)S(1)}, ...), branch_computations={%region_13.13_spmd, %region_14.15_spmd} | conditional | flops 811467136 | bytes 92420312 | solution.py:113
  469.0 11.8 %conditional.10 = (bf16[128,2048]{1,0:T(8,128)(2,1)S(1)}, f32[2048,512]{1,0:T(8,128)}, f32[2048,512]{0,1:T(8,128)}, bf16[1,128,2048]{2,1,0:T(8,128)(2,1)}) conditional(s32[]{:T(128)} %convert_element_type.162, (f32[2048,512]{1,0:T(8,128)}, f32[2048,512]{0,1:T(8,128)}) %tuple.96, (bf16[128,2048]{1,0:T(8,128)(2,1)S(1)}, f32[2048]{0:T(1024)S(1)}, ...), branch_computations={%region_7.7_spmd, %region_8.9_spmd} | conditional | flops 811467136 | bytes 96090360 | solution.py:113
  486.3 8.8 collective-permute-done
  505.1 31.8 %all-reduce.8.cloned.1.call-done = (bf16[128,512]{1,0:T(8,128)(2,1)}, bf16[128,512]{1,0:T(8,128)(2,1)}) async-done(((bf16[128,512]{1,0:T(8,128)(2,1)}, bf16[128,512]{1,0:T(8,128)(2,1)}), (bf16[128,512]{1,0:T(8,128)(2,1)}, bf16[128,512]{1,0:T(8,128)(2,1)})) %all-reduce.8.cloned.1.call-update) | async-done | bytes 262160 | tf_op jit(solution)/shard_map/while/body/eval_jaxpr/psum | solution.py:138
  536.9 13.9 %conditional.11 = (bf16[128,2048]{1,0:T(8,128)(2,1)}, f32[2048,512]{1,0:T(8,128)}, f32[2048,512]{0,1:T(8,128)}, bf16[1,128,2048]{2,1,0:T(8,128)(2,1)}) conditional(s32[]{:T(128)} %convert_element_type.163, (f32[2048,512]{1,0:T(8,128)}, f32[2048,512]{0,1:T(8,128)}) %tuple.102, (bf16[128,2048]{1,0:T(8,128)(2,1)S(1)}, f32[2048]{0:T(1024)S(1)}, ...), branch_computations={%region_13.13_spmd, %region_14.15_spmd} | conditional | flops 811467136 | bytes 92420312 | solution.py:113
  555.0 11.8 %conditional.10 = (bf16[128,2048]{1,0:T(8,128)(2,1)S(1)}, f32[2048,512]{1,0:T(8,128)}, f32[2048,512]{0,1:T(8,128)}, bf16[1,128,2048]{2,1,0:T(8,128)(2,1)}) conditional(s32[]{:T(128)} %convert_element_type.162, (f32[2048,512]{1,0:T(8,128)}, f32[2048,512]{0,1:T(8,128)}) %tuple.96, (bf16[128,2048]{1,0:T(8,128)(2,1)S(1)}, f32[2048]{0:T(1024)S(1)}, ...), branch_computations={%region_7.7_spmd, %region_8.9_spmd} | conditional | flops 811467136 | bytes 96090360 | solution.py:113
  590.7 31.8 %all-reduce.8.cloned.1.call-done = (bf16[128,512]{1,0:T(8,128)(2,1)}, bf16[128,512]{1,0:T(8,128)(2,1)}) async-done(((bf16[128,512]{1,0:T(8,128)(2,1)}, bf16[128,512]{1,0:T(8,128)(2,1)}), (bf16[128,512]{1,0:T(8,128)(2,1)}, bf16[128,512]{1,0:T(8,128)(2,1)})) %all-reduce.8.cloned.1.call-update) | async-done | bytes 262160 | tf_op jit(solution)/shard_map/while/body/eval_jaxpr/psum | solution.py:138
  624.2 16.4 %collective-permute-start.1 = (bf16[128,2048]{1,0:T(8,128)(2,1)}, bf16[128,2048]{1,0:T(8,128)(2,1)}, u32[]{:S(2)}, u32[]{:S(2)}) collective-permute-start(bf16[128,2048]{1,0:T(8,128)(2,1)} %get-tuple-element.978), channel_id=1, source_target_pairs={{0,16},{1,17},{2,18},{3,19},{4,20},{5,21},{6,22},{7,23},{8,24},{9,... | collective-permute-start | bytes 1572872 | tf_op jit(solution)/shard_map/while/body/eval_jaxpr/ppermute | solution.py:25
  640.6 11.8 %conditional.10 = (bf16[128,2048]{1,0:T(8,128)(2,1)S(1)}, f32[2048,512]{1,0:T(8,128)}, f32[2048,512]{0,1:T(8,128)}, bf16[1,128,2048]{2,1,0:T(8,128)(2,1)}) conditional(s32[]{:T(128)} %convert_element_type.162, (f32[2048,512]{1,0:T(8,128)}, f32[2048,512]{0,1:T(8,128)}) %tuple.96, (bf16[128,2048]{1,0:T(8,128)(2,1)S(1)}, f32[2048]{0:T(1024)S(1)}, ...), branch_computations={%region_7.7_spmd, %region_8.9_spmd} | conditional | flops 811467136 | bytes 96090360 | solution.py:113
  657.7 8.9 %collective-permute-done = bf16[128,2048]{1,0:T(8,128)(2,1)S(1)} collective-permute-done((bf16[128,2048]{1,0:T(8,128)(2,1)S(1)}, bf16[128,2048]{1,0:T(8,128)(2,1)S(1)}, u32[]{:S(2)}, u32[]{:S(2)}) %collective-permute-start) | collective-permute-done | bytes 524320 | tf_op jit(solution)/shard_map/while/body/eval_jaxpr/ppermute | solution.py:25
  683.8 85.1 %collective-permute-done.3 = bf16[2,2048,512]{2,1,0:T(8,128)(2,1)} collective-permute-done((bf16[2,2048,512]{2,1,0:T(8,128)(2,1)}, bf16[2,2048,512]{2,1,0:T(8,128)(2,1)}, u32[]{:S(2)}, u32[]{:S(2)}) %collective-permute-start.3) | collective-permute-done | bytes 4194336 | tf_op jit(solution)/shard_map/ppermute | solution.py:19
  775.7 11.3 %copy.17 = bf16[2,2048,512]{1,0,2:T(2,128)(2,1)} copy(bf16[2,2048,512]{2,1,0:T(8,128)(2,1)} %fusion.44) | data formatting | bytes 8388608
  793.7 76.9 %reduce-scatter.4.cloned.1.call-done = bf16[128,4096]{1,0:T(8,128)(2,1)} async-done(((bf16[512,4096]{1,0:T(8,128)(2,1)}), bf16[128,4096]{1,0:T(8,128)(2,1)}) %reduce-scatter.4.cloned.1.call-update) | async-done | bytes 1048592
  (294 shorter events, 297.7 us)
Async XLA Ops:
  7.2 30.4 %copy-start.17 = (f32[2,2048]{1,0:T(2,128)S(1)}, f32[2,2048]{1,0:T(2,128)}, u32[]{:S(2)}) copy-start(f32[2,2048]{1,0:T(2,128)} %param.20) | copy-start | bytes 49156
  7.2 181.0 %all-gather.2.cloned.1.call-start = ((), (), s32[]{:S(2)}) async-start(), calls=%async_computation.1 | async-start | bytes 10485760 | tf_op jit(solution)/shard_map/all_gather | solution.py:38
  8.5 26.2 %collective-permute-start.2 = (bf16[2,2048,128]{2,1,0:T(8,128)(2,1)S(1)}, bf16[2,2048,128]{2,1,0:T(8,128)(2,1)S(1)}, u32[]{:S(2)}, u32[]{:S(2)}) collective-permute-start(bf16[2,2048,128]{2,1,0:T(8,128)(2,1)S(1)} %pad_maximum_fusion.2), channel_id=1, source_target_pairs={{0,16},{16,0},{1,17},{17,1},{2,18},{18,2},{3,19},{19,3},{4,20},{20... | collective-permute-start | bytes 3145736 | tf_op jit(solution)/shard_map/ppermute | solution.py:19
  37.5 192.8 %all-reduce.6.cloned.1.call-start = ((), (), s32[]{:S(2)}) async-start(), calls=%async_computation.2 | async-start | bytes 2097152 | tf_op jit(solution)/shard_map/psum | solution.py:61
  250.1 41.5 %all-reduce.8.cloned.1.call-start = ((), (), s32[]{:S(2)}) async-start(), calls=%async_computation.4 | async-start | bytes 524288 | tf_op jit(solution)/shard_map/while/body/eval_jaxpr/psum | solution.py:138
  305.5 11.6 %collective-permute-start.1 = (bf16[128,2048]{1,0:T(8,128)(2,1)}, bf16[128,2048]{1,0:T(8,128)(2,1)}, u32[]{:S(2)}, u32[]{:S(2)}) collective-permute-start(bf16[128,2048]{1,0:T(8,128)(2,1)} %get-tuple-element.978), channel_id=1, source_target_pairs={{0,16},{1,17},{2,18},{3,19},{4,20},{5,21},{6,22},{7,23},{8,24},{9,... | collective-permute-start | bytes 1572872 | tf_op jit(solution)/shard_map/while/body/eval_jaxpr/ppermute | solution.py:25
  308.5 14.1 %collective-permute-start = (bf16[128,2048]{1,0:T(8,128)(2,1)S(1)}, bf16[128,2048]{1,0:T(8,128)(2,1)S(1)}, u32[]{:S(2)}, u32[]{:S(2)}) collective-permute-start(bf16[128,2048]{1,0:T(8,128)(2,1)S(1)} %get-tuple-element.976), channel_id=1, source_target_pairs={{16,0},{17,1},{18,2},{19,3},{20,4},{21,5},{22,6},{23,7},{24,8},{25... | collective-permute-start | bytes 1572872 | tf_op jit(solution)/shard_map/while/body/eval_jaxpr/ppermute | solution.py:25
  323.4 41.5 %all-reduce.8.cloned.1.call-start = ((), (), s32[]{:S(2)}) async-start(), calls=%async_computation.4 | async-start | bytes 524288 | tf_op jit(solution)/shard_map/while/body/eval_jaxpr/psum | solution.py:138
  364.9 18.1 %copy-start.12 = (bf16[128,512]{1,0:T(8,128)(2,1)S(1)}, bf16[128,512]{1,0:T(8,128)(2,1)}, u32[]{:S(2)}) copy-start(bf16[128,512]{1,0:T(8,128)(2,1)} %get-tuple-element.975) | copy-start | bytes 393220 | tf_op jit(solution)/shard_map/while
  378.8 21.5 %collective-permute-start.1 = (bf16[128,2048]{1,0:T(8,128)(2,1)}, bf16[128,2048]{1,0:T(8,128)(2,1)}, u32[]{:S(2)}, u32[]{:S(2)}) collective-permute-start(bf16[128,2048]{1,0:T(8,128)(2,1)} %get-tuple-element.978), channel_id=1, source_target_pairs={{0,16},{1,17},{2,18},{3,19},{4,20},{5,21},{6,22},{7,23},{8,24},{9,... | collective-permute-start | bytes 1572872 | tf_op jit(solution)/shard_map/while/body/eval_jaxpr/ppermute | solution.py:25
  394.8 14.3 %collective-permute-start = (bf16[128,2048]{1,0:T(8,128)(2,1)S(1)}, bf16[128,2048]{1,0:T(8,128)(2,1)S(1)}, u32[]{:S(2)}, u32[]{:S(2)}) collective-permute-start(bf16[128,2048]{1,0:T(8,128)(2,1)S(1)} %get-tuple-element.976), channel_id=1, source_target_pairs={{16,0},{17,1},{18,2},{19,3},{20,4},{21,5},{22,6},{23,7},{24,8},{25... | collective-permute-start | bytes 1572872 | tf_op jit(solution)/shard_map/while/body/eval_jaxpr/ppermute | solution.py:25
  409.9 41.1 %all-reduce.8.cloned.1.call-start = ((), (), s32[]{:S(2)}) async-start(), calls=%async_computation.4 | async-start | bytes 524288 | tf_op jit(solution)/shard_map/while/body/eval_jaxpr/psum | solution.py:138
  464.8 21.5 %collective-permute-start.1 = (bf16[128,2048]{1,0:T(8,128)(2,1)}, bf16[128,2048]{1,0:T(8,128)(2,1)}, u32[]{:S(2)}, u32[]{:S(2)}) collective-permute-start(bf16[128,2048]{1,0:T(8,128)(2,1)} %get-tuple-element.978), channel_id=1, source_target_pairs={{0,16},{1,17},{2,18},{3,19},{4,20},{5,21},{6,22},{7,23},{8,24},{9,... | collective-permute-start | bytes 1572872 | tf_op jit(solution)/shard_map/while/body/eval_jaxpr/ppermute | solution.py:25
  480.8 14.3 %collective-permute-start = (bf16[128,2048]{1,0:T(8,128)(2,1)S(1)}, bf16[128,2048]{1,0:T(8,128)(2,1)S(1)}, u32[]{:S(2)}, u32[]{:S(2)}) collective-permute-start(bf16[128,2048]{1,0:T(8,128)(2,1)S(1)} %get-tuple-element.976), channel_id=1, source_target_pairs={{16,0},{17,1},{18,2},{19,3},{20,4},{21,5},{22,6},{23,7},{24,8},{25... | collective-permute-start | bytes 1572872 | tf_op jit(solution)/shard_map/while/body/eval_jaxpr/ppermute | solution.py:25
  495.9 41.0 %all-reduce.8.cloned.1.call-start = ((), (), s32[]{:S(2)}) async-start(), calls=%async_computation.4 | async-start | bytes 524288 | tf_op jit(solution)/shard_map/while/body/eval_jaxpr/psum | solution.py:138
  536.9 18.1 %copy-start.12 = (bf16[128,512]{1,0:T(8,128)(2,1)S(1)}, bf16[128,512]{1,0:T(8,128)(2,1)}, u32[]{:S(2)}) copy-start(bf16[128,512]{1,0:T(8,128)(2,1)} %get-tuple-element.975) | copy-start | bytes 393220 | tf_op jit(solution)/shard_map/while
  550.8 21.5 %collective-permute-start.1 = (bf16[128,2048]{1,0:T(8,128)(2,1)}, bf16[128,2048]{1,0:T(8,128)(2,1)}, u32[]{:S(2)}, u32[]{:S(2)}) collective-permute-start(bf16[128,2048]{1,0:T(8,128)(2,1)} %get-tuple-element.978), channel_id=1, source_target_pairs={{0,16},{1,17},{2,18},{3,19},{4,20},{5,21},{6,22},{7,23},{8,24},{9,... | collective-permute-start | bytes 1572872 | tf_op jit(solution)/shard_map/while/body/eval_jaxpr/ppermute | solution.py:25
  566.8 14.3 %collective-permute-start = (bf16[128,2048]{1,0:T(8,128)(2,1)S(1)}, bf16[128,2048]{1,0:T(8,128)(2,1)S(1)}, u32[]{:S(2)}, u32[]{:S(2)}) collective-permute-start(bf16[128,2048]{1,0:T(8,128)(2,1)S(1)} %get-tuple-element.976), channel_id=1, source_target_pairs={{16,0},{17,1},{18,2},{19,3},{20,4},{21,5},{22,6},{23,7},{24,8},{25... | collective-permute-start | bytes 1572872 | tf_op jit(solution)/shard_map/while/body/eval_jaxpr/ppermute | solution.py:25
  581.8 40.6 %all-reduce.8.cloned.1.call-start = ((), (), s32[]{:S(2)}) async-start(), calls=%async_computation.4 | async-start | bytes 524288 | tf_op jit(solution)/shard_map/while/body/eval_jaxpr/psum | solution.py:138
  622.5 18.1 %copy-start.12 = (bf16[128,512]{1,0:T(8,128)(2,1)S(1)}, bf16[128,512]{1,0:T(8,128)(2,1)}, u32[]{:S(2)}) copy-start(bf16[128,512]{1,0:T(8,128)(2,1)} %get-tuple-element.975) | copy-start | bytes 393220 | tf_op jit(solution)/shard_map/while
  624.2 33.6 %collective-permute-start.1 = (bf16[128,2048]{1,0:T(8,128)(2,1)}, bf16[128,2048]{1,0:T(8,128)(2,1)}, u32[]{:S(2)}, u32[]{:S(2)}) collective-permute-start(bf16[128,2048]{1,0:T(8,128)(2,1)} %get-tuple-element.978), channel_id=1, source_target_pairs={{0,16},{1,17},{2,18},{3,19},{4,20},{5,21},{6,22},{7,23},{8,24},{9,... | collective-permute-start | bytes 1572872 | tf_op jit(solution)/shard_map/while/body/eval_jaxpr/ppermute | solution.py:25
  652.3 14.3 %collective-permute-start = (bf16[128,2048]{1,0:T(8,128)(2,1)S(1)}, bf16[128,2048]{1,0:T(8,128)(2,1)S(1)}, u32[]{:S(2)}, u32[]{:S(2)}) collective-permute-start(bf16[128,2048]{1,0:T(8,128)(2,1)S(1)} %get-tuple-element.976), channel_id=1, source_target_pairs={{16,0},{17,1},{18,2},{19,3},{20,4},{21,5},{22,6},{23,7},{24,8},{25... | collective-permute-start | bytes 1572872 | tf_op jit(solution)/shard_map/while/body/eval_jaxpr/ppermute | solution.py:25
  667.4 203.1 %reduce-scatter.4.cloned.1.call-start = ((), (), s32[]{:S(2)}) async-start(), calls=%async_computation.3 | async-start | bytes 5242880
  678.4 90.4 %collective-permute-start.3 = (bf16[2,2048,512]{2,1,0:T(8,128)(2,1)}, bf16[2,2048,512]{2,1,0:T(8,128)(2,1)}, u32[]{:S(2)}, u32[]{:S(2)}) collective-permute-start(bf16[2,2048,512]{2,1,0:T(8,128)(2,1)} %pad_maximum_fusion), channel_id=1, source_target_pairs={{0,16},{16,0},{1,17},{17,1},{2,18},{18,2},{3,19},{19,3},{4,20},{20... | collective-permute-start | bytes 12582920 | tf_op jit(solution)/shard_map/ppermute | solution.py:19
  (63 other events, 221.8 us)
Sparse Core Ops, SparseCore 0:
  37.6 150.5 all-gather.1
  195.9 34.2 all-reduce.5
  257.5 34.0 all-reduce.7
  332.8 32.0 all-reduce.7
  419.2 31.6 all-reduce.7
  505.3 31.5 all-reduce.7
  590.8 31.6 all-reduce.7
  793.8 76.6 reduce-scatter.3
where the time goes:
time: 884 us; the launch traced here: 882 us
  waiting for transfers between devices  552 us (62%)
  local copies, waits for them, and re-layouts  93.6 us (11%)
  matrix products  79.3 us (9%)
  other arithmetic  75.5 us (9%)
  starting transfers between devices  40.6 us (5%)
  loops' own time  20.4 us (2%)
  between operations  14.2 us (2%)
    psum x5, waiting for transfers between devices, advance(): lax.psum(unit_partial(grad_down, out_own, live_down).astype(jnp.bfloat16)...  162 us
    all_gather x1, waiting for transfers between devices, per_device(): lax.all_gather(jnp.concatenate((own_weights, mirrored), 0), 'dp', axis=2,...  133 us
    ppermute x2, waiting for transfers between devices, from_partner(): return lax.ppermute(block, axis, route)  108 us
    unnamed x4, waiting for transfers between devices  76.9 us
    ppermute x10, waiting for transfers between devices, shifted(): return lax.ppermute(array, axis, pairs)  43.9 us
    ppermute x10, starting transfers between devices, shifted(): return lax.ppermute(array, axis, pairs)  37.5 us
    psum x1, waiting for transfers between devices, per_device(): lax.psum(jnp.concatenate((part_down, part_up), 0).astype(jnp.bfloat16), '...  28.7 us
    cond x96, local copies, waits for them, and re-layouts  28.2 us
  transfers between devices with their start and end apart: 20, of which 16 were waited for; matrix products, arithmetic and copies ran while one was open for 10% of the time, Pallas kernels for 0%

commit v1 on v0

v1 whole, which is shorter than its diff:
```python
import jax
import jax.numpy as jnp
from jax import lax
from jax.sharding import PartitionSpec as P

EPS = 1e-05
F32 = jnp.float32
BF16 = jnp.bfloat16
PAD = 128


def rotate(block, shift):
    count = lax.axis_size("dp")
    return lax.ppermute(block, "dp", [(i, (i + shift) % count) for i in range(count)])


def gather_units(block):
    count = lax.axis_size("dp")
    return jnp.concatenate([block] + [rotate(block, -k) for k in range(1, count)], axis=-1)


def scatter_units(total):
    count = lax.axis_size("dp")
    width = total.shape[-1] // count
    parts = total.astype(BF16)
    kept = total[..., :width].astype(F32)
    for k in range(1, count):
        kept = kept + rotate(parts[..., k * width : (k + 1) * width], k).astype(F32)
    return kept


def swap_section(block):
    return lax.ppermute(block, "section", [(0, 1), (1, 0)])


def swap_core(block):
    return lax.ppermute(block, "mp", [(i, i ^ 1) for i in range(4)])


def swap_chip(block):
    return lax.ppermute(block, "mp", [(i, i ^ 2) for i in range(4)])


def swap_both(block):
    pairs = [(i, (i ^ 4) ^ 2) for i in range(8)]
    return lax.ppermute(block, ("section", "mp"), pairs)


def pick(array, index, axis):
    return lax.dynamic_index_in_dim(array, index, axis, keepdims=False)


def ordered(first, second, flipped, axis):
    return jnp.where(
        flipped,
        jnp.concatenate((second, first), axis),
        jnp.concatenate((first, second), axis),
    )


def pair_sum(partial):
    mp_index = lax.axis_index("mp")
    core, chip = mp_index % 2, mp_index // 2
    sets, slots, tokens, width = partial.shape
    parts = partial.reshape(sets, slots // 2, 2, tokens, width)
    narrow = parts.astype(BF16)
    mine = pick(parts, core, 2).astype(F32) + swap_core(pick(narrow, 1 - core, 2)).astype(F32)
    sent = mine.astype(BF16)
    total = pick(mine[0], chip, 0)
    total = total + swap_chip(pick(sent[0], 1 - chip, 0)).astype(F32)
    total = total + swap_section(pick(sent[1], chip, 0)).astype(F32)
    total = total + swap_both(pick(sent[1], 1 - chip, 0)).astype(F32)
    return total


def pair_spread(block):
    mp_index = lax.axis_index("mp")
    core, chip = mp_index % 2, mp_index // 2
    tokens, width = block.shape
    own = ordered(block[None], swap_chip(block)[None], chip == 1, 0)
    received = ordered(swap_section(block)[None], swap_both(block)[None], chip == 1, 0)
    mine = jnp.stack((own, received))
    both = ordered(mine[:, :, None], swap_core(mine)[:, :, None], core == 1, 2)
    return both.reshape(2, 4, tokens, width)


def any_sum(partial):
    sets, slots, tokens, width = partial.shape
    count = lax.axis_size("section") * lax.axis_size("mp")
    rows = partial.astype(BF16).reshape(count, sets * slots * tokens // count, width)
    moved = lax.all_to_all(rows, ("section", "mp"), 0, 0)
    return jnp.sum(moved.astype(F32), axis=0)


def any_spread(block, sets, slots, tokens):
    whole = lax.all_gather(block, ("section", "mp"), axis=0, tiled=True)
    return whole.reshape(sets, slots, tokens, block.shape[-1])


def row_terms(unit_sums, square_sums, features):
    inverse_rms = lax.rsqrt(square_sums / features + EPS)
    hidden_pre = inverse_rms * unit_sums
    sigma = jax.nn.sigmoid(hidden_pre)
    activated = (hidden_pre * sigma).astype(BF16)
    return inverse_rms, hidden_pre, sigma, activated


def unit_terms(unit_grads, unit_sums, inverse_rms, hidden_pre, sigma, features):
    grad_hidden = unit_grads * sigma * (1.0 + hidden_pre * (1.0 - sigma))
    scaled_grad = (inverse_rms * grad_hidden).astype(BF16)
    rms_term = jnp.sum(grad_hidden * unit_sums, axis=-1, keepdims=True)
    factor = inverse_rms**3 / features * rms_term
    return scaled_grad, factor


def project(rows, weights):
    return jnp.einsum("jktd,de->jkte", rows, weights, preferred_element_type=F32)


def accumulate(rows, units):
    return jnp.einsum("jktd,jkte->de", rows, units, preferred_element_type=F32)


def run_phase(stored, incoming, in_full, out_full, gain_row, features, sum_units, spread_units):
    units = in_full.shape[-1]
    wide = stored.astype(F32)
    normed = (wide * gain_row).astype(BF16)
    squares = jnp.sum(wide * wide, axis=-1, keepdims=True)
    part = project(normed, in_full)
    packed = jnp.concatenate((part, jnp.broadcast_to(squares, part.shape[:-1] + (PAD,))), axis=-1)
    hidden = sum_units(packed)
    unit_sums, square_sums = hidden[:, :units], hidden[:, units : units + 1]
    inverse_rms, hidden_pre, sigma, activated = row_terms(unit_sums, square_sums, features)
    activated = spread_units(activated)
    unit_grads = sum_units(project(incoming, out_full))
    scaled_grad, factor = unit_terms(
        unit_grads, unit_sums, inverse_rms, hidden_pre, sigma, features
    )
    factor = jnp.broadcast_to(factor.astype(BF16), (factor.shape[0], PAD))
    spread = spread_units(jnp.concatenate((scaled_grad, factor), axis=-1))
    scaled_grad, factor = spread[..., :units], spread[..., units : units + 1].astype(F32)
    back = jnp.einsum("jkte,de->jktd", scaled_grad, in_full, preferred_element_type=F32)
    result = (incoming.astype(F32) + gain_row * back - factor * wide).astype(BF16)
    return result, accumulate(normed, scaled_grad), accumulate(incoming, activated)


def two_sections(saved_inputs, cotangent, weight_in, weight_out, gain, plan):
    own = lax.axis_index("section")
    other = 1 - own
    stored = saved_inputs[0]
    slots, tokens, width = stored.shape
    half, part = slots // 2, width // 2
    features = width * lax.axis_size("mp")

    def columns(array, section):
        return lax.dynamic_slice_in_dim(array, section * part, part, array.ndim - 1)

    def rows(array, section):
        return lax.dynamic_slice_in_dim(array, section * part, part, 0)

    mine = jnp.stack((rows(weight_in[0], own), rows(weight_out[0], own)))
    moved = swap_section(jnp.stack((rows(weight_in[0], other), rows(weight_out[0], other))))
    sent_slots = [half * other, half * own]
    blocks = []
    for phase in range(2):
        local = lax.dynamic_slice_in_dim(stored, sent_slots[phase], half, 0)
        blocks.append((columns(local, own), swap_section(columns(local, other))))
    top = columns(cotangent, own)

    def chosen(start):
        return jnp.stack([pick(top, plan[start + i], 0) for i in range(half)])

    incoming = jnp.stack((chosen(sent_slots[0]), chosen(sent_slots[1])))
    outputs = jnp.zeros_like(stored)
    in_blocks = [None, None]
    out_blocks = [None, None]
    for phase in range(2):
        group = 1 - phase
        held = jnp.where(own == group, mine, moved)
        in_full = gather_units(held[0])
        out_full = gather_units(held[1])
        gain_row = columns(gain[group], own)
        result, in_total, out_total = run_phase(
            jnp.stack(blocks[phase]),
            incoming,
            in_full,
            out_full,
            gain_row,
            features,
            pair_sum,
            pair_spread,
        )
        in_blocks[phase] = scatter_units(in_total)
        out_blocks[phase] = scatter_units(out_total)
        returned = swap_section(result[1])
        outputs = lax.dynamic_update_slice(
            outputs, result[0], (sent_slots[phase], 0, own * part)
        )
        outputs = lax.dynamic_update_slice(
            outputs, returned, (sent_slots[phase], 0, other * part)
        )
        incoming = jnp.stack((result[1], result[0]))

    def whole(by_phase):
        kept = jnp.where(own == 1, by_phase[0], by_phase[1])
        given = jnp.where(own == 1, by_phase[1], by_phase[0]).astype(BF16)
        return ordered(kept, swap_section(given).astype(F32), own == 1, 0)

    return (whole(in_blocks)[None], whole(out_blocks)[None], outputs[None])


def any_sections(saved_inputs, cotangent, weight_in, weight_out, gain, plan):
    count = lax.axis_size("section")
    own = lax.axis_index("section")
    stored = saved_inputs[0]
    slots, tokens, width = stored.shape
    half, part = slots // 2, width // count
    features = width * lax.axis_size("mp")
    units = weight_in.shape[-1]

    def split_columns(array):
        return jnp.moveaxis(array.reshape(array.shape[:-1] + (count, part)), -2, 0)

    def moved(array):
        return lax.all_to_all(array, "section", 0, 0)

    inputs = moved(split_columns(stored))
    ins = moved(weight_in[0].reshape(count, part, units))
    outs = moved(weight_out[0].reshape(count, part, units))
    gains = pick(split_columns(gain), own, 0)
    top = lax.dynamic_slice_in_dim(cotangent, own * part, part, 2)
    incoming = jnp.stack([pick(top, plan[i], 0) for i in range(slots)])
    incoming = incoming.reshape(2, half, tokens, part)
    results = [[None, None] for _ in range(count)]
    in_blocks = [None] * count
    out_blocks = [None] * count
    for phase in range(count):
        group = count - 1 - phase
        result, in_total, out_total = run_phase(
            jnp.stack((inputs[group, :half], inputs[phase, half:])),
            incoming,
            gather_units(ins[group]),
            gather_units(outs[group]),
            gains[group],
            features,
            any_sum,
            lambda block: any_spread(block, 2, half, tokens),
        )
        in_blocks[group] = scatter_units(in_total)
        out_blocks[group] = scatter_units(out_total)
        results[group][0] = result[0]
        results[phase][1] = result[1]
        incoming = result

    def whole(blocks):
        return moved(jnp.stack(blocks).astype(BF16)).astype(F32).reshape(width, units)

    outputs = moved(jnp.stack([jnp.concatenate(pair) for pair in results]))
    outputs = jnp.moveaxis(outputs, 0, -2).reshape(stored.shape)
    return (whole(in_blocks)[None], whole(out_blocks)[None], outputs[None])


def solution(mesh):
    in_specs = (
        P("section", None, "dp", "mp"),
        P(None, "dp", "mp"),
        P("section", "mp", "dp"),
        P("section", "mp", "dp"),
        P(None, "mp"),
        P(),
    )
    out_specs = (P("section", "mp", "dp"), P("section", "mp", "dp"), P("section", None, "dp", "mp"))
    paired = mesh.shape["section"] == 2 and mesh.shape["mp"] == 4
    return jax.shard_map(
        two_sections if paired else any_sections,
        mesh=mesh,
        in_specs=in_specs,
        out_specs=out_specs,
        check_vma=False,
    )
```

time: 884 us -> 354 us (0.40)
  waiting for transfers between devices: 552 us -> 136 us
  starting transfers between devices: 40.6 us -> 97.3 us
  local copies, waits for them, and re-layouts: 93.6 us -> 39.3 us
  other arithmetic: 75.5 us -> 24.1 us
  matrix products: 79.3 us -> 34.1 us
  loops' own time: 20.4 us -> 0 us
    psum x6 -> x0, waiting for transfers between devices: 190 us -> none  [the longest x5 162 us: advance(): lax.psum(unit_partial(grad_down, out_own, live_down).astype(jnp.bfloat16)...]
    all_gather x1 -> x0, waiting for transfers between devices: 133 us -> none  [per_device(): lax.all_gather(jnp.concatenate((own_weights, mirrored), 0), 'dp', axis=2,...]
    unnamed x4 -> x0, waiting for transfers between devices: 76.9 us -> none
    ppermute x12 -> x63, starting transfers between devices: 40.5 us -> 97.3 us  [the longest x24 60.5 us: rotate(): lax.ppermute(block, 'dp', [(i, (i + shift) % count) for i in range(count)])]
    dot_general x34 -> x10, matrix products: 79.3 us -> 34.1 us  [the longest x4 15.4 us: accumulate(): return jnp.einsum('jktd,jkte->de', rows, units, preferred_element_type=F32)]
    cond x96 -> x0, local copies, waits for them, and re-layouts: 28.2 us -> none
    select_n x15, other arithmetic: 28.3 us -> 6.9 us  [the longest x14 5.78 us: ordered(): jnp.where(flipped, jnp.concatenate((second, first), axis), jnp.concatenat...]
    another operation x21 -> x0, loops' own time: 20.4 us -> none  [the longest x1 19.6 us: per_device(): final_state = lax.fori_loop(0, step_count, advance, initial)]
  transfers between devices with their start and end apart: 20 -> 63, of which waited for: 16 -> 25; matrix products, arithmetic and copies ran while one was open for 10% -> 26% of each run, Pallas kernels for 0% -> 0%
where the time goes in v1:
time: 354 us; the launch traced here: 348 us
  waiting for transfers between devices  136 us (38%)
  starting transfers between devices  97.3 us (27%)
  local copies, waits for them, and re-layouts  39.3 us (11%)
  matrix products  34.1 us (10%)
  other arithmetic  24.1 us (7%)
  between operations  16.8 us (5%)
    ppermute x24, waiting for transfers between devices, rotate(): lax.ppermute(block, 'dp', [(i, (i + shift) % count) for i in range(count)])  68.2 us
    ppermute x24, starting transfers between devices, rotate(): lax.ppermute(block, 'dp', [(i, (i + shift) % count) for i in range(count)])  60.5 us
    ppermute x15, waiting for transfers between devices, swap_section(): return lax.ppermute(block, 'section', [(0, 1), (1, 0)])  53.1 us
    dot_general x4, matrix products, accumulate(): return jnp.einsum('jktd,jkte->de', rows, units, preferred_element_type=F32)  15.4 us
    ppermute x15, starting transfers between devices, swap_section(): return lax.ppermute(block, 'section', [(0, 1), (1, 0)])  15.4 us
    ppermute x8, starting transfers between devices, swap_both(): return lax.ppermute(block, ('section', 'mp'), pairs)  13.1 us
    squeeze x25, local copies, waits for them, and re-layouts, pick(): return lax.dynamic_index_in_dim(array, index, axis, keepdims=False)  12 us
    ppermute x8, waiting for transfers between devices, swap_both(): return lax.ppermute(block, ('section', 'mp'), pairs)  11.6 us
  transfers between devices with their start and end apart: 63, of which 25 were waited for; matrix products, arithmetic and copies ran while one was open for 26% of the time, Pallas kernels for 0%

profile of v1, /device:TPU:0, one launch (start us, length us, event | category | flops | bytes accessed | tf_op | source)
XLA Modules:
  0.0 347.9 jit_solution(17822047454456293537)
XLA Ops:
  5.0 5.8 %constant_dynamic-slice_fusion.10 = (bf16[1,4,128,1024]{3,2,1,0:T(8,128)(2,1)S(1)}, bf16[4,128,1024]{2,1,0:T(8,128)(2,1)}, bf16[1,4,128,1024]{3,2,1,0:T(8,128)(2,1)S(1)}, bf16[4,128,1024]{2,1,0:T(8,128)(2,1)}) fusion(bf16[1,8,128,2048]{3,2,1,0:T(8,128)(2,1)} %param.6, s32[]{:T(128)S(6)} %select_n.407, s32[]{:T(128)S(6)} %select_n.371, s32[]{:T(128)S(6)} %select_n.369, ...), kind=kLoop, calls=%fused_computation.163 | loop fusion | bytes 8388624 | tf_op jit(solution)/shard_map/dynamic_slice | solution.py:156
  34.1 3.7 %collective-permute-start.17 = (bf16[1024,128]{1,0:T(8,128)(2,1)S(1)}, bf16[1024,128]{1,0:T(8,128)(2,1)S(1)}, u32[]{:S(2)}, u32[]{:S(2)}) collective-permute-start(bf16[1024,128]{1,0:T(8,128)(2,1)S(1)} %get-tuple-element.67), channel_id=1, source_target_pairs={{0,3},{1,0},{2,1},{3,2},{4,7},{5,4},{6,5},{7,6},{8,11},{9,8},{10,9... | collective-permute-start | bytes 786440 | tf_op jit(solution)/shard_map/ppermute | solution.py:14
  39.6 5.0 %collective-permute-done.17 = bf16[1024,128]{1,0:T(8,128)(2,1)S(1)} collective-permute-done((bf16[1024,128]{1,0:T(8,128)(2,1)S(1)}, bf16[1024,128]{1,0:T(8,128)(2,1)S(1)}, u32[]{:S(2)}, u32[]{:S(2)}) %collective-permute-start.17) | collective-permute-done | bytes 262176 | tf_op jit(solution)/shard_map/ppermute | solution.py:14
  44.6 4.3 %collective-permute-start.10 = (bf16[1024,128]{1,0:T(8,128)(2,1)S(1)}, bf16[1024,128]{1,0:T(8,128)(2,1)S(1)}, u32[]{:S(2)}, u32[]{:S(2)}) collective-permute-start(bf16[1024,128]{1,0:T(8,128)(2,1)S(1)} %get-tuple-element.68), channel_id=1, source_target_pairs={{0,3},{1,0},{2,1},{3,2},{4,7},{5,4},{6,5},{7,6},{8,11},{9,8},{10,9... | collective-permute-start | bytes 786440 | tf_op jit(solution)/shard_map/ppermute | solution.py:14
  48.9 18.1 %collective-permute-done.18 = bf16[1024,128]{1,0:T(8,128)(2,1)} collective-permute-done((bf16[1024,128]{1,0:T(8,128)(2,1)S(1)}, bf16[1024,128]{1,0:T(8,128)(2,1)}, u32[]{:S(2)}, u32[]{:S(2)}) %collective-permute-start.18) | collective-permute-done | bytes 262176 | tf_op jit(solution)/shard_map/ppermute | solution.py:14
  78.4 13.8 %collective-permute-done.11 = bf16[1024,128]{1,0:T(8,128)(2,1)S(1)} collective-permute-done((bf16[1024,128]{1,0:T(8,128)(2,1)S(1)}, bf16[1024,128]{1,0:T(8,128)(2,1)S(1)}, u32[]{:S(2)}, u32[]{:S(2)}) %collective-permute-start.11) | collective-permute-done | bytes 262176 | tf_op jit(solution)/shard_map/ppermute | solution.py:14
  92.2 3.8 %collective-permute-start.28 = (bf16[1024,128]{1,0:T(8,128)(2,1)}, bf16[1024,128]{1,0:T(8,128)(2,1)}, u32[]{:S(2)}, u32[]{:S(2)}) collective-permute-start(bf16[1024,128]{1,0:T(8,128)(2,1)} %get-tuple-element.69), channel_id=1, source_target_pairs={{0,3},{1,0},{2,1},{3,2},{4,7},{5,4},{6,5},{7,6},{8,11},{9,8},{10,9... | collective-permute-start | bytes 786440 | tf_op jit(solution)/shard_map/ppermute | solution.py:14
  103.5 8.3 %collective-permute-done.3 = bf16[1024,128]{1,0:T(8,128)(2,1)S(1)} collective-permute-done((bf16[1024,128]{1,0:T(8,128)(2,1)S(1)}, bf16[1024,128]{1,0:T(8,128)(2,1)S(1)}, u32[]{:S(2)}, u32[]{:S(2)}) %collective-permute-start.3) | collective-permute-done | bytes 262176 | tf_op jit(solution)/shard_map/ppermute | solution.py:14
  150.5 8.2 %collective-permute-done.7 = bf16[128,640]{0,1:T(8,128)(2,1)S(1)} collective-permute-done((bf16[128,640]{0,1:T(8,128)(2,1)S(1)}, bf16[128,640]{0,1:T(8,128)(2,1)S(1)}, u32[]{:S(2)}, u32[]{:S(2)}) %collective-permute-start.7) | collective-permute-done | bytes 163872 | tf_op jit(solution)/shard_map/ppermute | solution.py:33
  162.0 3.6 %collective-permute-done.55 = bf16[128,512]{0,1:T(8,128)(2,1)S(1)} collective-permute-done((bf16[128,512]{0,1:T(8,128)(2,1)S(1)}, bf16[128,512]{0,1:T(8,128)(2,1)S(1)}, u32[]{:S(2)}, u32[]{:S(2)}) %collective-permute-start.55) | collective-permute-done | bytes 131104 | tf_op jit(solution)/shard_map/ppermute | solution.py:33
  167.4 4.6 %collective-permute-done.25 = bf16[128,640]{0,1:T(8,128)(2,1)S(1)} collective-permute-done((bf16[128,640]{0,1:T(8,128)(2,1)S(1)}, bf16[128,640]{0,1:T(8,128)(2,1)S(1)}, u32[]{:S(2)}, u32[]{:S(2)}) %collective-permute-start.25) | collective-permute-done | bytes 163872 | tf_op jit(solution)/shard_map/ppermute | solution.py:46
  172.0 4.2 %collective-permute-start.30 = (bf16[1024,128]{1,0:T(8,128)(2,1)}, bf16[1024,128]{1,0:T(8,128)(2,1)}, u32[]{:S(2)}, u32[]{:S(2)}) collective-permute-start(bf16[1024,128]{1,0:T(8,128)(2,1)} %get-tuple-element.69), channel_id=1, source_target_pairs={{0,1},{1,2},{2,3},{3,0},{4,5},{5,6},{6,7},{7,4},{8,9},{9,10},{10,1... | collective-permute-start | bytes 786440 | tf_op jit(solution)/shard_map/ppermute | solution.py:14
  177.9 4.5 %fusion.106 = (bf16[1024,512]{1,0:T(8,128)(2,1)}, f32[1024,512]{1,0:T(8,128)}) fusion(bf16[2,4,128,512]{3,2,1,0:T(8,128)(2,1)S(1)} %bitcast.220, bf16[1,4,128,1024]{3,2,1,0:T(8,128)(2,1)} %get-tuple-element.110, bf16[1,4,128,1024]{3,2,1,0:T(8,128)(2,1)} %get-tuple-element.109), kind=kOutput, calls=%fused_computation.229 | convolution fusion | flops 1075314688 | bytes 6291456 | tf_op jit(solution)/shard_map/jktd,jkte->de/dot_general | solution.py:121
  186.5 3.8 %fusion.7 = bf16[2,4,128,1024]{3,2,1,0:T(8,128)(2,1)S(1)} fusion(f32[2,4,128]{2,1,0:T(4,128)S(1)} %convert_reduce_fusion.1, f32[1024]{0:T(1024)S(1)} %bitcast.245, bf16[2,4,128,640]{3,2,1,0:T(8,128)(2,1)} %bitcast.211, bf16[1,4,128,1024]{3,2,1,0:T(8,128)(2,1)} %get-tuple-element.110, bf16[1,4,128,1024]{3,2,1,0:T(8,128)(2,1)} %get-tuple-element.109, ...), kind=kOutput, calls=%fused_computation.13 | convolution fusion | flops 1087373312 | bytes 8396800 | tf_op jit(solution)/shard_map/jkte,de->jktd/dot_general | solution.py:142
  201.5 4.2 %fusion.104 = (bf16[1024,512]{1,0:T(8,128)(2,1)}, f32[1024,512]{1,0:T(8,128)}) fusion(bf16[2,4,128,640]{3,2,1,0:T(8,128)(2,1)S(1)} %bitcast.212, f32[1024]{0:T(1024)S(1)} %bitcast.246, bf16[1,4,128,1024]{3,2,1,0:T(8,128)(2,1)} %bitcast.26, bf16[1,4,128,1024]{3,2,1,0:T(8,128)(2,1)S(1)} %copy-done.4), kind=kOutput, calls=%fused_computation.227 | convolution fusion | flops 1078460416 | bytes 6295552 | tf_op jit(solution)/shard_map/jktd,jkte->de/dot_general | solution.py:121
  212.5 18.0 %collective-permute-done.33 = bf16[128,512]{0,1:T(8,128)(2,1)S(1)} collective-permute-done((bf16[128,512]{0,1:T(8,128)(2,1)S(1)}, bf16[128,512]{0,1:T(8,128)(2,1)S(1)}, u32[]{:S(2)}, u32[]{:S(2)}) %collective-permute-start.33) | collective-permute-done | bytes 131104 | tf_op jit(solution)/shard_map/ppermute | solution.py:33
  236.8 3.9 %collective-permute-done.47 = bf16[128,512]{0,1:T(8,128)(2,1)S(1)} collective-permute-done((bf16[128,512]{0,1:T(8,128)(2,1)S(1)}, bf16[128,512]{0,1:T(8,128)(2,1)S(1)}, u32[]{:S(2)}, u32[]{:S(2)}) %collective-permute-start.47) | collective-permute-done | bytes 131104 | tf_op jit(solution)/shard_map/ppermute | solution.py:46
  251.7 4.2 %fusion.105 = (bf16[1024,512]{1,0:T(8,128)(2,1)S(1)}, f32[1024,512]{1,0:T(8,128)}) fusion(bf16[2,4,128,512]{3,2,1,0:T(8,128)(2,1)S(1)} %bitcast.221, bf16[1,4,128,1024]{3,2,1,0:T(8,128)(2,1)} %copy-done.10, bf16[1,4,128,1024]{3,2,1,0:T(8,128)(2,1)} %copy-done.12), kind=kOutput, calls=%fused_computation.228 | convolution fusion | flops 1075314688 | bytes 6291456 | tf_op jit(solution)/shard_map/jktd,jkte->de/dot_general | solution.py:121
  261.6 3.7 %fusion.3 = bf16[2,4,128,1024]{3,2,1,0:T(8,128)(2,1)S(1)} fusion(f32[2,4,128]{2,1,0:T(4,128)S(1)} %convert_reduce_fusion, f32[1024]{0:T(1024)S(1)} %bitcast.242, bf16[2,4,128,640]{3,2,1,0:T(8,128)(2,1)} %bitcast.214, bf16[1,4,128,1024]{3,2,1,0:T(8,128)(2,1)S(1)} %copy-done.11, bf16[1,4,128,1024]{3,2,1,0:T(8,128)(2,1)} %copy-done.12, ...), kind=kOutput, calls=%fused_computation.9 | convolution fusion | flops 1087373312 | bytes 8396800 | tf_op jit(solution)/shard_map/jkte,de->jktd/dot_general | solution.py:142
  276.7 7.4 %collective-permute-done.51 = bf16[1024,128]{1,0:T(8,128)(2,1)S(1)} collective-permute-done((bf16[1024,128]{1,0:T(8,128)(2,1)S(1)}, bf16[1024,128]{1,0:T(8,128)(2,1)S(1)}, u32[]{:S(2)}, u32[]{:S(2)}) %collective-permute-start.51) | collective-permute-done | bytes 262176 | tf_op jit(solution)/shard_map/ppermute | solution.py:14
  284.9 19.3 %collective-permute-start.41 = (bf16[1024,128]{1,0:T(8,128)(2,1)S(1)}, bf16[1024,128]{1,0:T(8,128)(2,1)S(1)}, u32[]{:S(2)}, u32[]{:S(2)}) collective-permute-start(bf16[1024,128]{1,0:T(8,128)(2,1)S(1)} %get-tuple-element.47), channel_id=1, source_target_pairs={{0,3},{1,0},{2,1},{3,2},{4,7},{5,4},{6,5},{7,6},{8,11},{9,8},{10,9... | collective-permute-start | bytes 786440 | tf_op jit(solution)/shard_map/ppermute | solution.py:14
  306.0 5.5 %collective-permute-done.43 = bf16[1024,128]{1,0:T(8,128)(2,1)S(1)} collective-permute-done((bf16[1024,128]{1,0:T(8,128)(2,1)S(1)}, bf16[1024,128]{1,0:T(8,128)(2,1)S(1)}, u32[]{:S(2)}, u32[]{:S(2)}) %collective-permute-start.43) | collective-permute-done | bytes 262176 | tf_op jit(solution)/shard_map/ppermute | solution.py:14
  313.5 9.2 %collective-permute-done.40 = bf16[1024,128]{1,0:T(8,128)(2,1)S(1)} collective-permute-done((bf16[1024,128]{1,0:T(8,128)(2,1)S(1)}, bf16[1024,128]{1,0:T(8,128)(2,1)S(1)}, u32[]{:S(2)}, u32[]{:S(2)}) %collective-permute-start.40) | collective-permute-done | bytes 262176 | tf_op jit(solution)/shard_map/ppermute | solution.py:14
  325.8 17.0 %collective-permute-done.60 = bf16[1024,128]{1,0:T(8,128)(2,1)S(1)} collective-permute-done((bf16[1024,128]{1,0:T(8,128)(2,1)S(1)}, bf16[1024,128]{1,0:T(8,128)(2,1)S(1)}, u32[]{:S(2)}, u32[]{:S(2)}) %collective-permute-start.60) | collective-permute-done | bytes 262176 | tf_op jit(solution)/shard_map/ppermute | solution.py:33
  (291 shorter events, 146.8 us)
Async XLA Ops:
  2.0 31.0 %collective-permute-start.1 = (bf16[2,1024,128]{2,1,0:T(8,128)(2,1)S(1)}, bf16[2,1024,128]{2,1,0:T(8,128)(2,1)}, u32[]{:S(2)}, u32[]{:S(2)}) collective-permute-start(bf16[2,1024,128]{2,1,0:T(8,128)(2,1)S(1)} %pad_maximum_fusion.13), channel_id=1, source_target_pairs={{0,16},{16,0},{1,17},{17,1},{2,18},{18,2},{3,19},{19,3},{4,20},{20... | collective-permute-start | bytes 1572872 | tf_op jit(solution)/shard_map/ppermute | solution.py:33
  10.8 61.6 %collective-permute-start.9 = (bf16[4,128,1024]{2,1,0:T(8,128)(2,1)}, bf16[4,128,1024]{2,1,0:T(8,128)(2,1)}, u32[]{:S(2)}, u32[]{:S(2)}) collective-permute-start(bf16[4,128,1024]{2,1,0:T(8,128)(2,1)} %get-tuple-element.30), channel_id=1, source_target_pairs={{0,16},{16,0},{1,17},{17,1},{2,18},{18,2},{3,19},{19,3},{4,20},{20... | collective-permute-start | bytes 3145736 | tf_op jit(solution)/shard_map/ppermute | solution.py:33
  10.9 101.5 %collective-permute-start = (bf16[4,128,1024]{2,1,0:T(8,128)(2,1)}, bf16[4,128,1024]{2,1,0:T(8,128)(2,1)}, u32[]{:S(2)}, u32[]{:S(2)}) collective-permute-start(bf16[4,128,1024]{2,1,0:T(8,128)(2,1)} %get-tuple-element.28), channel_id=1, source_target_pairs={{0,16},{16,0},{1,17},{17,1},{2,18},{18,2},{3,19},{19,3},{4,20},{20... | collective-permute-start | bytes 3145736 | tf_op jit(solution)/shard_map/ppermute | solution.py:33
  37.8 29.2 %collective-permute-start.18 = (bf16[1024,128]{1,0:T(8,128)(2,1)S(1)}, bf16[1024,128]{1,0:T(8,128)(2,1)}, u32[]{:S(2)}, u32[]{:S(2)}) collective-permute-start(bf16[1024,128]{1,0:T(8,128)(2,1)S(1)} %get-tuple-element.67), channel_id=1, source_target_pairs={{0,2},{1,3},{2,0},{3,1},{4,6},{5,7},{6,4},{7,5},{8,10},{9,11},{10,... | collective-permute-start | bytes 786440 | tf_op jit(solution)/shard_map/ppermute | solution.py:14
  37.8 29.2 %collective-permute-start.19 = (bf16[1024,128]{1,0:T(8,128)(2,1)S(1)}, bf16[1024,128]{1,0:T(8,128)(2,1)}, u32[]{:S(2)}, u32[]{:S(2)}) collective-permute-start(bf16[1024,128]{1,0:T(8,128)(2,1)S(1)} %get-tuple-element.67), channel_id=1, source_target_pairs={{0,1},{1,2},{2,3},{3,0},{4,5},{5,6},{6,7},{7,4},{8,9},{9,10},{10,1... | collective-permute-start | bytes 786440 | tf_op jit(solution)/shard_map/ppermute | solution.py:14
  44.6 31.0 %collective-permute-start.10 = (bf16[1024,128]{1,0:T(8,128)(2,1)S(1)}, bf16[1024,128]{1,0:T(8,128)(2,1)S(1)}, u32[]{:S(2)}, u32[]{:S(2)}) collective-permute-start(bf16[1024,128]{1,0:T(8,128)(2,1)S(1)} %get-tuple-element.68), channel_id=1, source_target_pairs={{0,3},{1,0},{2,1},{3,2},{4,7},{5,4},{6,5},{7,6},{8,11},{9,8},{10,9... | collective-permute-start | bytes 786440 | tf_op jit(solution)/shard_map/ppermute | solution.py:14
  67.0 25.2 %collective-permute-start.11 = (bf16[1024,128]{1,0:T(8,128)(2,1)S(1)}, bf16[1024,128]{1,0:T(8,128)(2,1)S(1)}, u32[]{:S(2)}, u32[]{:S(2)}) collective-permute-start(bf16[1024,128]{1,0:T(8,128)(2,1)S(1)} %get-tuple-element.68), channel_id=1, source_target_pairs={{0,2},{1,3},{2,0},{3,1},{4,6},{5,7},{6,4},{7,5},{8,10},{9,11},{10,... | collective-permute-start | bytes 786440 | tf_op jit(solution)/shard_map/ppermute | solution.py:14
  67.0 25.2 %collective-permute-start.12 = (bf16[1024,128]{1,0:T(8,128)(2,1)S(1)}, bf16[1024,128]{1,0:T(8,128)(2,1)S(1)}, u32[]{:S(2)}, u32[]{:S(2)}) collective-permute-start(bf16[1024,128]{1,0:T(8,128)(2,1)S(1)} %get-tuple-element.68), channel_id=1, source_target_pairs={{0,1},{1,2},{2,3},{3,0},{4,5},{5,6},{6,7},{7,4},{8,9},{9,10},{10,1... | collective-permute-start | bytes 786440 | tf_op jit(solution)/shard_map/ppermute | solution.py:14
  72.5 27.5 %collective-permute-start.2 = (bf16[1024,128]{1,0:T(8,128)(2,1)S(1)}, bf16[1024,128]{1,0:T(8,128)(2,1)S(1)}, u32[]{:S(2)}, u32[]{:S(2)}) collective-permute-start(bf16[1024,128]{1,0:T(8,128)(2,1)S(1)} %get-tuple-element.70), channel_id=1, source_target_pairs={{0,3},{1,0},{2,1},{3,2},{4,7},{5,4},{6,5},{7,6},{8,11},{9,8},{10,9... | collective-permute-start | bytes 786440 | tf_op jit(solution)/shard_map/ppermute | solution.py:14
  75.6 36.2 %collective-permute-start.3 = (bf16[1024,128]{1,0:T(8,128)(2,1)S(1)}, bf16[1024,128]{1,0:T(8,128)(2,1)S(1)}, u32[]{:S(2)}, u32[]{:S(2)}) collective-permute-start(bf16[1024,128]{1,0:T(8,128)(2,1)S(1)} %get-tuple-element.70), channel_id=1, source_target_pairs={{0,2},{1,3},{2,0},{3,1},{4,6},{5,7},{6,4},{7,5},{8,10},{9,11},{10,... | collective-permute-start | bytes 786440 | tf_op jit(solution)/shard_map/ppermute | solution.py:14
  92.2 100.0 %collective-permute-start.28 = (bf16[1024,128]{1,0:T(8,128)(2,1)}, bf16[1024,128]{1,0:T(8,128)(2,1)}, u32[]{:S(2)}, u32[]{:S(2)}) collective-permute-start(bf16[1024,128]{1,0:T(8,128)(2,1)} %get-tuple-element.69), channel_id=1, source_target_pairs={{0,3},{1,0},{2,1},{3,2},{4,7},{5,4},{6,5},{7,6},{8,11},{9,8},{10,9... | collective-permute-start | bytes 786440 | tf_op jit(solution)/shard_map/ppermute | solution.py:14
  100.0 92.2 %collective-permute-start.29 = (bf16[1024,128]{1,0:T(8,128)(2,1)}, bf16[1024,128]{1,0:T(8,128)(2,1)}, u32[]{:S(2)}, u32[]{:S(2)}) collective-permute-start(bf16[1024,128]{1,0:T(8,128)(2,1)} %get-tuple-element.69), channel_id=1, source_target_pairs={{0,2},{1,3},{2,0},{3,1},{4,6},{5,7},{6,4},{7,5},{8,10},{9,11},{10,... | collective-permute-start | bytes 786440 | tf_op jit(solution)/shard_map/ppermute | solution.py:14
  197.2 70.7 %collective-permute-start.57 = (bf16[1024,128]{1,0:T(8,128)(2,1)}, bf16[1024,128]{1,0:T(8,128)(2,1)}, u32[]{:S(2)}, u32[]{:S(2)}) collective-permute-start(bf16[1024,128]{1,0:T(8,128)(2,1)} %get-tuple-element.37), channel_id=1, source_target_pairs={{0,1},{1,2},{2,3},{3,0},{4,5},{5,6},{6,7},{7,4},{8,9},{9,10},{10,1... | collective-permute-start | bytes 786440 | tf_op jit(solution)/shard_map/ppermute | solution.py:14
  199.8 48.6 %collective-permute-start.61 = (bf16[4,128,1024]{2,1,0:T(8,128)(2,1)}, bf16[4,128,1024]{2,1,0:T(8,128)(2,1)S(1)}, u32[]{:S(2)}, u32[]{:S(2)}) collective-permute-start(bf16[4,128,1024]{2,1,0:T(8,128)(2,1)} %get-tuple-element.33), channel_id=1, source_target_pairs={{0,16},{16,0},{1,17},{17,1},{2,18},{18,2},{3,19},{19,3},{4,20},{20... | collective-permute-start | bytes 3145736 | tf_op jit(solution)/shard_map/ppermute | solution.py:33
  243.1 27.5 %collective-permute-start.58 = (bf16[1024,128]{1,0:T(8,128)(2,1)}, bf16[1024,128]{1,0:T(8,128)(2,1)}, u32[]{:S(2)}, u32[]{:S(2)}) collective-permute-start(bf16[1024,128]{1,0:T(8,128)(2,1)} %get-tuple-element.39), channel_id=1, source_target_pairs={{0,2},{1,3},{2,0},{3,1},{4,6},{5,7},{6,4},{7,5},{8,10},{9,11},{10,... | collective-permute-start | bytes 786440 | tf_op jit(solution)/shard_map/ppermute | solution.py:14
  247.0 25.6 %collective-permute-start.59 = (bf16[1024,128]{1,0:T(8,128)(2,1)}, bf16[1024,128]{1,0:T(8,128)(2,1)}, u32[]{:S(2)}, u32[]{:S(2)}) collective-permute-start(bf16[1024,128]{1,0:T(8,128)(2,1)} %get-tuple-element.38), channel_id=1, source_target_pairs={{0,3},{1,0},{2,1},{3,2},{4,7},{5,4},{6,5},{7,6},{8,11},{9,8},{10,9... | collective-permute-start | bytes 786440 | tf_op jit(solution)/shard_map/ppermute | solution.py:14
  248.4 26.2 %collective-permute-start.42 = (bf16[1024,128]{1,0:T(8,128)(2,1)}, bf16[1024,128]{1,0:T(8,128)(2,1)}, u32[]{:S(2)}, u32[]{:S(2)}) collective-permute-start(bf16[1024,128]{1,0:T(8,128)(2,1)} %get-tuple-element.43), channel_id=1, source_target_pairs={{0,1},{1,2},{2,3},{3,0},{4,5},{5,6},{6,7},{7,4},{8,9},{9,10},{10,1... | collective-permute-start | bytes 786440 | tf_op jit(solution)/shard_map/ppermute | solution.py:14
  272.6 38.9 %collective-permute-start.43 = (bf16[1024,128]{1,0:T(8,128)(2,1)S(1)}, bf16[1024,128]{1,0:T(8,128)(2,1)S(1)}, u32[]{:S(2)}, u32[]{:S(2)}) collective-permute-start(bf16[1024,128]{1,0:T(8,128)(2,1)S(1)} %copy-done.18), channel_id=1, source_target_pairs={{0,2},{1,3},{2,0},{3,1},{4,6},{5,7},{6,4},{7,5},{8,10},{9,11},{10,... | collective-permute-start | bytes 786440 | tf_op jit(solution)/shard_map/ppermute | solution.py:14
  274.7 38.4 %collective-permute-start.44 = (bf16[1024,128]{1,0:T(8,128)(2,1)S(1)}, bf16[1024,128]{1,0:T(8,128)(2,1)S(1)}, u32[]{:S(2)}, u32[]{:S(2)}) collective-permute-start(bf16[1024,128]{1,0:T(8,128)(2,1)S(1)} %copy-done.17), channel_id=1, source_target_pairs={{0,3},{1,0},{2,1},{3,2},{4,7},{5,4},{6,5},{7,6},{8,11},{9,8},{10,9... | collective-permute-start | bytes 786440 | tf_op jit(solution)/shard_map/ppermute | solution.py:14
  276.4 37.1 %collective-permute-start.39 = (bf16[1024,128]{1,0:T(8,128)(2,1)S(1)}, bf16[1024,128]{1,0:T(8,128)(2,1)S(1)}, u32[]{:S(2)}, u32[]{:S(2)}) collective-permute-start(bf16[1024,128]{1,0:T(8,128)(2,1)S(1)} %get-tuple-element.46), channel_id=1, source_target_pairs={{0,1},{1,2},{2,3},{3,0},{4,5},{5,6},{6,7},{7,4},{8,9},{9,10},{10,1... | collective-permute-start | bytes 786440 | tf_op jit(solution)/shard_map/ppermute | solution.py:14
  284.1 38.7 %collective-permute-start.40 = (bf16[1024,128]{1,0:T(8,128)(2,1)S(1)}, bf16[1024,128]{1,0:T(8,128)(2,1)S(1)}, u32[]{:S(2)}, u32[]{:S(2)}) collective-permute-start(bf16[1024,128]{1,0:T(8,128)(2,1)S(1)} %get-tuple-element.48), channel_id=1, source_target_pairs={{0,2},{1,3},{2,0},{3,1},{4,6},{5,7},{6,4},{7,5},{8,10},{9,11},{10,... | collective-permute-start | bytes 786440 | tf_op jit(solution)/shard_map/ppermute | solution.py:14
  284.9 37.9 %collective-permute-start.41 = (bf16[1024,128]{1,0:T(8,128)(2,1)S(1)}, bf16[1024,128]{1,0:T(8,128)(2,1)S(1)}, u32[]{:S(2)}, u32[]{:S(2)}) collective-permute-start(bf16[1024,128]{1,0:T(8,128)(2,1)S(1)} %get-tuple-element.47), channel_id=1, source_target_pairs={{0,3},{1,0},{2,1},{3,2},{4,7},{5,4},{6,5},{7,6},{8,11},{9,8},{10,9... | collective-permute-start | bytes 786440 | tf_op jit(solution)/shard_map/ppermute | solution.py:14
  311.5 35.3 %collective-permute-start.62 = (bf16[4,128,1024]{2,1,0:T(8,128)(2,1)S(1)}, bf16[4,128,1024]{2,1,0:T(8,128)(2,1)S(1)}, u32[]{:S(2)}, u32[]{:S(2)}) collective-permute-start(bf16[4,128,1024]{2,1,0:T(8,128)(2,1)S(1)} %get-tuple-element.31), channel_id=1, source_target_pairs={{0,16},{16,0},{1,17},{17,1},{2,18},{18,2},{3,19},{19,3},{4,20},{20... | collective-permute-start | bytes 3145736 | tf_op jit(solution)/shard_map/ppermute | solution.py:33
  313.1 29.8 %collective-permute-start.60 = (bf16[1024,128]{1,0:T(8,128)(2,1)S(1)}, bf16[1024,128]{1,0:T(8,128)(2,1)S(1)}, u32[]{:S(2)}, u32[]{:S(2)}) collective-permute-start(bf16[1024,128]{1,0:T(8,128)(2,1)S(1)} %get-tuple-element.15), channel_id=1, source_target_pairs={{0,16},{16,0},{1,17},{17,1},{2,18},{18,2},{3,19},{19,3},{4,20},{20... | collective-permute-start | bytes 786440 | tf_op jit(solution)/shard_map/ppermute | solution.py:33
  (72 other events, 897.5 us)

commit v2 on v1

--- a/solution.py
+++ b/solution.py
@@ -1,6 +1,8 @@
 import jax
 import jax.numpy as jnp
 from jax import lax
+from jax.experimental import pallas as pl
+from jax.experimental.pallas import tpu as pltpu
 from jax.sharding import PartitionSpec as P
 
 EPS = 1e-05
@@ -42,46 +44,476 @@
 
 
 def swap_both(block):
-    pairs = [(i, (i ^ 4) ^ 2) for i in range(8)]
-    return lax.ppermute(block, ("section", "mp"), pairs)
+    return lax.ppermute(block, ("section", "mp"), [(i, i ^ 6) for i in range(8)])
+
+
+def after(array, *others):
+    return lax.optimization_barrier((array,) + others)[0]
+
+
+CORE, CHIP, SECTION, OWN, PLAN = 0, 1, 2, 3, 5
+STEPS = 4
+VMEM_BYTES = 48 * 1024 * 1024
+
+
+def step_place():
+    step = pl.program_id(0)
+    return step, 1 - step // 2, step % 2
+
+
+def slot_at(place, a, b):
+    return 2 * (place[CHIP] ^ a) + (place[CORE] ^ b)
+
+
+def join_units(step, parts, whole):
+    @pl.when(step == 0)
+    def _():
+        for k, part in enumerate(parts):
+            whole[:, k * part.shape[1] : (k + 1) * part.shape[1]] = part[...]
+
+
+def join_slots(step, parts, whole):
+    @pl.when(step == 0)
+    def _():
+        for k in range(4):
+            whole[0, k // 2, k % 2] = parts[k][...]
+        whole[1] = parts[4][...]
+
+
+def load_set(place, refs, rows):
+    step, b, which = step_place()
+    tokens = refs[0].shape[1]
+    for k in range(2):
+
+        @pl.when(which == k)
+        def _(k=k):
+            for a in range(2):
+                rows[a * tokens : (a + 1) * tokens] = refs[k][slot_at(place, a, b)]
+
+
+def load_top(phase, place, top, rows):
+    step, b, which = step_place()
+    tokens, half = top.shape[1], top.shape[0] // 2
+    for a in range(2):
+        slot = half * (place[OWN + phase] ^ which) + slot_at(place, a, b)
+        rows[a * tokens : (a + 1) * tokens] = top[place[PLAN + slot]]
+
+
+def put_partial(value, sent, kept, step, which):
+    value = value.astype(BF16).reshape(sent.shape[1:])
+
+    @pl.when(step < 2)
+    def _():
+        sent[which] = value
+
+    @pl.when(step >= 2)
+    def _():
+        kept[which] = value
+
+
+def hidden_kernel(group, place, own, received, gain, w0, w1, w2, w3, sent, kept, weights, rows):
+    step, b, which = step_place()
+    join_units(step, (w0, w1, w2, w3), weights)
+    load_set(place, (own, received), rows)
+    wide = rows[...].astype(F32)
+    normed = (wide * gain[group : group + 1, :]).astype(BF16)
+    part = jnp.dot(normed, weights[...], preferred_element_type=F32)
+    squares = jnp.sum(wide * wide, axis=1, keepdims=True)
+    packed = jnp.concatenate((part, jnp.broadcast_to(squares, (part.shape[0], PAD))), axis=1)
+    put_partial(packed, sent, kept, step, which)
+
+
+def top_kernel(phase, place, top, w0, w1, w2, w3, sent, kept, weights, rows):
+    step, b, which = step_place()
+    join_units(step, (w0, w1, w2, w3), weights)
+    load_top(phase, place, top, rows)
+    part = jnp.dot(rows[...], weights[...], preferred_element_type=F32)
+    put_partial(part, sent, kept, step, which)
+
+
+def back_step(group, place, own, received, gain, spread, weights, rows, incoming):
+    step, b, which = step_place()
+    load_set(place, (own, received), rows)
+    units = weights.shape[1]
+    packed = spread[b, which].reshape(rows.shape[0], units + PAD)
+    back = lax.dot_general(
+        packed[:, :units], weights[...], (((1,), (1,)), ((), ())), preferred_element_type=F32
+    )
+    factor = packed[:, units : units + 1].astype(F32)
+    result = (
+        incoming.astype(F32)
+        + gain[group : group + 1, :] * back
+        - factor * rows[...].astype(F32)
+    )
+    return result.astype(BF16)
+
+
+def put_result(place, result, results):
+    step, b, which = step_place()
+    tokens = result.shape[0] // 2
+    for k in range(2):
+
+        @pl.when(which == k)
+        def _(k=k):
+            for a in range(2):
+                results[k][slot_at(place, a, b)] = result[a * tokens : (a + 1) * tokens]
+
+
+def first_back_kernel(
+    group, place, own, received, gain, top, p0, p1, p2, p3, p4, w0, w1, w2, w3, v0, v1, v2, v3,
+    result0, result1, sent, kept, weights, outward, spread, rows, grads,
+):
+    step, b, which = step_place()
+    join_units(step, (w0, w1, w2, w3), weights)
+    join_units(step, (v0, v1, v2, v3), outward)
+    join_slots(step, (p0, p1, p2, p3, p4), spread)
+    load_top(0, place, top, grads)
+    result = back_step(group, place, own, received, gain, spread, weights, rows, grads[...])
+    put_result(place, result, (result0, result1))
+    part = jnp.dot(result, outward[...], preferred_element_type=F32)
+    put_partial(part, sent, kept, step, 1 - which)
+
+
+def last_back_kernel(
+    group, place, own, received, gain, in0, in1, p0, p1, p2, p3, p4, w0, w1, w2, w3,
+    result0, result1, weights, spread, rows, grads,
+):
+    step, b, which = step_place()
+    join_units(step, (w0, w1, w2, w3), weights)
+    join_slots(step, (p0, p1, p2, p3, p4), spread)
+    load_set(place, (in0, in1), grads)
+    result = back_step(group, place, own, received, gain, spread, weights, rows, grads[...])
+    put_result(place, result, (result0, result1))
+
+
+def add_grad(step, total, units, rows):
+    part = lax.dot_general(units, rows, (((0,), (0,)), ((), ())), preferred_element_type=F32)
+
+    @pl.when(step == 0)
+    def _():
+        total[...] = part
+
+    @pl.when(step > 0)
+    def _():
+        total[...] += part
+
+
+def put_grad(step, total, kept, parts):
+    @pl.when(step == STEPS - 1)
+    def _():
+        height = kept.shape[0]
+        kept[...] = total[:height]
+        for k, part in enumerate(parts):
+            part[...] = total[(k + 1) * height : (k + 2) * height].astype(BF16)
+
+
+def in_grad_kernel(
+    group, place, own, received, gain, p0, p1, p2, p3, p4, kept, c1, c2, c3, total, spread, rows
+):
+    step, b, which = step_place()
+    join_slots(step, (p0, p1, p2, p3, p4), spread)
+    load_set(place, (own, received), rows)
+    normed = (rows[...].astype(F32) * gain[group : group + 1, :]).astype(BF16)
+    packed = spread[b, which].reshape(rows.shape[0], spread.shape[-1])
+    add_grad(step, total, packed[:, : total.shape[0]], normed)
+    put_grad(step, total, kept, (c1, c2, c3))
+
+
+def top_grad_kernel(place, top, p0, p1, p2, p3, p4, kept, c1, c2, c3, total, spread, rows):
+    step, b, which = step_place()
+    join_slots(step, (p0, p1, p2, p3, p4), spread)
+    load_top(0, place, top, rows)
+    packed = spread[b, which].reshape(rows.shape[0], spread.shape[-1])
+    add_grad(step, total, packed, rows[...])
+    put_grad(step, total, kept, (c1, c2, c3))
+
+
+def out_grad_kernel(place, in0, in1, p0, p1, p2, p3, p4, kept, c1, c2, c3, total, spread, rows):
+    step, b, which = step_place()
+    join_slots(step, (p0, p1, p2, p3, p4), spread)
+    load_set(place, (in0, in1), rows)
+    packed = spread[b, which].reshape(rows.shape[0], spread.shape[-1])
+    add_grad(step, total, packed, rows[...])
+    put_grad(step, total, kept, (c1, c2, c3))
+
+
+def core_sum_kernel(kept, moved, own, chip, section, both):
+    def at(k):
+        return kept[k // 2, k % 2].astype(F32) + moved[k // 2, k % 2].astype(F32)
+
+    own[...] = at(0)
+    chip[...] = at(1).astype(BF16)
+    section[...] = at(2).astype(BF16)
+    both[...] = at(3).astype(BF16)
+
+
+def whole_sum(own, chip, section, both):
+    return own[...] + chip[...].astype(F32) + section[...].astype(F32) + both[...].astype(F32)
+
+
+def active_kernel(features, own, chip, section, both, hidden, activated):
+    total = whole_sum(own, chip, section, both)
+    hidden[...] = total
+    units = activated.shape[1]
+    terms = row_terms(total[:, :units], total[:, units : units + 1], features)
+    activated[...] = terms[3]
+
+
+def unit_kernel(features, hidden, own, chip, section, both, packed):
+    units = own.shape[1]
+    unit_sums, square_sums = hidden[:, :units], hidden[:, units : units + 1]
+    inverse_rms, hidden_pre, sigma, _ = row_terms(unit_sums, square_sums, features)
+    scaled_grad, factor = unit_terms(
+        whole_sum(own, chip, section, both), unit_sums, inverse_rms, hidden_pre, sigma, features
+    )
+    packed[:, :units] = scaled_grad
+    packed[:, units:] = jnp.broadcast_to(factor, (factor.shape[0], PAD)).astype(BF16)
+
+
+def call(kernel, name, outs, args, scratch=(), specs=None, place=None, flops=0):
+    size = sum(a.size * a.dtype.itemsize for a in args)
+    size += sum(o.size * o.dtype.itemsize for o in outs)
+    cost = pl.CostEstimate(flops=flops, bytes_accessed=size, transcendentals=0)
+    params = pltpu.CompilerParams(vmem_limit_bytes=VMEM_BYTES)
+    if place is None:
+        return pl.pallas_call(
+            kernel, out_shape=outs, compiler_params=params, cost_estimate=cost, name=name
+        )(*args)
+
+    def whole(shape):
+        return pl.BlockSpec(shape, lambda i, s: (0,) * len(shape))
+
+    specs = specs or {}
+    return pl.pallas_call(
+        kernel,
+        out_shape=outs,
+        grid_spec=pltpu.PrefetchScalarGridSpec(
+            num_scalar_prefetch=1,
+            grid=(STEPS,),
+            in_specs=[specs.get(k, whole(a.shape)) for k, a in enumerate(args)],
+            out_specs=[whole(o.shape) for o in outs],
+            scratch_shapes=[pltpu.VMEM(shape, dtype) for shape, dtype in scratch],
+        ),
+        compiler_params=params,
+        cost_estimate=cost,
+        name=name,
+    )(place, *args)
+
+
+def shape_of(shape, dtype=BF16):
+    return jax.ShapeDtypeStruct(shape, dtype)
+
+
+def pair_sum(sent, kept):
+    moved = swap_core(sent)
+    small = sent.shape[2:]
+    own, chip, section, both = call(
+        core_sum_kernel,
+        "core_sum",
+        [shape_of(small, F32)] + [shape_of(small)] * 3,
+        (kept, moved),
+    )
+    return own, swap_chip(chip), swap_section(section), swap_both(both)
+
+
+def pair_spread(block):
+    parts = (block, swap_chip(block), swap_section(block), swap_both(block))
+    four = jnp.stack(parts).reshape((2, 2) + block.shape)
+    return parts + (swap_core(four),)
+
+
+def two_sections(saved_inputs, cotangent, weight_in, weight_out, gain, plan):
+    own = lax.axis_index("section")
+    other = 1 - own
+    mp_index = lax.axis_index("mp")
+    stored = saved_inputs[0]
+    slots, tokens, width = stored.shape
+    half, part = slots // 2, width // 2
+    features = width * lax.axis_size("mp")
+    place = jnp.concatenate(
+        (jnp.stack((mp_index % 2, mp_index // 2, own, other, own)).astype(jnp.int32), plan)
+    )
+
+    def rows(array, section):
+        return lax.dynamic_slice_in_dim(array, section * part, part, 0)
+
+    mine = jnp.stack((rows(weight_in[0], own), rows(weight_out[0], own)))
+    moved = swap_section(jnp.stack((rows(weight_in[0], other), rows(weight_out[0], other))))
+
+    def sent_inputs(phase):
+        first = half * place[OWN + phase]
+        return lax.dynamic_slice(stored, (first, 0, other * part), (half, tokens, part))
+
+    received = [None, None]
+    received[0] = swap_section(after(sent_inputs(0), moved))
+    received[1] = swap_section(after(sent_inputs(1), received[0]))
+
+    def unit_parts(block):
+        count = lax.axis_size("dp")
+        return (block,) + tuple(rotate(block, -k) for k in range(1, count))
+
+    in_parts, out_parts = [], []
+    for phase in range(2):
+        held = jnp.where(own == 1 - phase, mine, moved)
+        in_parts.append(unit_parts(held[0]))
+        out_parts.append(unit_parts(held[1]))
+    units = 4 * mine.shape[-1]
+    rows2 = 2 * tokens
+    gain_spec = pl.BlockSpec((2, part), lambda i, s: (0, s[SECTION]))
+    top_spec = pl.BlockSpec((slots, tokens, part), lambda i, s: (0, 0, s[SECTION]))
+    partial_shapes = [shape_of((2, 2, tokens, units))] * 2
+    hidden_shapes = [shape_of((2, 2, tokens, units + PAD))] * 2
+    set_shape = shape_of((half, tokens, part))
+    weight_scratch = ((part, units), BF16)
+    rows_scratch = ((rows2, part), BF16)
+    spread_scratch = ((2, 2, 2, tokens, units + PAD), BF16)
+    act_scratch = ((2, 2, 2, tokens, units), BF16)
+    grad_scratch = ((units, part), F32)
+    grad_shapes = [shape_of((units // 4, part), F32)] + [shape_of((units // 4, part))] * 3
+    one_dot = 2 * slots * tokens * part * units
+
+    def own_spec(phase):
+        return pl.BlockSpec(
+            (half, tokens, part), lambda i, s: (s[OWN + phase], 0, s[SECTION])
+        )
+
+    def bind(kernel, *first):
+        def bound(*refs):
+            kernel(*first, *refs)
+
+        return bound
+
+    def hidden_part(phase):
+        return call(
+            bind(hidden_kernel, 1 - phase),
+            "hidden_part",
+            hidden_shapes,
+            (stored, received[phase], gain) + in_parts[phase],
+            [weight_scratch, rows_scratch],
+            {0: own_spec(phase), 2: gain_spec},
+            place,
+            one_dot,
+        )
+
+    def hidden_terms(sums):
+        return call(
+            bind(active_kernel, features),
+            "activated",
+            [shape_of((tokens, units + PAD), F32), shape_of((tokens, units))],
+            sums,
+        )
+
+    def unit_grad_terms(hidden, sums):
+        return call(
+            bind(unit_kernel, features),
+            "unit_grads",
+            [shape_of((tokens, units + PAD))],
+            (hidden,) + sums,
+        )[0]
+
+    def in_grad(phase, scaled):
+        return call(
+            bind(in_grad_kernel, 1 - phase),
+            "in_grad",
+            grad_shapes,
+            (stored, received[phase], gain) + scaled,
+            [grad_scratch, spread_scratch, rows_scratch],
+            {0: own_spec(phase), 2: gain_spec},
+            place,
+            one_dot,
+        )
+
+    def scatter(parts):
+        total = parts[0]
+        for k in range(1, 4):
+            total = total + rotate(parts[k], k).astype(F32)
+        return total
+
+    hidden0, act0 = hidden_terms(pair_sum(*hidden_part(0)))
+    act0 = pair_spread(act0)
+    sent, kept = call(
+        bind(top_kernel, 0),
+        "top_part",
+        partial_shapes,
+        (cotangent,) + out_parts[0],
+        [weight_scratch, rows_scratch],
+        {0: top_spec},
+        place,
+        one_dot,
+    )
+    scaled0 = pair_spread(unit_grad_terms(hidden0, pair_sum(sent, kept)))
+    result0, result1, sent, kept = call(
+        bind(first_back_kernel, 1),
+        "first_back",
+        [set_shape, set_shape] + partial_shapes,
+        (stored, received[0], gain, cotangent) + scaled0 + in_parts[0] + out_parts[1],
+        [weight_scratch, weight_scratch, spread_scratch, rows_scratch, rows_scratch],
+        {0: own_spec(0), 2: gain_spec, 3: top_spec},
+        place,
+        2 * one_dot,
+    )
+    in_total0 = scatter(in_grad(0, scaled0))
+    out_total0 = scatter(
+        call(
+            top_grad_kernel,
+            "top_grad",
+            grad_shapes,
+            (cotangent,) + act0,
+            [grad_scratch, act_scratch, rows_scratch],
+            {0: top_spec},
+            place,
+            one_dot,
+        )
+    )
+    hidden1, act1 = hidden_terms(pair_sum(*hidden_part(1)))
+    act1 = pair_spread(act1)
+    out_total1 = scatter(
+        call(
+            out_grad_kernel,
+            "out_grad",
+            grad_shapes,
+            (result1, result0) + act1,
+            [grad_scratch, act_scratch, rows_scratch],
+            None,
+            place,
+            one_dot,
+        )
+    )
+    scaled1 = pair_spread(unit_grad_terms(hidden1, pair_sum(sent, kept)))
+    returned0 = swap_section(after(result1, scaled1[4]))
+    in_total1 = scatter(in_grad(1, scaled1))
+    result2, result3 = call(
+        bind(last_back_kernel, 0),
+        "last_back",
+        [set_shape, set_shape],
+        (stored, received[1], gain, result1, result0) + scaled1 + in_parts[1],
+        [weight_scratch, spread_scratch, rows_scratch, rows_scratch],
+        {0: own_spec(1), 2: gain_spec},
+        place,
+        one_dot,
+    )
+    returned1 = swap_section(result3)
+    outputs = jnp.zeros_like(stored)
+    for phase, block, back in ((0, result0, returned0), (1, result2, returned1)):
+        first = half * place[OWN + phase]
+        outputs = lax.dynamic_update_slice(outputs, block, (first, 0, own * part))
+        outputs = lax.dynamic_update_slice(outputs, back, (first, 0, other * part))
+
+    def whole(total0, total1):
+        kept = jnp.where(own == 1, total0, total1)
+        given = jnp.where(own == 1, total1, total0).astype(BF16)
+        back = swap_section(given).astype(F32)
+        return jnp.where(
+            own == 1,
+            jnp.concatenate((back, kept), 1),
+            jnp.concatenate((kept, back), 1),
+        ).T
+
+    return (whole(in_total0, in_total1)[None], whole(out_total0, out_total1)[None], outputs[None])
 
 
 def pick(array, index, axis):
     return lax.dynamic_index_in_dim(array, index, axis, keepdims=False)
-
-
-def ordered(first, second, flipped, axis):
-    return jnp.where(
-        flipped,
-        jnp.concatenate((second, first), axis),
-        jnp.concatenate((first, second), axis),
-    )
-
-
-def pair_sum(partial):
-    mp_index = lax.axis_index("mp")
-    core, chip = mp_index % 2, mp_index // 2
-    sets, slots, tokens, width = partial.shape
-    parts = partial.reshape(sets, slots // 2, 2, tokens, width)
-    narrow = parts.astype(BF16)
-    mine = pick(parts, core, 2).astype(F32) + swap_core(pick(narrow, 1 - core, 2)).astype(F32)
-    sent = mine.astype(BF16)
-    total = pick(mine[0], chip, 0)
-    total = total + swap_chip(pick(sent[0], 1 - chip, 0)).astype(F32)
-    total = total + swap_section(pick(sent[1], chip, 0)).astype(F32)
-    total = total + swap_both(pick(sent[1], 1 - chip, 0)).astype(F32)
-    return total
-
-
-def pair_spread(block):
-    mp_index = lax.axis_index("mp")
-    core, chip = mp_index % 2, mp_index // 2
-    tokens, width = block.shape
-    own = ordered(block[None], swap_chip(block)[None], chip == 1, 0)
-    received = ordered(swap_section(block)[None], swap_both(block)[None], chip == 1, 0)
-    mine = jnp.stack((own, received))
-    both = ordered(mine[:, :, None], swap_core(mine)[:, :, None], core == 1, 2)
-    return both.reshape(2, 4, tokens, width)
 
 
 def any_sum(partial):
@@ -142,71 +574,6 @@
     back = jnp.einsum("jkte,de->jktd", scaled_grad, in_full, preferred_element_type=F32)
     result = (incoming.astype(F32) + gain_row * back - factor * wide).astype(BF16)
     return result, accumulate(normed, scaled_grad), accumulate(incoming, activated)
-
-
-def two_sections(saved_inputs, cotangent, weight_in, weight_out, gain, plan):
-    own = lax.axis_index("section")
-    other = 1 - own
-    stored = saved_inputs[0]
-    slots, tokens, width = stored.shape
-    half, part = slots // 2, width // 2
-    features = width * lax.axis_size("mp")
-
-    def columns(array, section):
-        return lax.dynamic_slice_in_dim(array, section * part, part, array.ndim - 1)
-
-    def rows(array, section):
-        return lax.dynamic_slice_in_dim(array, section * part, part, 0)
-
-    mine = jnp.stack((rows(weight_in[0], own), rows(weight_out[0], own)))
-    moved = swap_section(jnp.stack((rows(weight_in[0], other), rows(weight_out[0], other))))
-    sent_slots = [half * other, half * own]
-    blocks = []
-    for phase in range(2):
-        local = lax.dynamic_slice_in_dim(stored, sent_slots[phase], half, 0)
-        blocks.append((columns(local, own), swap_section(columns(local, other))))
-    top = columns(cotangent, own)
-
-    def chosen(start):
-        return jnp.stack([pick(top, plan[start + i], 0) for i in range(half)])
-
-    incoming = jnp.stack((chosen(sent_slots[0]), chosen(sent_slots[1])))
-    outputs = jnp.zeros_like(stored)
-    in_blocks = [None, None]
-    out_blocks = [None, None]
-    for phase in range(2):
-        group = 1 - phase
-        held = jnp.where(own == group, mine, moved)
-        in_full = gather_units(held[0])
-        out_full = gather_units(held[1])
-        gain_row = columns(gain[group], own)
-        result, in_total, out_total = run_phase(
-            jnp.stack(blocks[phase]),
-            incoming,
-            in_full,
-            out_full,
-            gain_row,
-            features,
-            pair_sum,
-            pair_spread,
-        )
-        in_blocks[phase] = scatter_units(in_total)
-        out_blocks[phase] = scatter_units(out_total)
-        returned = swap_section(result[1])
-        outputs = lax.dynamic_update_slice(
-            outputs, result[0], (sent_slots[phase], 0, own * part)
-        )
-        outputs = lax.dynamic_update_slice(
-            outputs, returned, (sent_slots[phase], 0, other * part)
-        )
-        incoming = jnp.stack((result[1], result[0]))
-
-    def whole(by_phase):
-        kept = jnp.where(own == 1, by_phase[0], by_phase[1])
-        given = jnp.where(own == 1, by_phase[1], by_phase[0]).astype(BF16)
-        return ordered(kept, swap_section(given).astype(F32), own == 1, 0)
-
-    return (whole(in_blocks)[None], whole(out_blocks)[None], outputs[None])
 
 
 def any_sections(saved_inputs, cotangent, weight_in, weight_out, gain, plan):

time: 354 us -> 316 us (0.89); the launches traced: 348 us -> 316 us
  Pallas kernels: 0 us -> 47.1 us
  matrix products: 34.1 us -> 0 us
  starting transfers between devices: 97.3 us -> 126 us
  local copies, waits for them, and re-layouts: 39.3 us -> 13.3 us
  other arithmetic: 24.1 us -> 5.24 us
  between operations: 16.8 us -> 1.05 us
  waiting for transfers between devices: 136 us -> 123 us
    pallas_call x0 -> x17, Pallas kernels: none -> 47.1 us  [the longest x9 45.6 us: call(): pl.pallas_call(kernel, out_shape=outs, grid_spec=pltpu.PrefetchScalarGrid...]
    dot_general x10 -> x0, matrix products: 34.1 us -> none  [the longest x4 15.4 us: accumulate(): return jnp.einsum('jktd,jkte->de', rows, units, preferred_element_type=F32)]
    ppermute x24, starting transfers between devices: 60.5 us -> 87.8 us  [rotate(): lax.ppermute(block, 'dp', [(i, (i + shift) % count) for i in range(count)])]
    squeeze x29 -> x2, local copies, waits for them, and re-layouts: 15.3 us -> 0.07 us  [two_sections(): out_parts.append(unit_parts(held[1]))]
    ppermute x24, waiting for transfers between devices: 68.2 us -> 58 us  [rotate(): lax.ppermute(block, 'dp', [(i, (i + shift) % count) for i in range(count)])]
    dynamic_slice x12 -> x1, local copies, waits for them, and re-layouts: 9.68 us -> 3.03 us  [sent_inputs(): lax.dynamic_slice(stored, (first, 0, other * part), (half, tokens, part))]
    select_n x15 -> x1, other arithmetic: 6.9 us -> 0.89 us  [two_sections(): held = jnp.where(own == 1 - phase, mine, moved)]
    slice x13 -> x0, local copies, waits for them, and re-layouts: 5.11 us -> none  [the longest x4 4.03 us: scatter_units(): kept = kept + rotate(parts[..., k * width:(k + 1) * width], k).astype(F32)]
  transfers between devices with their start and end apart: 63 -> 63, of which waited for: 25 -> 22; matrix products, arithmetic and copies ran while one was open for 26% -> 5% of each run, Pallas kernels for 0% -> 15%
where the time goes in v2:
time: 316 us
  starting transfers between devices  126 us (40%)
  waiting for transfers between devices  123 us (39%)
  Pallas kernels  47.1 us (15%)
  local copies, waits for them, and re-layouts  13.3 us (4%)
  other arithmetic  5.24 us (2%)
    ppermute x24, starting transfers between devices, rotate(): lax.ppermute(block, 'dp', [(i, (i + shift) % count) for i in range(count)])  87.8 us
    ppermute x24, waiting for transfers between devices, rotate(): lax.ppermute(block, 'dp', [(i, (i + shift) % count) for i in range(count)])  58 us
    ppermute x15, waiting for transfers between devices, swap_section(): return lax.ppermute(block, 'section', [(0, 1), (1, 0)])  53.3 us
    pallas_call x9, Pallas kernels, call(): pl.pallas_call(kernel, out_shape=outs, grid_spec=pltpu.PrefetchScalarGrid...  45.6 us
    ppermute x15, starting transfers between devices, swap_section(): return lax.ppermute(block, 'section', [(0, 1), (1, 0)])  18.3 us
    ppermute x8, starting transfers between devices, swap_both(): lax.ppermute(block, ('section', 'mp'), [(i, i ^ 6) for i in range(8)])  10.6 us
    ppermute x8, starting transfers between devices, swap_chip(): return lax.ppermute(block, 'mp', [(i, i ^ 2) for i in range(4)])  8.98 us
    ppermute x8, waiting for transfers between devices, swap_both(): lax.ppermute(block, ('section', 'mp'), [(i, i ^ 6) for i in range(8)])  7.87 us
  transfers between devices with their start and end apart: 63, of which 22 were waited for; matrix products, arithmetic and copies ran while one was open for 5% of the time, Pallas kernels for 15%

profile of v2, /device:TPU:0, one launch (start us, length us, event | category | flops | bytes accessed | tf_op | source)
XLA Modules:
  0.0 315.9 jit_solution(7430222002821551365)
XLA Ops:
  8.1 8.9 %collective-permute-done = bf16[2,1024,128]{2,1,0:T(8,128)(2,1)S(1)} collective-permute-done((bf16[2,1024,128]{2,1,0:T(8,128)(2,1)S(1)}, bf16[2,1024,128]{2,1,0:T(8,128)(2,1)S(1)}, u32[]{:S(2)}, u32[]{:S(2)}) %collective-permute-start) | collective-permute-done | bytes 524320 | tf_op jit(solution)/shard_map/ppermute | solution.py:35
  25.9 4.9 %collective-permute-done.12.refs_7_.refs_13_ = bf16[1024,128]{1,0:T(8,128)(2,1)S(1)} collective-permute-done((bf16[1024,128]{1,0:T(8,128)(2,1)S(1)}, bf16[1024,128]{1,0:T(8,128)(2,1)S(1)}, u32[]{:S(2)}, u32[]{:S(2)}) %collective-permute-start.12) | collective-permute-done | bytes 262176 | tf_op jit(solution)/shard_map/ppermute | solution.py:16
  30.8 12.0 %collective-permute-start.18 = (bf16[1024,128]{1,0:T(8,128)(2,1)S(1)}, bf16[1024,128]{1,0:T(8,128)(2,1)S(1)}, u32[]{:S(2)}, u32[]{:S(2)}) collective-permute-start(bf16[1024,128]{1,0:T(8,128)(2,1)S(1)} %get-tuple-element.118.refs_2_), channel_id=1, source_target_pairs={{0,2},{1,3},{2,0},{3,1},{4,6},{5,7},{6,4},{7,5},{8,10},{9,11},{10,... | collective-permute-start | bytes 786440 | tf_op jit(solution)/shard_map/ppermute | solution.py:16
  42.8 14.9 %collective-permute-start.17 = (bf16[1024,128]{1,0:T(8,128)(2,1)S(1)}, bf16[1024,128]{1,0:T(8,128)(2,1)S(1)}, u32[]{:S(2)}, u32[]{:S(2)}) collective-permute-start(bf16[1024,128]{1,0:T(8,128)(2,1)S(1)} %get-tuple-element.118.refs_2_), channel_id=1, source_target_pairs={{0,3},{1,0},{2,1},{3,2},{4,7},{5,4},{6,5},{7,6},{8,11},{9,8},{10,9... | collective-permute-start | bytes 786440 | tf_op jit(solution)/shard_map/ppermute | solution.py:16
  79.1 22.5 %collective-permute-done.22.refs_3_ = bf16[128,512]{1,0:T(8,128)(2,1)S(1)} collective-permute-done((bf16[128,512]{1,0:T(8,128)(2,1)S(1)}, bf16[128,512]{1,0:T(8,128)(2,1)S(1)}, u32[]{:S(2)}, u32[]{:S(2)}) %collective-permute-start.22) | collective-permute-done | bytes 131104 | tf_op jit(solution)/shard_map/ppermute | solution.py:35
  110.7 4.3 %collective-permute-done.23.refs_4_ = bf16[128,512]{1,0:T(8,128)(2,1)S(1)} collective-permute-done((bf16[128,512]{1,0:T(8,128)(2,1)S(1)}, bf16[128,512]{1,0:T(8,128)(2,1)S(1)}, u32[]{:S(2)}, u32[]{:S(2)}) %collective-permute-start.23) | collective-permute-done | bytes 131104 | tf_op jit(solution)/shard_map/ppermute | solution.py:47
  118.4 4.8 %collective-permute-done.4.refs_6_.refs_13_ = bf16[1024,128]{1,0:T(8,128)(2,1)S(1)} collective-permute-done((bf16[1024,128]{1,0:T(8,128)(2,1)S(1)}, bf16[1024,128]{1,0:T(8,128)(2,1)S(1)}, u32[]{:S(2)}, u32[]{:S(2)}) %collective-permute-start.4) | collective-permute-done | bytes 262176 | tf_op jit(solution)/shard_map/ppermute | solution.py:16
  129.5 4.6 %collective-permute-start.30 = (bf16[1024,128]{1,0:T(8,128)(2,1)S(1)}, bf16[1024,128]{1,0:T(8,128)(2,1)S(1)}, u32[]{:S(2)}, u32[]{:S(2)}) collective-permute-start(bf16[1024,128]{1,0:T(8,128)(2,1)S(1)} %get-tuple-element.116.refs_14_), channel_id=1, source_target_pairs={{0,1},{1,2},{2,3},{3,0},{4,5},{5,6},{6,7},{7,4},{8,9},{9,10},{10,1... | collective-permute-start | bytes 786440 | tf_op jit(solution)/shard_map/ppermute | solution.py:16
  138.1 5.4 %collective-permute-done.30.refs_17_ = bf16[1024,128]{1,0:T(8,128)(2,1)S(1)} collective-permute-done((bf16[1024,128]{1,0:T(8,128)(2,1)S(1)}, bf16[1024,128]{1,0:T(8,128)(2,1)S(1)}, u32[]{:S(2)}, u32[]{:S(2)}) %collective-permute-start.30) | collective-permute-done | bytes 262176 | tf_op jit(solution)/shard_map/ppermute | solution.py:16
  144.2 10.0 %collective-permute-done.29.refs_16_ = bf16[1024,128]{1,0:T(8,128)(2,1)S(1)} collective-permute-done((bf16[1024,128]{1,0:T(8,128)(2,1)S(1)}, bf16[1024,128]{1,0:T(8,128)(2,1)S(1)}, u32[]{:S(2)}, u32[]{:S(2)}) %collective-permute-start.29) | collective-permute-done | bytes 262176 | tf_op jit(solution)/shard_map/ppermute | solution.py:16
  158.2 8.6 %first_back.1 = (bf16[4,128,1024]{2,1,0:T(8,128)(2,1)S(1)}, bf16[4,128,1024]{2,1,0:T(8,128)(2,1)}, bf16[2,2,128,512]{3,2,1,0:T(8,128)(2,1)S(1)}, bf16[2,2,128,512]{3,2,1,0:T(8,128)(2,1)S(1)}) custom-call(s32[13]{0:T(128)S(1)} %concatenate.15.refs_0_.place, bf16[8,128,2048]{2,1,0:T(8,128)(2,1)} %bitcast.71, bf16[4,128,1024]{2,1,0:T(8,128)(2,1)} %copy-done, ...), custom_call_target="tpu_custom_call" | custom-call | flops 2147483648 | bytes 16007168 | tf_op jit(solution)/shard_map/first_back/pallas_call | solution.py:287
  180.6 5.0 %top_grad.1 = (f32[128,1024]{1,0:T(8,128)S(1)}, bf16[128,1024]{1,0:T(8,128)(2,1)S(1)}, bf16[128,1024]{1,0:T(8,128)(2,1)S(1)}, bf16[128,1024]{1,0:T(8,128)(2,1)S(1)}) custom-call(s32[13]{0:T(128)S(1)} %concatenate.15.refs_0_.place, bf16[8,128,2048]{2,1,0:T(8,128)(2,1)} %top.1, bf16[128,512]{1,0:T(8,128)(2,1)S(1)} %get-tuple-element.97.p0, ...), custom_call_target="tpu_custom_call" | custom-call | flops 1073741824 | bytes 6553600 | tf_op jit(solution)/shard_map/top_grad/pallas_call | solution.py:287
  185.6 5.4 %collective-permute-start.57 = (bf16[128,1024]{1,0:T(8,128)(2,1)S(1)}, bf16[128,1024]{1,0:T(8,128)(2,1)S(1)}, u32[]{:S(2)}, u32[]{:S(2)}) collective-permute-start(bf16[128,1024]{1,0:T(8,128)(2,1)S(1)} %get-tuple-element.99), channel_id=1, source_target_pairs={{0,1},{1,2},{2,3},{3,0},{4,5},{5,6},{6,7},{7,4},{8,9},{9,10},{10,1... | collective-permute-start | bytes 786440 | tf_op jit(solution)/shard_map/ppermute | solution.py:16
  205.9 4.3 %collective-permute-done.58 = bf16[128,1024]{1,0:T(8,128)(2,1)S(1)} collective-permute-done((bf16[128,1024]{1,0:T(8,128)(2,1)S(1)}, bf16[128,1024]{1,0:T(8,128)(2,1)S(1)}, u32[]{:S(2)}, u32[]{:S(2)}) %collective-permute-start.58) | collective-permute-done | bytes 262176 | tf_op jit(solution)/shard_map/ppermute | solution.py:16
  210.2 4.9 %in_grad.3 = (f32[128,1024]{1,0:T(8,128)S(1)}, bf16[128,1024]{1,0:T(8,128)(2,1)S(1)}, bf16[128,1024]{1,0:T(8,128)(2,1)S(1)}, bf16[128,1024]{1,0:T(8,128)(2,1)S(1)}) custom-call(s32[13]{0:T(128)S(1)} %concatenate.15.refs_0_.place, bf16[8,128,2048]{2,1,0:T(8,128)(2,1)} %bitcast.72, bf16[4,128,1024]{2,1,0:T(8,128)(2,1)S(1)} %copy-done.1, ...), custom_call_target="tpu_custom_call" | custom-call | flops 1073741824 | bytes 7880704 | tf_op jit(solution)/shard_map/in_grad/pallas_call | solution.py:287
  219.2 8.0 %collective-permute-start.42 = (bf16[128,1024]{1,0:T(8,128)(2,1)S(1)}, bf16[128,1024]{1,0:T(8,128)(2,1)S(1)}, u32[]{:S(2)}, u32[]{:S(2)}) collective-permute-start(bf16[128,1024]{1,0:T(8,128)(2,1)S(1)} %get-tuple-element.87), channel_id=1, source_target_pairs={{0,1},{1,2},{2,3},{3,0},{4,5},{5,6},{6,7},{7,4},{8,9},{9,10},{10,1... | collective-permute-start | bytes 786440 | tf_op jit(solution)/shard_map/ppermute | solution.py:16
  227.3 5.9 %collective-permute-start.43 = (bf16[128,1024]{1,0:T(8,128)(2,1)S(1)}, bf16[128,1024]{1,0:T(8,128)(2,1)S(1)}, u32[]{:S(2)}, u32[]{:S(2)}) collective-permute-start(bf16[128,1024]{1,0:T(8,128)(2,1)S(1)} %get-tuple-element.88), channel_id=1, source_target_pairs={{0,2},{1,3},{2,0},{3,1},{4,6},{5,7},{6,4},{7,5},{8,10},{9,11},{10,... | collective-permute-start | bytes 786440 | tf_op jit(solution)/shard_map/ppermute | solution.py:16
  233.2 9.3 %collective-permute-done.51 = bf16[128,1024]{1,0:T(8,128)(2,1)S(1)} collective-permute-done((bf16[128,1024]{1,0:T(8,128)(2,1)S(1)}, bf16[128,1024]{1,0:T(8,128)(2,1)S(1)}, u32[]{:S(2)}, u32[]{:S(2)}) %collective-permute-start.51) | collective-permute-done | bytes 262176 | tf_op jit(solution)/shard_map/ppermute | solution.py:16
  246.7 4.9 %in_grad.2 = (f32[128,1024]{1,0:T(8,128)S(1)}, bf16[128,1024]{1,0:T(8,128)(2,1)S(1)}, bf16[128,1024]{1,0:T(8,128)(2,1)S(1)}, bf16[128,1024]{1,0:T(8,128)(2,1)S(1)}) custom-call(s32[13]{0:T(128)S(1)} %concatenate.15.refs_0_.place, bf16[8,128,2048]{2,1,0:T(8,128)(2,1)} %bitcast.73, bf16[4,128,1024]{2,1,0:T(8,128)(2,1)S(1)} %collective-permute-done.2.refs_2_, ...), custom_call_target="tpu_custom_call" | custom-call | flops 1073741824 | bytes 7880704 | tf_op jit(solution)/shard_map/in_grad/pallas_call | solution.py:287
  257.0 5.3 %collective-permute-start.41 = (bf16[128,1024]{1,0:T(8,128)(2,1)S(1)}, bf16[128,1024]{1,0:T(8,128)(2,1)S(1)}, u32[]{:S(2)}, u32[]{:S(2)}) collective-permute-start(bf16[128,1024]{1,0:T(8,128)(2,1)S(1)} %get-tuple-element.85), channel_id=1, source_target_pairs={{0,3},{1,0},{2,1},{3,2},{4,7},{5,4},{6,5},{7,6},{8,11},{9,8},{10,9... | collective-permute-start | bytes 786440 | tf_op jit(solution)/shard_map/ppermute | solution.py:16
  265.0 11.3 %collective-permute-done.40 = bf16[128,1024]{1,0:T(8,128)(2,1)S(1)} collective-permute-done((bf16[128,1024]{1,0:T(8,128)(2,1)S(1)}, bf16[128,1024]{1,0:T(8,128)(2,1)S(1)}, u32[]{:S(2)}, u32[]{:S(2)}) %collective-permute-start.40) | collective-permute-done | bytes 262176 | tf_op jit(solution)/shard_map/ppermute | solution.py:16
  278.8 6.3 %last_back.1 = (bf16[4,128,1024]{2,1,0:T(8,128)(2,1)S(1)}, bf16[4,128,1024]{2,1,0:T(8,128)(2,1)}) custom-call(s32[13]{0:T(128)S(1)} %concatenate.15.refs_0_.place, bf16[8,128,2048]{2,1,0:T(8,128)(2,1)} %bitcast.74, bf16[4,128,1024]{2,1,0:T(8,128)(2,1)S(1)} %collective-permute-done.2.refs_2_, f32[2,2048]{1,0:T(2,128)S(1)} %copy-done.4, ...), custom_call_target="tpu_custom_call" | custom-call | flops 1073741824 | bytes 11812864 | tf_op jit(solution)/shard_map/last_back/pallas_call | solution.py:287
  287.2 6.9 %collective-permute-done.45 = bf16[128,1024]{1,0:T(8,128)(2,1)} collective-permute-done((bf16[128,1024]{1,0:T(8,128)(2,1)S(1)}, bf16[128,1024]{1,0:T(8,128)(2,1)}, u32[]{:S(2)}, u32[]{:S(2)}) %collective-permute-start.45) | collective-permute-done | bytes 262176 | tf_op jit(solution)/shard_map/ppermute | solution.py:35
  301.0 12.6 %collective-permute-done.62 = bf16[4,128,1024]{2,1,0:T(8,128)(2,1)} collective-permute-done((bf16[4,128,1024]{2,1,0:T(8,128)(2,1)}, bf16[4,128,1024]{2,1,0:T(8,128)(2,1)}, u32[]{:S(2)}, u32[]{:S(2)}) %collective-permute-start.62) | collective-permute-done | bytes 1048608 | tf_op jit(solution)/shard_map/ppermute | solution.py:35
  (161 shorter events, 124.0 us)
Async XLA Ops:
  17.0 40.9 %collective-permute-start.1 = (bf16[4,128,1024]{2,1,0:T(8,128)(2,1)}, bf16[4,128,1024]{2,1,0:T(8,128)(2,1)S(1)}, u32[]{:S(2)}, u32[]{:S(2)}) collective-permute-start(bf16[4,128,1024]{2,1,0:T(8,128)(2,1)} %get-tuple-element.54), channel_id=1, source_target_pairs={{0,16},{16,0},{1,17},{17,1},{2,18},{18,2},{3,19},{19,3},{4,20},{20... | collective-permute-start | bytes 3145736 | tf_op jit(solution)/shard_map/ppermute | solution.py:35
  21.3 21.5 %collective-permute-start.11 = (bf16[1024,128]{1,0:T(8,128)(2,1)S(1)}, bf16[1024,128]{1,0:T(8,128)(2,1)S(1)}, u32[]{:S(2)}, u32[]{:S(2)}) collective-permute-start(bf16[1024,128]{1,0:T(8,128)(2,1)S(1)} %get-tuple-element.119.refs_4_.refs_10_), channel_id=1, source_target_pairs={{0,2},{1,3},{2,0},{3,1},{4,6},{5,7},{6,4},{7,5},{8,10},{9,11},{10,... | collective-permute-start | bytes 786440 | tf_op jit(solution)/shard_map/ppermute | solution.py:16
  23.8 34.0 %collective-permute-start.10 = (bf16[1024,128]{1,0:T(8,128)(2,1)S(1)}, bf16[1024,128]{1,0:T(8,128)(2,1)S(1)}, u32[]{:S(2)}, u32[]{:S(2)}) collective-permute-start(bf16[1024,128]{1,0:T(8,128)(2,1)S(1)} %get-tuple-element.119.refs_4_.refs_10_), channel_id=1, source_target_pairs={{0,3},{1,0},{2,1},{3,2},{4,7},{5,4},{6,5},{7,6},{8,11},{9,8},{10,9... | collective-permute-start | bytes 786440 | tf_op jit(solution)/shard_map/ppermute | solution.py:16
  25.2 36.9 %collective-permute-start.19 = (bf16[1024,128]{1,0:T(8,128)(2,1)S(1)}, bf16[1024,128]{1,0:T(8,128)(2,1)S(1)}, u32[]{:S(2)}, u32[]{:S(2)}) collective-permute-start(bf16[1024,128]{1,0:T(8,128)(2,1)S(1)} %get-tuple-element.118.refs_2_), channel_id=1, source_target_pairs={{0,1},{1,2},{2,3},{3,0},{4,5},{5,6},{6,7},{7,4},{8,9},{9,10},{10,1... | collective-permute-start | bytes 786440 | tf_op jit(solution)/shard_map/ppermute | solution.py:16
  30.8 31.5 %collective-permute-start.18 = (bf16[1024,128]{1,0:T(8,128)(2,1)S(1)}, bf16[1024,128]{1,0:T(8,128)(2,1)S(1)}, u32[]{:S(2)}, u32[]{:S(2)}) collective-permute-start(bf16[1024,128]{1,0:T(8,128)(2,1)S(1)} %get-tuple-element.118.refs_2_), channel_id=1, source_target_pairs={{0,2},{1,3},{2,0},{3,1},{4,6},{5,7},{6,4},{7,5},{8,10},{9,11},{10,... | collective-permute-start | bytes 786440 | tf_op jit(solution)/shard_map/ppermute | solution.py:16
  42.8 22.1 %collective-permute-start.17 = (bf16[1024,128]{1,0:T(8,128)(2,1)S(1)}, bf16[1024,128]{1,0:T(8,128)(2,1)S(1)}, u32[]{:S(2)}, u32[]{:S(2)}) collective-permute-start(bf16[1024,128]{1,0:T(8,128)(2,1)S(1)} %get-tuple-element.118.refs_2_), channel_id=1, source_target_pairs={{0,3},{1,0},{2,1},{3,2},{4,7},{5,4},{6,5},{7,6},{8,11},{9,8},{10,9... | collective-permute-start | bytes 786440 | tf_op jit(solution)/shard_map/ppermute | solution.py:16
  69.2 55.4 %collective-permute-start.2 = (bf16[4,128,1024]{2,1,0:T(8,128)(2,1)S(1)}, bf16[4,128,1024]{2,1,0:T(8,128)(2,1)S(1)}, u32[]{:S(2)}, u32[]{:S(2)}) collective-permute-start(bf16[4,128,1024]{2,1,0:T(8,128)(2,1)S(1)} %copy-done.7), channel_id=1, source_target_pairs={{0,16},{16,0},{1,17},{17,1},{2,18},{18,2},{3,19},{19,3},{4,20},{20... | collective-permute-start | bytes 3145736 | tf_op jit(solution)/shard_map/ppermute | solution.py:35
  72.8 28.8 %collective-permute-start.22 = (bf16[128,512]{1,0:T(8,128)(2,1)S(1)}, bf16[128,512]{1,0:T(8,128)(2,1)S(1)}, u32[]{:S(2)}, u32[]{:S(2)}) collective-permute-start(bf16[128,512]{1,0:T(8,128)(2,1)S(1)} %get-tuple-element.74), channel_id=1, source_target_pairs={{0,16},{16,0},{1,17},{17,1},{2,18},{18,2},{3,19},{19,3},{4,20},{20... | collective-permute-start | bytes 393224 | tf_op jit(solution)/shard_map/ppermute | solution.py:35
  73.4 31.6 %collective-permute-start.14 = (bf16[128,640]{1,0:T(8,128)(2,1)S(1)}, bf16[128,640]{1,0:T(8,128)(2,1)S(1)}, u32[]{:S(2)}, u32[]{:S(2)}) collective-permute-start(bf16[128,640]{1,0:T(8,128)(2,1)S(1)} %get-tuple-element.66), channel_id=1, source_target_pairs={{0,8},{4,12},{8,0},{12,4},{1,9},{5,13},{9,1},{13,5},{2,10},{6,14},... | collective-permute-start | bytes 491528 | tf_op jit(solution)/shard_map/ppermute | solution.py:43
  74.0 32.6 %collective-permute-start.15 = (bf16[128,640]{1,0:T(8,128)(2,1)S(1)}, bf16[128,640]{1,0:T(8,128)(2,1)S(1)}, u32[]{:S(2)}, u32[]{:S(2)}) collective-permute-start(bf16[128,640]{1,0:T(8,128)(2,1)S(1)} %get-tuple-element.67), channel_id=1, source_target_pairs={{0,16},{16,0},{1,17},{17,1},{2,18},{18,2},{3,19},{19,3},{4,20},{20... | collective-permute-start | bytes 491528 | tf_op jit(solution)/shard_map/ppermute | solution.py:35
  77.6 31.5 %collective-permute-start.16 = (bf16[128,640]{1,0:T(8,128)(2,1)S(1)}, bf16[128,640]{1,0:T(8,128)(2,1)S(1)}, u32[]{:S(2)}, u32[]{:S(2)}) collective-permute-start(bf16[128,640]{1,0:T(8,128)(2,1)S(1)} %get-tuple-element.68), channel_id=1, source_target_pairs={{0,24},{4,28},{8,16},{12,20},{16,8},{20,12},{24,0},{28,4},{1,25},{... | collective-permute-start | bytes 491528 | tf_op jit(solution)/shard_map/ppermute | solution.py:47
  129.2 26.5 %collective-permute-start.27 = (bf16[2,2,128,640]{3,2,1,0:T(8,128)(2,1)S(1)}, bf16[2,2,128,640]{3,2,1,0:T(8,128)(2,1)S(1)}, u32[]{:S(2)}, u32[]{:S(2)}) collective-permute-start(bf16[2,2,128,640]{3,2,1,0:T(8,128)(2,1)S(1)} %bitcast.76), channel_id=1, source_target_pairs={{0,4},{4,0},{8,12},{12,8},{1,5},{5,1},{9,13},{13,9},{2,6},{6,2},{1... | collective-permute-start | bytes 1966088 | tf_op jit(solution)/shard_map/ppermute | solution.py:39
  137.0 20.3 %collective-permute-start.7 = (bf16[128,640]{1,0:T(8,128)(2,1)S(1)}, bf16[128,640]{1,0:T(8,128)(2,1)S(1)}, u32[]{:S(2)}, u32[]{:S(2)}) collective-permute-start(bf16[128,640]{1,0:T(8,128)(2,1)S(1)} %get-tuple-element.59), channel_id=1, source_target_pairs={{0,8},{4,12},{8,0},{12,4},{1,9},{5,13},{9,1},{13,5},{2,10},{6,14},... | collective-permute-start | bytes 491528 | tf_op jit(solution)/shard_map/ppermute | solution.py:43
  143.5 25.6 %collective-permute-start.55 = (bf16[128,512]{1,0:T(8,128)(2,1)S(1)}, bf16[128,512]{1,0:T(8,128)(2,1)S(1)}, u32[]{:S(2)}, u32[]{:S(2)}) collective-permute-start(bf16[128,512]{1,0:T(8,128)(2,1)S(1)} %get-tuple-element.97.p0), channel_id=1, source_target_pairs={{0,24},{4,28},{8,16},{12,20},{16,8},{20,12},{24,0},{28,4},{1,25},{... | collective-permute-start | bytes 393224 | tf_op jit(solution)/shard_map/ppermute | solution.py:47
  201.7 25.6 %collective-permute-start.50 = (bf16[128,1024]{1,0:T(8,128)(2,1)S(1)}, bf16[128,1024]{1,0:T(8,128)(2,1)S(1)}, u32[]{:S(2)}, u32[]{:S(2)}) collective-permute-start(bf16[128,1024]{1,0:T(8,128)(2,1)S(1)} %get-tuple-element.94), channel_id=1, source_target_pairs={{0,1},{1,2},{2,3},{3,0},{4,5},{5,6},{6,7},{7,4},{8,9},{9,10},{10,1... | collective-permute-start | bytes 786440 | tf_op jit(solution)/shard_map/ppermute | solution.py:16
  201.7 40.8 %collective-permute-start.51 = (bf16[128,1024]{1,0:T(8,128)(2,1)S(1)}, bf16[128,1024]{1,0:T(8,128)(2,1)S(1)}, u32[]{:S(2)}, u32[]{:S(2)}) collective-permute-start(bf16[128,1024]{1,0:T(8,128)(2,1)S(1)} %get-tuple-element.95), channel_id=1, source_target_pairs={{0,2},{1,3},{2,0},{3,1},{4,6},{5,7},{6,4},{7,5},{8,10},{9,11},{10,... | collective-permute-start | bytes 786440 | tf_op jit(solution)/shard_map/ppermute | solution.py:16
  203.5 39.0 %collective-permute-start.52 = (bf16[128,1024]{1,0:T(8,128)(2,1)S(1)}, bf16[128,1024]{1,0:T(8,128)(2,1)S(1)}, u32[]{:S(2)}, u32[]{:S(2)}) collective-permute-start(bf16[128,1024]{1,0:T(8,128)(2,1)S(1)} %get-tuple-element.96), channel_id=1, source_target_pairs={{0,3},{1,0},{2,1},{3,2},{4,7},{5,4},{6,5},{7,6},{8,11},{9,8},{10,9... | collective-permute-start | bytes 786440 | tf_op jit(solution)/shard_map/ppermute | solution.py:16
  210.2 36.5 %collective-permute-start.38 = (bf16[2,2,128,640]{3,2,1,0:T(8,128)(2,1)S(1)}, bf16[2,2,128,640]{3,2,1,0:T(8,128)(2,1)S(1)}, u32[]{:S(2)}, u32[]{:S(2)}) collective-permute-start(bf16[2,2,128,640]{3,2,1,0:T(8,128)(2,1)S(1)} %bitcast.75), channel_id=1, source_target_pairs={{0,4},{4,0},{8,12},{12,8},{1,5},{5,1},{9,13},{13,9},{2,6},{6,2},{1... | collective-permute-start | bytes 1966088 | tf_op jit(solution)/shard_map/ppermute | solution.py:39
  219.2 36.2 %collective-permute-start.42 = (bf16[128,1024]{1,0:T(8,128)(2,1)S(1)}, bf16[128,1024]{1,0:T(8,128)(2,1)S(1)}, u32[]{:S(2)}, u32[]{:S(2)}) collective-permute-start(bf16[128,1024]{1,0:T(8,128)(2,1)S(1)} %get-tuple-element.87), channel_id=1, source_target_pairs={{0,1},{1,2},{2,3},{3,0},{4,5},{5,6},{6,7},{7,4},{8,9},{9,10},{10,1... | collective-permute-start | bytes 786440 | tf_op jit(solution)/shard_map/ppermute | solution.py:16
  227.3 29.7 %collective-permute-start.43 = (bf16[128,1024]{1,0:T(8,128)(2,1)S(1)}, bf16[128,1024]{1,0:T(8,128)(2,1)S(1)}, u32[]{:S(2)}, u32[]{:S(2)}) collective-permute-start(bf16[128,1024]{1,0:T(8,128)(2,1)S(1)} %get-tuple-element.88), channel_id=1, source_target_pairs={{0,2},{1,3},{2,0},{3,1},{4,6},{5,7},{6,4},{7,5},{8,10},{9,11},{10,... | collective-permute-start | bytes 786440 | tf_op jit(solution)/shard_map/ppermute | solution.py:16
  244.3 20.7 %collective-permute-start.44 = (bf16[128,1024]{1,0:T(8,128)(2,1)S(1)}, bf16[128,1024]{1,0:T(8,128)(2,1)S(1)}, u32[]{:S(2)}, u32[]{:S(2)}) collective-permute-start(bf16[128,1024]{1,0:T(8,128)(2,1)S(1)} %get-tuple-element.89), channel_id=1, source_target_pairs={{0,3},{1,0},{2,1},{3,2},{4,7},{5,4},{6,5},{7,6},{8,11},{9,8},{10,9... | collective-permute-start | bytes 786440 | tf_op jit(solution)/shard_map/ppermute | solution.py:16
  255.4 20.8 %collective-permute-start.40 = (bf16[128,1024]{1,0:T(8,128)(2,1)S(1)}, bf16[128,1024]{1,0:T(8,128)(2,1)S(1)}, u32[]{:S(2)}, u32[]{:S(2)}) collective-permute-start(bf16[128,1024]{1,0:T(8,128)(2,1)S(1)} %get-tuple-element.84), channel_id=1, source_target_pairs={{0,2},{1,3},{2,0},{3,1},{4,6},{5,7},{6,4},{7,5},{8,10},{9,11},{10,... | collective-permute-start | bytes 786440 | tf_op jit(solution)/shard_map/ppermute | solution.py:16
  262.2 35.5 %collective-permute-start.61 = (bf16[4,128,1024]{2,1,0:T(8,128)(2,1)S(1)}, bf16[4,128,1024]{2,1,0:T(8,128)(2,1)}, u32[]{:S(2)}, u32[]{:S(2)}) collective-permute-start(bf16[4,128,1024]{2,1,0:T(8,128)(2,1)S(1)} %copy-done.3), channel_id=1, source_target_pairs={{0,16},{16,0},{1,17},{17,1},{2,18},{18,2},{3,19},{19,3},{4,20},{20... | collective-permute-start | bytes 3145736 | tf_op jit(solution)/shard_map/ppermute | solution.py:35
  285.1 28.5 %collective-permute-start.62 = (bf16[4,128,1024]{2,1,0:T(8,128)(2,1)}, bf16[4,128,1024]{2,1,0:T(8,128)(2,1)}, u32[]{:S(2)}, u32[]{:S(2)}) collective-permute-start(bf16[4,128,1024]{2,1,0:T(8,128)(2,1)} %get-tuple-element.104), channel_id=1, source_target_pairs={{0,16},{16,0},{1,17},{17,1},{2,18},{18,2},{3,19},{19,3},{4,20},{20... | collective-permute-start | bytes 3145736 | tf_op jit(solution)/shard_map/ppermute | solution.py:35
  (48 other events, 800.8 us)

commit v3 on v2

--- a/solution.py
+++ b/solution.py
@@ -31,6 +31,18 @@
     return kept
 
 
+def trade_inner(block):
+    return lax.ppermute(block, "dp", [(1, 2), (2, 1)])
+
+
+def trade_outward(block):
+    return lax.ppermute(block, "dp", [(2, 3), (1, 0)])
+
+
+def trade_inward(block):
+    return lax.ppermute(block, "dp", [(3, 2), (0, 1)])
+
+
 def swap_section(block):
     return lax.ppermute(block, "section", [(0, 1), (1, 0)])
 
@@ -113,7 +125,7 @@
 
 def hidden_kernel(group, place, own, received, gain, w0, w1, w2, w3, sent, kept, weights, rows):
     step, b, which = step_place()
-    join_units(step, (w0, w1, w2, w3), weights)
+    join_units(step, (w0.at[0], w1.at[0], w2.at[0], w3.at[0]), weights)
     load_set(place, (own, received), rows)
     wide = rows[...].astype(F32)
     normed = (wide * gain[group : group + 1, :]).astype(BF16)
@@ -123,12 +135,21 @@
     put_partial(packed, sent, kept, step, which)
 
 
-def top_kernel(phase, place, top, w0, w1, w2, w3, sent, kept, weights, rows):
-    step, b, which = step_place()
-    join_units(step, (w0, w1, w2, w3), weights)
-    load_top(phase, place, top, rows)
-    part = jnp.dot(rows[...], weights[...], preferred_element_type=F32)
-    put_partial(part, sent, kept, step, which)
+def first_part_kernel(
+    group, place, own, received, gain, top, w0, w1, w2, w3, sent, kept, weights, outward, rows
+):
+    step, b, which = step_place()
+    join_units(step, (w0.at[0], w1.at[0], w2.at[0], w3.at[0]), weights)
+    join_units(step, (w0.at[1], w1.at[1], w2.at[1], w3.at[1]), outward)
+    load_set(place, (own, received), rows)
+    wide = rows[...].astype(F32)
+    normed = (wide * gain[group : group + 1, :]).astype(BF16)
+    part = jnp.dot(normed, weights[...], preferred_element_type=F32)
+    squares = jnp.sum(wide * wide, axis=1, keepdims=True)
+    load_top(0, place, top, rows)
+    top_part = jnp.dot(rows[...], outward[...], preferred_element_type=F32)
+    padded = jnp.broadcast_to(squares, (part.shape[0], PAD))
+    put_partial(jnp.concatenate((part, padded, top_part), axis=1), sent, kept, step, which)
 
 
 def back_step(group, place, own, received, gain, spread, weights, rows, incoming):
@@ -164,8 +185,8 @@
     result0, result1, sent, kept, weights, outward, spread, rows, grads,
 ):
     step, b, which = step_place()
-    join_units(step, (w0, w1, w2, w3), weights)
-    join_units(step, (v0, v1, v2, v3), outward)
+    join_units(step, (w0.at[0], w1.at[0], w2.at[0], w3.at[0]), weights)
+    join_units(step, (v0.at[1], v1.at[1], v2.at[1], v3.at[1]), outward)
     join_slots(step, (p0, p1, p2, p3, p4), spread)
     load_top(0, place, top, grads)
     result = back_step(group, place, own, received, gain, spread, weights, rows, grads[...])
@@ -179,7 +200,7 @@
     result0, result1, weights, spread, rows, grads,
 ):
     step, b, which = step_place()
-    join_units(step, (w0, w1, w2, w3), weights)
+    join_units(step, (w0.at[0], w1.at[0], w2.at[0], w3.at[0]), weights)
     join_slots(step, (p0, p1, p2, p3, p4), spread)
     load_set(place, (in0, in1), grads)
     result = back_step(group, place, own, received, gain, spread, weights, rows, grads[...])
@@ -198,13 +219,13 @@
         total[...] += part
 
 
-def put_grad(step, total, kept, parts):
+def put_grad(step, total, kept, parts, at=0):
     @pl.when(step == STEPS - 1)
     def _():
-        height = kept.shape[0]
-        kept[...] = total[:height]
+        height = kept.shape[1]
+        kept[at] = total[:height]
         for k, part in enumerate(parts):
-            part[...] = total[(k + 1) * height : (k + 2) * height].astype(BF16)
+            part[at] = total[(k + 1) * height : (k + 2) * height].astype(BF16)
 
 
 def in_grad_kernel(
@@ -219,13 +240,21 @@
     put_grad(step, total, kept, (c1, c2, c3))
 
 
-def top_grad_kernel(place, top, p0, p1, p2, p3, p4, kept, c1, c2, c3, total, spread, rows):
+def first_grad_kernel(
+    group, place, own, received, gain, top, p0, p1, p2, p3, p4, a0, a1, a2, a3, a4,
+    kept, c1, c2, c3, total, out_total, spread, active, rows,
+):
     step, b, which = step_place()
     join_slots(step, (p0, p1, p2, p3, p4), spread)
+    join_slots(step, (a0, a1, a2, a3, a4), active)
+    load_set(place, (own, received), rows)
+    normed = (rows[...].astype(F32) * gain[group : group + 1, :]).astype(BF16)
+    packed = spread[b, which].reshape(rows.shape[0], spread.shape[-1])
+    add_grad(step, total, packed[:, : total.shape[0]], normed)
     load_top(0, place, top, rows)
-    packed = spread[b, which].reshape(rows.shape[0], spread.shape[-1])
-    add_grad(step, total, packed, rows[...])
-    put_grad(step, total, kept, (c1, c2, c3))
+    add_grad(step, out_total, active[b, which].reshape(rows.shape[0], active.shape[-1]), rows[...])
+    put_grad(step, total, kept, (c1, c2, c3), 0)
+    put_grad(step, out_total, kept, (c1, c2, c3), 1)
 
 
 def out_grad_kernel(place, in0, in1, p0, p1, p2, p3, p4, kept, c1, c2, c3, total, spread, rows):
@@ -259,15 +288,26 @@
     activated[...] = terms[3]
 
 
-def unit_kernel(features, hidden, own, chip, section, both, packed):
-    units = own.shape[1]
+def put_units(features, hidden, unit_grads, packed):
+    units = unit_grads.shape[1]
     unit_sums, square_sums = hidden[:, :units], hidden[:, units : units + 1]
-    inverse_rms, hidden_pre, sigma, _ = row_terms(unit_sums, square_sums, features)
+    inverse_rms, hidden_pre, sigma, activated = row_terms(unit_sums, square_sums, features)
     scaled_grad, factor = unit_terms(
-        whole_sum(own, chip, section, both), unit_sums, inverse_rms, hidden_pre, sigma, features
+        unit_grads, unit_sums, inverse_rms, hidden_pre, sigma, features
     )
     packed[:, :units] = scaled_grad
     packed[:, units:] = jnp.broadcast_to(factor, (factor.shape[0], PAD)).astype(BF16)
+    return activated
+
+
+def first_unit_kernel(features, own, chip, section, both, packed, activated):
+    units = activated.shape[1]
+    total = whole_sum(own, chip, section, both)
+    activated[...] = put_units(features, total, total[:, units + PAD :], packed)
+
+
+def unit_kernel(features, hidden, own, chip, section, both, packed):
+    put_units(features, hidden, whole_sum(own, chip, section, both), packed)
 
 
 def call(kernel, name, outs, args, scratch=(), specs=None, place=None, flops=0):
@@ -344,19 +384,28 @@
         first = half * place[OWN + phase]
         return lax.dynamic_slice(stored, (first, 0, other * part), (half, tokens, part))
 
-    received = [None, None]
-    received[0] = swap_section(after(sent_inputs(0), moved))
-    received[1] = swap_section(after(sent_inputs(1), received[0]))
-
-    def unit_parts(block):
-        count = lax.axis_size("dp")
-        return (block,) + tuple(rotate(block, -k) for k in range(1, count))
-
-    in_parts, out_parts = [], []
-    for phase in range(2):
-        held = jnp.where(own == 1 - phase, mine, moved)
-        in_parts.append(unit_parts(held[0]))
-        out_parts.append(unit_parts(held[1]))
+    received = swap_section(after(jnp.stack((sent_inputs(0), sent_inputs(1))), moved))
+
+    position = lax.axis_index("dp")
+
+    def near(block):
+        return rotate(block, 1), rotate(block, -1)
+
+    def far(below, above):
+        inner = trade_inner(jnp.where(position == 1, below, above))
+        outward = trade_outward(jnp.where(position == 2, below, above))
+        return inner, outward
+
+    def joined(inner, outward):
+        return jnp.where((position == 1) | (position == 2), inner, outward)
+
+    held0 = jnp.where(own == 1, mine, moved)
+    held1 = jnp.where(own == 0, mine, moved)
+    below, above = near(held0)
+    weights0 = (held0, above, joined(*far(below, above)), below)
+    below, above = near(after(held1, below, above))
+    far1 = far(below, above)
+    weights1 = (held1, above, joined(*far1), below)
     units = 4 * mine.shape[-1]
     rows2 = 2 * tokens
     gain_spec = pl.BlockSpec((2, part), lambda i, s: (0, s[SECTION]))
@@ -369,8 +418,16 @@
     spread_scratch = ((2, 2, 2, tokens, units + PAD), BF16)
     act_scratch = ((2, 2, 2, tokens, units), BF16)
     grad_scratch = ((units, part), F32)
-    grad_shapes = [shape_of((units // 4, part), F32)] + [shape_of((units // 4, part))] * 3
+    grad_shapes = [shape_of((1, units // 4, part), F32)] + [shape_of((1, units // 4, part))] * 3
     one_dot = 2 * slots * tokens * part * units
+
+    both_grad_shapes = [shape_of((2, units // 4, part), F32)] + [
+        shape_of((2, units // 4, part))
+    ] * 3
+    first_shapes = [shape_of((2, 2, tokens, 2 * units + PAD))] * 2
+
+    def received_spec(phase):
+        return pl.BlockSpec((None, half, tokens, part), lambda i, s: (phase, 0, 0, 0))
 
     def own_spec(phase):
         return pl.BlockSpec(
@@ -383,91 +440,86 @@
 
         return bound
 
-    def hidden_part(phase):
-        return call(
-            bind(hidden_kernel, 1 - phase),
-            "hidden_part",
-            hidden_shapes,
-            (stored, received[phase], gain) + in_parts[phase],
-            [weight_scratch, rows_scratch],
-            {0: own_spec(phase), 2: gain_spec},
-            place,
-            one_dot,
-        )
-
-    def hidden_terms(sums):
-        return call(
-            bind(active_kernel, features),
-            "activated",
-            [shape_of((tokens, units + PAD), F32), shape_of((tokens, units))],
-            sums,
-        )
-
-    def unit_grad_terms(hidden, sums):
-        return call(
-            bind(unit_kernel, features),
-            "unit_grads",
-            [shape_of((tokens, units + PAD))],
-            (hidden,) + sums,
-        )[0]
-
-    def in_grad(phase, scaled):
-        return call(
-            bind(in_grad_kernel, 1 - phase),
-            "in_grad",
-            grad_shapes,
-            (stored, received[phase], gain) + scaled,
-            [grad_scratch, spread_scratch, rows_scratch],
-            {0: own_spec(phase), 2: gain_spec},
-            place,
-            one_dot,
-        )
-
     def scatter(parts):
-        total = parts[0]
-        for k in range(1, 4):
-            total = total + rotate(parts[k], k).astype(F32)
-        return total
-
-    hidden0, act0 = hidden_terms(pair_sum(*hidden_part(0)))
+        kept, next_part, far_part, last_part = parts
+        inner, inward = trade_inner(far_part), trade_inward(far_part)
+        onward = jnp.where(position == 2, inner, inward)
+        backward = jnp.where(position == 1, inner, inward)
+        middle = (position == 1) | (position == 2)
+        zero = jnp.zeros((), F32)
+        forth = next_part.astype(F32) + jnp.where(middle, onward.astype(F32), zero)
+        back = last_part.astype(F32) + jnp.where(middle, backward.astype(F32), zero)
+        return kept, rotate(forth.astype(BF16), 1), rotate(back.astype(BF16), -1)
+
+    def total(parts):
+        return parts[0] + parts[1].astype(F32) + parts[2].astype(F32)
+
+    sent, kept = call(
+        bind(first_part_kernel, 1),
+        "first_part",
+        first_shapes,
+        (stored, received, gain, cotangent) + weights0,
+        [weight_scratch, weight_scratch, rows_scratch],
+        {0: own_spec(0), 1: received_spec(0), 2: gain_spec, 3: top_spec},
+        place,
+        2 * one_dot,
+    )
+    scaled0, act0 = call(
+        bind(first_unit_kernel, features),
+        "first_units",
+        [shape_of((tokens, units + PAD)), shape_of((tokens, units))],
+        pair_sum(sent, kept),
+    )
+    scaled0 = pair_spread(scaled0)
     act0 = pair_spread(act0)
-    sent, kept = call(
-        bind(top_kernel, 0),
-        "top_part",
-        partial_shapes,
-        (cotangent,) + out_parts[0],
-        [weight_scratch, rows_scratch],
-        {0: top_spec},
-        place,
-        one_dot,
-    )
-    scaled0 = pair_spread(unit_grad_terms(hidden0, pair_sum(sent, kept)))
     result0, result1, sent, kept = call(
         bind(first_back_kernel, 1),
         "first_back",
         [set_shape, set_shape] + partial_shapes,
-        (stored, received[0], gain, cotangent) + scaled0 + in_parts[0] + out_parts[1],
+        (stored, received, gain, cotangent) + scaled0 + weights0 + weights1,
         [weight_scratch, weight_scratch, spread_scratch, rows_scratch, rows_scratch],
-        {0: own_spec(0), 2: gain_spec, 3: top_spec},
+        {0: own_spec(0), 1: received_spec(0), 2: gain_spec, 3: top_spec},
         place,
         2 * one_dot,
     )
-    in_total0 = scatter(in_grad(0, scaled0))
-    out_total0 = scatter(
-        call(
-            top_grad_kernel,
-            "top_grad",
-            grad_shapes,
-            (cotangent,) + act0,
-            [grad_scratch, act_scratch, rows_scratch],
-            {0: top_spec},
-            place,
-            one_dot,
-        )
-    )
-    hidden1, act1 = hidden_terms(pair_sum(*hidden_part(1)))
+    hidden1, act1 = call(
+        bind(active_kernel, features),
+        "activated",
+        [shape_of((tokens, units + PAD), F32), shape_of((tokens, units))],
+        pair_sum(
+            *call(
+                bind(hidden_kernel, 0),
+                "hidden_part",
+                hidden_shapes,
+                (stored, received, gain) + weights1,
+                [weight_scratch, rows_scratch],
+                {0: own_spec(1), 1: received_spec(1), 2: gain_spec},
+                place,
+                one_dot,
+            )
+        ),
+    )
     act1 = pair_spread(act1)
-    out_total1 = scatter(
+    grads0 = call(
+        bind(first_grad_kernel, 1),
+        "first_grads",
+        both_grad_shapes,
+        (stored, received, gain, cotangent) + scaled0 + act0,
+        [grad_scratch, grad_scratch, spread_scratch, act_scratch, rows_scratch],
+        {0: own_spec(0), 1: received_spec(0), 2: gain_spec, 3: top_spec},
+        place,
+        2 * one_dot,
+    )
+    sums = pair_sum(sent, kept)
+    scaled1 = call(
+        bind(unit_kernel, features),
+        "unit_grads",
+        [shape_of((tokens, units + PAD))],
+        (after(hidden1, grads0[0]),) + sums,
+    )[0]
+    scaled1 = pair_spread(scaled1)
+    totals0 = scatter(grads0)
+    out_totals1 = scatter(
         call(
             out_grad_kernel,
             "out_grad",
@@ -479,20 +531,33 @@
             one_dot,
         )
     )
-    scaled1 = pair_spread(unit_grad_terms(hidden1, pair_sum(sent, kept)))
-    returned0 = swap_section(after(result1, scaled1[4]))
-    in_total1 = scatter(in_grad(1, scaled1))
+    returned0 = swap_section(after(result1, scaled1[1]))
+    in_grads1 = call(
+        bind(in_grad_kernel, 0),
+        "in_grad",
+        grad_shapes,
+        (stored, received, gain) + scaled1,
+        [grad_scratch, spread_scratch, rows_scratch],
+        {0: own_spec(1), 1: received_spec(1), 2: gain_spec},
+        place,
+        one_dot,
+    )
+    in_totals1 = scatter(in_grads1)
     result2, result3 = call(
         bind(last_back_kernel, 0),
         "last_back",
         [set_shape, set_shape],
-        (stored, received[1], gain, result1, result0) + scaled1 + in_parts[1],
+        (stored, received, gain, result1, after(result0, in_grads1[0])) + scaled1 + weights1,
         [weight_scratch, spread_scratch, rows_scratch, rows_scratch],
-        {0: own_spec(1), 2: gain_spec},
+        {0: own_spec(1), 1: received_spec(1), 2: gain_spec},
         place,
         one_dot,
     )
     returned1 = swap_section(result3)
+    total0 = total(totals0)
+    out_total1 = total(out_totals1)[0]
+    in_total1 = total(after(in_totals1, result3))[0]
+    in_total0, out_total0 = total0[0], total0[1]
     outputs = jnp.zeros_like(stored)
     for phase, block, back in ((0, result0, returned0), (1, result2, returned1)):
         first = half * place[OWN + phase]

time: 316 us -> 275 us (0.87)
  starting transfers between devices: 126 us -> 85.8 us
  waiting for transfers between devices: 123 us -> 117 us
  other arithmetic: 5.24 us -> 9.77 us
  local copies, waits for them, and re-layouts: 13.3 us -> 16.5 us
    ppermute x24 -> x10, starting transfers between devices: 87.8 us -> 29.4 us  [rotate(): lax.ppermute(block, 'dp', [(i, (i + shift) % count) for i in range(count)])]
    ppermute x0 -> x10, starting transfers between devices: none -> 23.2 us  [the longest x3 16.2 us: trade_inward(): return lax.ppermute(block, 'dp', [(3, 2), (0, 1)])]
    ppermute x0 -> x10, waiting for transfers between devices: none -> 16.3 us  [the longest x2 13.4 us: trade_outward(): return lax.ppermute(block, 'dp', [(2, 3), (1, 0)])]
    ppermute x15 -> x13, waiting for transfers between devices: 53.3 us -> 37 us  [swap_section(): return lax.ppermute(block, 'section', [(0, 1), (1, 0)])]
    ppermute x24 -> x10, waiting for transfers between devices: 58 us -> 51.7 us  [rotate(): lax.ppermute(block, 'dp', [(i, (i + shift) % count) for i in range(count)])]
    select_n x1 -> x6, other arithmetic: 0.89 us -> 4.98 us  [the longest x2 2.31 us: far(): outward = trade_outward(jnp.where(position == 2, below, above))]
    ppermute x15 -> x13, starting transfers between devices: 18.3 us -> 15.3 us  [swap_section(): return lax.ppermute(block, 'section', [(0, 1), (1, 0)])]
    pallas_call x9 -> x7, Pallas kernels: 45.6 us -> 43.1 us  [call(): pl.pallas_call(kernel, out_shape=outs, grid_spec=pltpu.PrefetchScalarGrid...]
  transfers between devices with their start and end apart: 63 -> 54, of which waited for: 22 -> 21; matrix products, arithmetic and copies ran while one was open for 5% -> 7% of each run, Pallas kernels for 15% -> 14%
where the time goes in v3:
time: 275 us; the launch traced here: 274 us
  waiting for transfers between devices  117 us (43%)
  starting transfers between devices  85.8 us (31%)
  Pallas kernels  44.5 us (16%)
  local copies, waits for them, and re-layouts  16.5 us (6%)
  other arithmetic  9.77 us (4%)
    ppermute x10, waiting for transfers between devices, rotate(): lax.ppermute(block, 'dp', [(i, (i + shift) % count) for i in range(count)])  51.7 us
    pallas_call x7, Pallas kernels, call(): pl.pallas_call(kernel, out_shape=outs, grid_spec=pltpu.PrefetchScalarGrid...  43.1 us
    ppermute x13, waiting for transfers between devices, swap_section(): return lax.ppermute(block, 'section', [(0, 1), (1, 0)])  37 us
    ppermute x10, starting transfers between devices, rotate(): lax.ppermute(block, 'dp', [(i, (i + shift) % count) for i in range(count)])  29.4 us
    ppermute x3, starting transfers between devices, trade_inward(): return lax.ppermute(block, 'dp', [(3, 2), (0, 1)])  16.2 us
    ppermute x13, starting transfers between devices, swap_section(): return lax.ppermute(block, 'section', [(0, 1), (1, 0)])  15.3 us
    ppermute x2, waiting for transfers between devices, trade_outward(): return lax.ppermute(block, 'dp', [(2, 3), (1, 0)])  13.4 us
    ppermute x7, starting transfers between devices, swap_both(): lax.ppermute(block, ('section', 'mp'), [(i, i ^ 6) for i in range(8)])  10 us
  transfers between devices with their start and end apart: 54, of which 21 were waited for; matrix products, arithmetic and copies ran while one was open for 7% of the time, Pallas kernels for 14%

profile of v3, /device:TPU:0, one launch (start us, length us, event | category | flops | bytes accessed | tf_op | source)
XLA Modules:
  0.0 274.3 jit_solution(9115266453320656637)
XLA Ops:
  8.9 8.8 %collective-permute-done = bf16[2,1024,128]{2,1,0:T(8,128)(2,1)} collective-permute-done((bf16[2,1024,128]{2,1,0:T(8,128)(2,1)S(1)}, bf16[2,1024,128]{2,1,0:T(8,128)(2,1)}, u32[]{:S(2)}, u32[]{:S(2)}) %collective-permute-start) | collective-permute-done | bytes 524320 | tf_op jit(solution)/shard_map/ppermute | solution.py:47
  20.6 3.7 %collective-permute-start.3 = (bf16[2,1024,128]{2,1,0:T(8,128)(2,1)S(1)}, bf16[2,1024,128]{2,1,0:T(8,128)(2,1)}, u32[]{:S(2)}, u32[]{:S(2)}) collective-permute-start(bf16[2,1024,128]{2,1,0:T(8,128)(2,1)S(1)} %get-tuple-element.107.refs_5_.refs_10_), channel_id=1, source_target_pairs={{0,3},{1,0},{2,1},{3,2},{4,7},{5,4},{6,5},{7,6},{8,11},{9,8},{10,9... | collective-permute-start | bytes 1572872 | tf_op jit(solution)/shard_map/ppermute | solution.py:16
  24.3 12.4 %collective-permute-done.3.refs_6_.refs_11_ = bf16[2,1024,128]{2,1,0:T(8,128)(2,1)} collective-permute-done((bf16[2,1024,128]{2,1,0:T(8,128)(2,1)S(1)}, bf16[2,1024,128]{2,1,0:T(8,128)(2,1)}, u32[]{:S(2)}, u32[]{:S(2)}) %collective-permute-start.3) | collective-permute-done | bytes 524320 | tf_op jit(solution)/shard_map/ppermute | solution.py:16
  36.7 9.9 %collective-permute-done.2.refs_8_.refs_13_ = bf16[2,1024,128]{2,1,0:T(8,128)(2,1)} collective-permute-done((bf16[2,1024,128]{2,1,0:T(8,128)(2,1)S(1)}, bf16[2,1024,128]{2,1,0:T(8,128)(2,1)}, u32[]{:S(2)}, u32[]{:S(2)}) %collective-permute-start.2) | collective-permute-done | bytes 524320 | tf_op jit(solution)/shard_map/ppermute | solution.py:16
  51.7 10.9 %collective-permute-done.13 = bf16[2,1024,128]{2,1,0:T(8,128)(2,1)} collective-permute-done((bf16[2,1024,128]{2,1,0:T(8,128)(2,1)}, bf16[2,1024,128]{2,1,0:T(8,128)(2,1)}, u32[]{:S(2)}, u32[]{:S(2)}) %collective-permute-start.13) | collective-permute-done | bytes 524320 | tf_op jit(solution)/shard_map/ppermute | solution.py:39
  66.1 6.8 %first_part.1 = (bf16[2,2,128,1152]{3,2,1,0:T(8,128)(2,1)S(1)}, bf16[2,2,128,1152]{3,2,1,0:T(8,128)(2,1)S(1)}) custom-call(s32[13]{0:T(128)S(1)} %concatenate.15.refs_0_.place, bf16[8,128,2048]{2,1,0:T(8,128)(2,1)} %bitcast.65, bf16[2,4,128,1024]{3,2,1,0:T(8,128)(2,1)} %copy-done, f32[2,2048]{1,0:T(2,128)S(1)} %copy-done.7, bf16[8,128,2048]{2,1,0:T(8,128)(2,1)} %refs_4_.5, ...), custom_call_target="tpu_custom_call" | custom-call | flops 2147483648 | bytes 14958592 | tf_op jit(solution)/shard_map/first_part/pallas_call | solution.py:327
  80.7 8.9 %collective-permute-done.5.refs_7_.refs_17_.refs_14_ = bf16[2,1024,128]{2,1,0:T(8,128)(2,1)S(1)} collective-permute-done((bf16[2,1024,128]{2,1,0:T(8,128)(2,1)S(1)}, bf16[2,1024,128]{2,1,0:T(8,128)(2,1)S(1)}, u32[]{:S(2)}, u32[]{:S(2)}) %collective-permute-start.5) | collective-permute-done | bytes 524320 | tf_op jit(solution)/shard_map/ppermute | solution.py:16
  89.6 10.7 %collective-permute-done.4.refs_5_.refs_15_.refs_12_ = bf16[2,1024,128]{2,1,0:T(8,128)(2,1)S(1)} collective-permute-done((bf16[2,1024,128]{2,1,0:T(8,128)(2,1)S(1)}, bf16[2,1024,128]{2,1,0:T(8,128)(2,1)S(1)}, u32[]{:S(2)}, u32[]{:S(2)}) %collective-permute-start.4) | collective-permute-done | bytes 524320 | tf_op jit(solution)/shard_map/ppermute | solution.py:16
  106.3 4.5 %collective-permute-done.20.refs_8_ = bf16[128,640]{1,0:T(8,128)(2,1)S(1)} collective-permute-done((bf16[128,640]{1,0:T(8,128)(2,1)S(1)}, bf16[128,640]{1,0:T(8,128)(2,1)S(1)}, u32[]{:S(2)}, u32[]{:S(2)}) %collective-permute-start.20) | collective-permute-done | bytes 163872 | tf_op jit(solution)/shard_map/ppermute | solution.py:59
  116.3 4.1 %hidden_part.1 = (bf16[2,2,128,640]{3,2,1,0:T(8,128)(2,1)S(1)}, bf16[2,2,128,640]{3,2,1,0:T(8,128)(2,1)S(1)}) custom-call(s32[13]{0:T(128)S(1)} %concatenate.15.refs_0_.place, bf16[8,128,2048]{2,1,0:T(8,128)(2,1)} %bitcast.66, bf16[2,4,128,1024]{3,2,1,0:T(8,128)(2,1)S(1)} %copy-done.1, f32[2,2048]{1,0:T(2,128)S(1)} %copy-done.7, ...), custom_call_target="tpu_custom_call" | custom-call | flops 1073741824 | bytes 9715712 | tf_op jit(solution)/shard_map/hidden_part/pallas_call | solution.py:327
  124.8 9.5 %first_back.1 = (bf16[4,128,1024]{2,1,0:T(8,128)(2,1)}, bf16[4,128,1024]{2,1,0:T(8,128)(2,1)}, bf16[2,2,128,512]{3,2,1,0:T(8,128)(2,1)S(1)}, bf16[2,2,128,512]{3,2,1,0:T(8,128)(2,1)S(1)}) custom-call(s32[13]{0:T(128)S(1)} %concatenate.15.refs_0_.place, bf16[8,128,2048]{2,1,0:T(8,128)(2,1)} %bitcast.67, bf16[2,4,128,1024]{3,2,1,0:T(8,128)(2,1)} %copy-done, ...), custom_call_target="tpu_custom_call" | custom-call | flops 2147483648 | bytes 19152896 | tf_op jit(solution)/shard_map/first_back/pallas_call | solution.py:327
  138.7 3.6 %collective-permute-done.9.refs_1_ = bf16[128,640]{1,0:T(8,128)(2,1)S(1)} collective-permute-done((bf16[128,640]{1,0:T(8,128)(2,1)S(1)}, bf16[128,640]{1,0:T(8,128)(2,1)S(1)}, u32[]{:S(2)}, u32[]{:S(2)}) %collective-permute-start.9) | collective-permute-done | bytes 163872 | tf_op jit(solution)/shard_map/ppermute | solution.py:55
  142.3 3.7 %collective-permute-done.10.refs_2_ = bf16[128,640]{1,0:T(8,128)(2,1)S(1)} collective-permute-done((bf16[128,640]{1,0:T(8,128)(2,1)S(1)}, bf16[128,640]{1,0:T(8,128)(2,1)S(1)}, u32[]{:S(2)}, u32[]{:S(2)}) %collective-permute-start.10) | collective-permute-done | bytes 163872 | tf_op jit(solution)/shard_map/ppermute | solution.py:47
  155.6 8.6 %first_grads.1 = (f32[2,128,1024]{2,1,0:T(8,128)S(1)}, bf16[2,128,1024]{2,1,0:T(8,128)(2,1)S(1)}, bf16[2,128,1024]{2,1,0:T(8,128)(2,1)S(1)}, bf16[2,128,1024]{2,1,0:T(8,128)(2,1)S(1)}) custom-call(s32[13]{0:T(128)S(1)} %concatenate.15.refs_0_.place, bf16[8,128,2048]{2,1,0:T(8,128)(2,1)} %bitcast.68, bf16[2,4,128,1024]{3,2,1,0:T(8,128)(2,1)} %copy-done, ...), custom_call_target="tpu_custom_call" | custom-call | flops 2147483648 | bytes 15482880 | tf_op jit(solution)/shard_map/first_grads/pallas_call | solution.py:327
  164.2 6.0 %collective-permute-start.39 = (bf16[2,128,1024]{2,1,0:T(8,128)(2,1)S(1)}, bf16[2,128,1024]{2,1,0:T(8,128)(2,1)S(1)}, u32[]{:S(2)}, u32[]{:S(2)}) collective-permute-start(bf16[2,128,1024]{2,1,0:T(8,128)(2,1)S(1)} %get-tuple-element.86), channel_id=1, source_target_pairs={{3,2},{0,1},{7,6},{4,5},{11,10},{8,9},{15,14},{12,13},{19,18},{16,... | collective-permute-start | bytes 1572872 | tf_op jit(solution)/shard_map/ppermute | solution.py:43
  173.4 5.8 %collective-permute-done.28.refs_3_ = bf16[128,512]{1,0:T(8,128)(2,1)S(1)} collective-permute-done((bf16[128,512]{1,0:T(8,128)(2,1)S(1)}, bf16[128,512]{1,0:T(8,128)(2,1)S(1)}, u32[]{:S(2)}, u32[]{:S(2)}) %collective-permute-start.28) | collective-permute-done | bytes 131104 | tf_op jit(solution)/shard_map/ppermute | solution.py:47
  186.8 4.7 %collective-permute-start.48 = (bf16[1,128,1024]{2,1,0:T(8,128)(2,1)S(1)}, bf16[1,128,1024]{2,1,0:T(8,128)(2,1)S(1)}, u32[]{:S(2)}, u32[]{:S(2)}) collective-permute-start(bf16[1,128,1024]{2,1,0:T(8,128)(2,1)S(1)} %get-tuple-element.91), channel_id=1, source_target_pairs={{3,2},{0,1},{7,6},{4,5},{11,10},{8,9},{15,14},{12,13},{19,18},{16,... | collective-permute-start | bytes 786440 | tf_op jit(solution)/shard_map/ppermute | solution.py:43
  200.7 13.2 %collective-permute-start.49 = (bf16[1,128,1024]{2,1,0:T(8,128)(2,1)S(1)}, bf16[1,128,1024]{2,1,0:T(8,128)(2,1)S(1)}, u32[]{:S(2)}, u32[]{:S(2)}) collective-permute-start(bf16[1,128,1024]{2,1,0:T(8,128)(2,1)S(1)} %get-tuple-element.112), channel_id=1, source_target_pairs={{0,1},{1,2},{2,3},{3,0},{4,5},{5,6},{6,7},{7,4},{8,9},{9,10},{10,1... | collective-permute-start | bytes 786440 | tf_op jit(solution)/shard_map/ppermute | solution.py:16
  213.9 4.9 %in_grad.1 = (f32[1,128,1024]{2,1,0:T(8,128)S(1)}, bf16[1,128,1024]{2,1,0:T(8,128)(2,1)S(1)}, bf16[1,128,1024]{2,1,0:T(8,128)(2,1)S(1)}, bf16[1,128,1024]{2,1,0:T(8,128)(2,1)S(1)}) custom-call(s32[13]{0:T(128)S(1)} %concatenate.15.refs_0_.place, bf16[8,128,2048]{2,1,0:T(8,128)(2,1)} %bitcast.69, bf16[2,4,128,1024]{3,2,1,0:T(8,128)(2,1)S(1)} %copy-done.2, ...), custom_call_target="tpu_custom_call" | custom-call | flops 1073741824 | bytes 8929280 | tf_op jit(solution)/shard_map/in_grad/pallas_call | solution.py:327
  218.8 5.5 %collective-permute-start.35 = (bf16[1,128,1024]{2,1,0:T(8,128)(2,1)S(1)}, bf16[1,128,1024]{2,1,0:T(8,128)(2,1)S(1)}, u32[]{:S(2)}, u32[]{:S(2)}) collective-permute-start(bf16[1,128,1024]{2,1,0:T(8,128)(2,1)S(1)} %get-tuple-element.76), channel_id=1, source_target_pairs={{3,2},{0,1},{7,6},{4,5},{11,10},{8,9},{15,14},{12,13},{19,18},{16,... | collective-permute-start | bytes 786440 | tf_op jit(solution)/shard_map/ppermute | solution.py:43
  226.3 5.7 %last_back.1 = (bf16[4,128,1024]{2,1,0:T(8,128)(2,1)S(1)}, bf16[4,128,1024]{2,1,0:T(8,128)(2,1)S(1)}) custom-call(s32[13]{0:T(128)S(1)} %concatenate.15.refs_0_.place, bf16[8,128,2048]{2,1,0:T(8,128)(2,1)} %bitcast.70, bf16[2,4,128,1024]{3,2,1,0:T(8,128)(2,1)} %copy-done, f32[2,2048]{1,0:T(2,128)S(1)} %copy-done.7, ...), custom_call_target="tpu_custom_call" | custom-call | flops 1073741824 | bytes 13910016 | tf_op jit(solution)/shard_map/last_back/pallas_call | solution.py:327
  242.7 4.8 %collective-permute-done.37 = bf16[1,128,1024]{2,1,0:T(8,128)(2,1)S(1)} collective-permute-done((bf16[1,128,1024]{2,1,0:T(8,128)(2,1)S(1)}, bf16[1,128,1024]{2,1,0:T(8,128)(2,1)S(1)}, u32[]{:S(2)}, u32[]{:S(2)}) %collective-permute-start.37) | collective-permute-done | bytes 262176 | tf_op jit(solution)/shard_map/ppermute | solution.py:16
  247.5 5.0 %collective-permute-done.36 = bf16[1,128,1024]{2,1,0:T(8,128)(2,1)S(1)} collective-permute-done((bf16[1,128,1024]{2,1,0:T(8,128)(2,1)S(1)}, bf16[1,128,1024]{2,1,0:T(8,128)(2,1)S(1)}, u32[]{:S(2)}, u32[]{:S(2)}) %collective-permute-start.36) | collective-permute-done | bytes 262176 | tf_op jit(solution)/shard_map/ppermute | solution.py:16
  255.3 11.2 %collective-permute-done.51 = bf16[128,1024]{1,0:T(8,128)(2,1)S(1)} collective-permute-done((bf16[128,1024]{1,0:T(8,128)(2,1)S(1)}, bf16[128,1024]{1,0:T(8,128)(2,1)S(1)}, u32[]{:S(2)}, u32[]{:S(2)}) %collective-permute-start.51) | collective-permute-done | bytes 262176 | tf_op jit(solution)/shard_map/ppermute | solution.py:47
  (146 shorter events, 100.3 us)
Async XLA Ops:
  17.7 47.0 %collective-permute-start.1 = (bf16[2,4,128,1024]{3,2,1,0:T(8,128)(2,1)}, bf16[2,4,128,1024]{3,2,1,0:T(8,128)(2,1)S(1)}, u32[]{:S(2)}, u32[]{:S(2)}) collective-permute-start(bf16[2,4,128,1024]{3,2,1,0:T(8,128)(2,1)} %pad_maximum_fusion), channel_id=1, source_target_pairs={{0,16},{16,0},{1,17},{17,1},{2,18},{18,2},{3,19},{19,3},{4,20},{20... | collective-permute-start | bytes 6291464 | tf_op jit(solution)/shard_map/ppermute | solution.py:47
  20.6 16.0 %collective-permute-start.3 = (bf16[2,1024,128]{2,1,0:T(8,128)(2,1)S(1)}, bf16[2,1024,128]{2,1,0:T(8,128)(2,1)}, u32[]{:S(2)}, u32[]{:S(2)}) collective-permute-start(bf16[2,1024,128]{2,1,0:T(8,128)(2,1)S(1)} %get-tuple-element.107.refs_5_.refs_10_), channel_id=1, source_target_pairs={{0,3},{1,0},{2,1},{3,2},{4,7},{5,4},{6,5},{7,6},{8,11},{9,8},{10,9... | collective-permute-start | bytes 1572872 | tf_op jit(solution)/shard_map/ppermute | solution.py:16
  24.3 22.3 %collective-permute-start.2 = (bf16[2,1024,128]{2,1,0:T(8,128)(2,1)S(1)}, bf16[2,1024,128]{2,1,0:T(8,128)(2,1)}, u32[]{:S(2)}, u32[]{:S(2)}) collective-permute-start(bf16[2,1024,128]{2,1,0:T(8,128)(2,1)S(1)} %get-tuple-element.107.refs_5_.refs_10_), channel_id=1, source_target_pairs={{0,1},{1,2},{2,3},{3,0},{4,5},{5,6},{6,7},{7,4},{8,9},{9,10},{10,1... | collective-permute-start | bytes 1572872 | tf_op jit(solution)/shard_map/ppermute | solution.py:16
  73.0 16.6 %collective-permute-start.5 = (bf16[2,1024,128]{2,1,0:T(8,128)(2,1)S(1)}, bf16[2,1024,128]{2,1,0:T(8,128)(2,1)S(1)}, u32[]{:S(2)}, u32[]{:S(2)}) collective-permute-start(bf16[2,1024,128]{2,1,0:T(8,128)(2,1)S(1)} %get-tuple-element.50.refs_4_.refs_14_.refs_11_), channel_id=1, source_target_pairs={{0,1},{1,2},{2,3},{3,0},{4,5},{5,6},{6,7},{7,4},{8,9},{9,10},{10,1... | collective-permute-start | bytes 1572872 | tf_op jit(solution)/shard_map/ppermute | solution.py:16
  76.5 23.9 %collective-permute-start.4 = (bf16[2,1024,128]{2,1,0:T(8,128)(2,1)S(1)}, bf16[2,1024,128]{2,1,0:T(8,128)(2,1)S(1)}, u32[]{:S(2)}, u32[]{:S(2)}) collective-permute-start(bf16[2,1024,128]{2,1,0:T(8,128)(2,1)S(1)} %get-tuple-element.50.refs_4_.refs_14_.refs_11_), channel_id=1, source_target_pairs={{0,3},{1,0},{2,1},{3,2},{4,7},{5,4},{6,5},{7,6},{8,11},{9,8},{10,9... | collective-permute-start | bytes 1572872 | tf_op jit(solution)/shard_map/ppermute | solution.py:16
  77.1 25.3 %collective-permute-start.15 = (bf16[128,1152]{1,0:T(8,128)(2,1)S(1)}, bf16[128,1152]{1,0:T(8,128)(2,1)S(1)}, u32[]{:S(2)}, u32[]{:S(2)}) collective-permute-start(bf16[128,1152]{1,0:T(8,128)(2,1)S(1)} %get-tuple-element.61), channel_id=1, source_target_pairs={{0,8},{4,12},{8,0},{12,4},{1,9},{5,13},{9,1},{13,5},{2,10},{6,14},... | collective-permute-start | bytes 884744 | tf_op jit(solution)/shard_map/ppermute | solution.py:55
  78.6 23.8 %collective-permute-start.16 = (bf16[128,1152]{1,0:T(8,128)(2,1)S(1)}, bf16[128,1152]{1,0:T(8,128)(2,1)S(1)}, u32[]{:S(2)}, u32[]{:S(2)}) collective-permute-start(bf16[128,1152]{1,0:T(8,128)(2,1)S(1)} %get-tuple-element.62), channel_id=1, source_target_pairs={{0,16},{16,0},{1,17},{17,1},{2,18},{18,2},{3,19},{19,3},{4,20},{20... | collective-permute-start | bytes 884744 | tf_op jit(solution)/shard_map/ppermute | solution.py:47
  80.1 22.3 %collective-permute-start.17 = (bf16[128,1152]{1,0:T(8,128)(2,1)S(1)}, bf16[128,1152]{1,0:T(8,128)(2,1)S(1)}, u32[]{:S(2)}, u32[]{:S(2)}) collective-permute-start(bf16[128,1152]{1,0:T(8,128)(2,1)S(1)} %get-tuple-element.63), channel_id=1, source_target_pairs={{0,24},{4,28},{8,16},{12,20},{16,8},{20,12},{24,0},{28,4},{1,25},{... | collective-permute-start | bytes 884744 | tf_op jit(solution)/shard_map/ppermute | solution.py:59
  100.4 15.8 %collective-permute-start.7 = (bf16[2,1024,128]{2,1,0:T(8,128)(2,1)S(1)}, bf16[2,1024,128]{2,1,0:T(8,128)(2,1)S(1)}, u32[]{:S(2)}, u32[]{:S(2)}) collective-permute-start(bf16[2,1024,128]{2,1,0:T(8,128)(2,1)S(1)} %get-tuple-element.104), channel_id=1, source_target_pairs={{2,3},{1,0},{6,7},{5,4},{10,11},{9,8},{14,15},{13,12},{18,19},{17,... | collective-permute-start | bytes 1572872 | tf_op jit(solution)/shard_map/ppermute | solution.py:39
  134.3 20.2 %collective-permute-start.26 = (bf16[2,2,128,512]{3,2,1,0:T(8,128)(2,1)S(1)}, bf16[2,2,128,512]{3,2,1,0:T(8,128)(2,1)S(1)}, u32[]{:S(2)}, u32[]{:S(2)}) collective-permute-start(bf16[2,2,128,512]{3,2,1,0:T(8,128)(2,1)S(1)} %get-tuple-element.69), channel_id=1, source_target_pairs={{0,4},{4,0},{8,12},{12,8},{1,5},{5,1},{9,13},{13,9},{2,6},{6,2},{1... | collective-permute-start | bytes 1572872 | tf_op jit(solution)/shard_map/ppermute | solution.py:51
  134.4 21.2 %collective-permute-start.25 = (bf16[2,2,128,512]{3,2,1,0:T(8,128)(2,1)S(1)}, bf16[2,2,128,512]{3,2,1,0:T(8,128)(2,1)S(1)}, u32[]{:S(2)}, u32[]{:S(2)}) collective-permute-start(bf16[2,2,128,512]{3,2,1,0:T(8,128)(2,1)S(1)} %bitcast.73), channel_id=1, source_target_pairs={{0,4},{4,0},{8,12},{12,8},{1,5},{5,1},{9,13},{13,9},{2,6},{6,2},{1... | collective-permute-start | bytes 1572872 | tf_op jit(solution)/shard_map/ppermute | solution.py:51
  154.4 27.5 %collective-permute-start.46 = (bf16[2,2,128,512]{3,2,1,0:T(8,128)(2,1)S(1)}, bf16[2,2,128,512]{3,2,1,0:T(8,128)(2,1)S(1)}, u32[]{:S(2)}, u32[]{:S(2)}) collective-permute-start(bf16[2,2,128,512]{3,2,1,0:T(8,128)(2,1)S(1)} %bitcast.74), channel_id=1, source_target_pairs={{0,4},{4,0},{8,12},{12,8},{1,5},{5,1},{9,13},{13,9},{2,6},{6,2},{1... | collective-permute-start | bytes 1572872 | tf_op jit(solution)/shard_map/ppermute | solution.py:51
  154.7 17.5 %collective-permute-start.27 = (bf16[128,512]{1,0:T(8,128)(2,1)S(1)}, bf16[128,512]{1,0:T(8,128)(2,1)S(1)}, u32[]{:S(2)}, u32[]{:S(2)}) collective-permute-start(bf16[128,512]{1,0:T(8,128)(2,1)S(1)} %get-tuple-element.71), channel_id=1, source_target_pairs={{0,8},{4,12},{8,0},{12,4},{1,9},{5,13},{9,1},{13,5},{2,10},{6,14},... | collective-permute-start | bytes 393224 | tf_op jit(solution)/shard_map/ppermute | solution.py:55
  164.2 28.2 %collective-permute-start.39 = (bf16[2,128,1024]{2,1,0:T(8,128)(2,1)S(1)}, bf16[2,128,1024]{2,1,0:T(8,128)(2,1)S(1)}, u32[]{:S(2)}, u32[]{:S(2)}) collective-permute-start(bf16[2,128,1024]{2,1,0:T(8,128)(2,1)S(1)} %get-tuple-element.86), channel_id=1, source_target_pairs={{3,2},{0,1},{7,6},{4,5},{11,10},{8,9},{15,14},{12,13},{19,18},{16,... | collective-permute-start | bytes 1572872 | tf_op jit(solution)/shard_map/ppermute | solution.py:43
  170.2 22.2 %collective-permute-start.38 = (bf16[2,128,1024]{2,1,0:T(8,128)(2,1)S(1)}, bf16[2,128,1024]{2,1,0:T(8,128)(2,1)S(1)}, u32[]{:S(2)}, u32[]{:S(2)}) collective-permute-start(bf16[2,128,1024]{2,1,0:T(8,128)(2,1)S(1)} %get-tuple-element.86), channel_id=1, source_target_pairs={{1,2},{2,1},{5,6},{6,5},{9,10},{10,9},{13,14},{14,13},{17,18},{18,... | collective-permute-start | bytes 1572872 | tf_op jit(solution)/shard_map/ppermute | solution.py:35
  192.3 21.6 %collective-permute-start.33 = (bf16[2,2,128,640]{3,2,1,0:T(8,128)(2,1)S(1)}, bf16[2,2,128,640]{3,2,1,0:T(8,128)(2,1)S(1)}, u32[]{:S(2)}, u32[]{:S(2)}) collective-permute-start(bf16[2,2,128,640]{3,2,1,0:T(8,128)(2,1)S(1)} %bitcast.71), channel_id=1, source_target_pairs={{0,4},{4,0},{8,12},{12,8},{1,5},{5,1},{9,13},{13,9},{2,6},{6,2},{1... | collective-permute-start | bytes 1966088 | tf_op jit(solution)/shard_map/ppermute | solution.py:51
  192.9 25.9 %collective-permute-start.40 = (bf16[2,128,1024]{2,1,0:T(8,128)(2,1)S(1)}, bf16[2,128,1024]{2,1,0:T(8,128)(2,1)S(1)}, u32[]{:S(2)}, u32[]{:S(2)}) collective-permute-start(bf16[2,128,1024]{2,1,0:T(8,128)(2,1)S(1)} %get-tuple-element.108), channel_id=1, source_target_pairs={{0,1},{1,2},{2,3},{3,0},{4,5},{5,6},{6,7},{7,4},{8,9},{9,10},{10,1... | collective-permute-start | bytes 1572872 | tf_op jit(solution)/shard_map/ppermute | solution.py:16
  194.0 30.3 %collective-permute-start.41 = (bf16[2,128,1024]{2,1,0:T(8,128)(2,1)S(1)}, bf16[2,128,1024]{2,1,0:T(8,128)(2,1)}, u32[]{:S(2)}, u32[]{:S(2)}) collective-permute-start(bf16[2,128,1024]{2,1,0:T(8,128)(2,1)S(1)} %get-tuple-element.109), channel_id=1, source_target_pairs={{0,3},{1,0},{2,1},{3,2},{4,7},{5,4},{6,5},{7,6},{8,11},{9,8},{10,9... | collective-permute-start | bytes 1572872 | tf_op jit(solution)/shard_map/ppermute | solution.py:16
  196.8 40.8 %collective-permute-start.52 = (bf16[4,128,1024]{2,1,0:T(8,128)(2,1)S(1)}, bf16[4,128,1024]{2,1,0:T(8,128)(2,1)S(1)}, u32[]{:S(2)}, u32[]{:S(2)}) collective-permute-start(bf16[4,128,1024]{2,1,0:T(8,128)(2,1)S(1)} %copy-done.6), channel_id=1, source_target_pairs={{0,16},{16,0},{1,17},{17,1},{2,18},{18,2},{3,19},{19,3},{4,20},{20... | collective-permute-start | bytes 3145736 | tf_op jit(solution)/shard_map/ppermute | solution.py:47
  200.7 51.9 %collective-permute-start.49 = (bf16[1,128,1024]{2,1,0:T(8,128)(2,1)S(1)}, bf16[1,128,1024]{2,1,0:T(8,128)(2,1)S(1)}, u32[]{:S(2)}, u32[]{:S(2)}) collective-permute-start(bf16[1,128,1024]{2,1,0:T(8,128)(2,1)S(1)} %get-tuple-element.112), channel_id=1, source_target_pairs={{0,1},{1,2},{2,3},{3,0},{4,5},{5,6},{6,7},{7,4},{8,9},{9,10},{10,1... | collective-permute-start | bytes 786440 | tf_op jit(solution)/shard_map/ppermute | solution.py:16
  213.9 38.6 %collective-permute-start.50 = (bf16[1,128,1024]{2,1,0:T(8,128)(2,1)S(1)}, bf16[1,128,1024]{2,1,0:T(8,128)(2,1)S(1)}, u32[]{:S(2)}, u32[]{:S(2)}) collective-permute-start(bf16[1,128,1024]{2,1,0:T(8,128)(2,1)S(1)} %get-tuple-element.113), channel_id=1, source_target_pairs={{0,3},{1,0},{2,1},{3,2},{4,7},{5,4},{6,5},{7,6},{8,11},{9,8},{10,9... | collective-permute-start | bytes 786440 | tf_op jit(solution)/shard_map/ppermute | solution.py:16
  218.8 16.0 %collective-permute-start.35 = (bf16[1,128,1024]{2,1,0:T(8,128)(2,1)S(1)}, bf16[1,128,1024]{2,1,0:T(8,128)(2,1)S(1)}, u32[]{:S(2)}, u32[]{:S(2)}) collective-permute-start(bf16[1,128,1024]{2,1,0:T(8,128)(2,1)S(1)} %get-tuple-element.76), channel_id=1, source_target_pairs={{3,2},{0,1},{7,6},{4,5},{11,10},{8,9},{15,14},{12,13},{19,18},{16,... | collective-permute-start | bytes 786440 | tf_op jit(solution)/shard_map/ppermute | solution.py:43
  234.8 37.2 %collective-permute-start.53 = (bf16[4,128,1024]{2,1,0:T(8,128)(2,1)S(1)}, bf16[4,128,1024]{2,1,0:T(8,128)(2,1)}, u32[]{:S(2)}, u32[]{:S(2)}) collective-permute-start(bf16[4,128,1024]{2,1,0:T(8,128)(2,1)S(1)} %get-tuple-element.81), channel_id=1, source_target_pairs={{0,16},{16,0},{1,17},{17,1},{2,18},{18,2},{3,19},{19,3},{4,20},{20... | collective-permute-start | bytes 3145736 | tf_op jit(solution)/shard_map/ppermute | solution.py:47
  254.3 16.2 %collective-permute-start.42 = (bf16[128,1024]{1,0:T(8,128)(2,1)S(1)}, bf16[128,1024]{1,0:T(8,128)(2,1)S(1)}, u32[]{:S(2)}, u32[]{:S(2)}) collective-permute-start(bf16[128,1024]{1,0:T(8,128)(2,1)S(1)} %get-tuple-element.101), channel_id=1, source_target_pairs={{0,16},{16,0},{1,17},{17,1},{2,18},{18,2},{3,19},{19,3},{4,20},{20... | collective-permute-start | bytes 786440 | tf_op jit(solution)/shard_map/ppermute | solution.py:47
  (39 other events, 545.7 us)

commit v4 on v3

--- a/solution.py
+++ b/solution.py
@@ -31,18 +31,6 @@
     return kept
 
 
-def trade_inner(block):
-    return lax.ppermute(block, "dp", [(1, 2), (2, 1)])
-
-
-def trade_outward(block):
-    return lax.ppermute(block, "dp", [(2, 3), (1, 0)])
-
-
-def trade_inward(block):
-    return lax.ppermute(block, "dp", [(3, 2), (0, 1)])
-
-
 def swap_section(block):
     return lax.ppermute(block, "section", [(0, 1), (1, 0)])
 
@@ -77,19 +65,21 @@
     return 2 * (place[CHIP] ^ a) + (place[CORE] ^ b)
 
 
-def join_units(step, parts, whole):
+def join_units(step, which, parts, whole):
+    held, above, below, *far = parts
+
     @pl.when(step == 0)
     def _():
-        for k, part in enumerate(parts):
-            whole[:, k * part.shape[1] : (k + 1) * part.shape[1]] = part[...]
+        width = held.shape[-1]
+        for k, part in enumerate((held.at[which], above.at[which], far[which], below.at[which])):
+            whole[:, k * width : (k + 1) * width] = part[...]
 
 
 def join_slots(step, parts, whole):
     @pl.when(step == 0)
     def _():
-        for k in range(4):
-            whole[0, k // 2, k % 2] = parts[k][...]
-        whole[1] = parts[4][...]
+        whole[0] = parts[0][...]
+        whole[1] = parts[1][...]
 
 
 def load_set(place, refs, rows):
@@ -123,9 +113,9 @@
         kept[which] = value
 
 
-def hidden_kernel(group, place, own, received, gain, w0, w1, w2, w3, sent, kept, weights, rows):
-    step, b, which = step_place()
-    join_units(step, (w0.at[0], w1.at[0], w2.at[0], w3.at[0]), weights)
+def hidden_kernel(group, place, own, received, gain, w0, w1, w2, w3, w4, sent, kept, weights, rows):
+    step, b, which = step_place()
+    join_units(step, 0, (w0, w1, w2, w3, w4), weights)
     load_set(place, (own, received), rows)
     wide = rows[...].astype(F32)
     normed = (wide * gain[group : group + 1, :]).astype(BF16)
@@ -136,20 +126,22 @@
 
 
 def first_part_kernel(
-    group, place, own, received, gain, top, w0, w1, w2, w3, sent, kept, weights, outward, rows
+    group, place, own, received, gain, top, w0, w1, w2, w3, w4, sent0, kept0, sent1, kept1,
+    weights, outward, rows,
 ):
     step, b, which = step_place()
-    join_units(step, (w0.at[0], w1.at[0], w2.at[0], w3.at[0]), weights)
-    join_units(step, (w0.at[1], w1.at[1], w2.at[1], w3.at[1]), outward)
+    join_units(step, 0, (w0, w1, w2, w3, w4), weights)
+    join_units(step, 1, (w0, w1, w2, w3, w4), outward)
     load_set(place, (own, received), rows)
     wide = rows[...].astype(F32)
     normed = (wide * gain[group : group + 1, :]).astype(BF16)
     part = jnp.dot(normed, weights[...], preferred_element_type=F32)
     squares = jnp.sum(wide * wide, axis=1, keepdims=True)
+    packed = jnp.concatenate((part, jnp.broadcast_to(squares, (part.shape[0], PAD))), axis=1)
+    put_partial(packed, sent0, kept0, step, which)
     load_top(0, place, top, rows)
-    top_part = jnp.dot(rows[...], outward[...], preferred_element_type=F32)
-    padded = jnp.broadcast_to(squares, (part.shape[0], PAD))
-    put_partial(jnp.concatenate((part, padded, top_part), axis=1), sent, kept, step, which)
+    part = jnp.dot(rows[...], outward[...], preferred_element_type=F32)
+    put_partial(part, sent1, kept1, step, which)
 
 
 def back_step(group, place, own, received, gain, spread, weights, rows, incoming):
@@ -181,13 +173,13 @@
 
 
 def first_back_kernel(
-    group, place, own, received, gain, top, p0, p1, p2, p3, p4, w0, w1, w2, w3, v0, v1, v2, v3,
+    group, place, own, received, gain, top, p0, p1, w0, w1, w2, w3, w4, v0, v1, v2, v3, v4,
     result0, result1, sent, kept, weights, outward, spread, rows, grads,
 ):
     step, b, which = step_place()
-    join_units(step, (w0.at[0], w1.at[0], w2.at[0], w3.at[0]), weights)
-    join_units(step, (v0.at[1], v1.at[1], v2.at[1], v3.at[1]), outward)
-    join_slots(step, (p0, p1, p2, p3, p4), spread)
+    join_units(step, 0, (w0, w1, w2, w3, w4), weights)
+    join_units(step, 1, (v0, v1, v2, v3, v4), outward)
+    join_slots(step, (p0, p1), spread)
     load_top(0, place, top, grads)
     result = back_step(group, place, own, received, gain, spread, weights, rows, grads[...])
     put_result(place, result, (result0, result1))
@@ -196,12 +188,12 @@
 
 
 def last_back_kernel(
-    group, place, own, received, gain, in0, in1, p0, p1, p2, p3, p4, w0, w1, w2, w3,
+    group, place, own, received, gain, in0, in1, p0, p1, w0, w1, w2, w3, w4,
     result0, result1, weights, spread, rows, grads,
 ):
     step, b, which = step_place()
-    join_units(step, (w0.at[0], w1.at[0], w2.at[0], w3.at[0]), weights)
-    join_slots(step, (p0, p1, p2, p3, p4), spread)
+    join_units(step, 0, (w0, w1, w2, w3, w4), weights)
+    join_slots(step, (p0, p1), spread)
     load_set(place, (in0, in1), grads)
     result = back_step(group, place, own, received, gain, spread, weights, rows, grads[...])
     put_result(place, result, (result0, result1))
@@ -219,20 +211,20 @@
         total[...] += part
 
 
-def put_grad(step, total, kept, parts, at=0):
+def put_grad(step, total, kept, parts):
     @pl.when(step == STEPS - 1)
     def _():
-        height = kept.shape[1]
-        kept[at] = total[:height]
+        height = kept.shape[0]
+        kept[...] = total[:height]
         for k, part in enumerate(parts):
-            part[at] = total[(k + 1) * height : (k + 2) * height].astype(BF16)
+            part[...] = total[(k + 1) * height : (k + 2) * height].astype(BF16)
 
 
 def in_grad_kernel(
-    group, place, own, received, gain, p0, p1, p2, p3, p4, kept, c1, c2, c3, total, spread, rows
+    group, place, own, received, gain, p0, p1, kept, c1, c2, c3, total, spread, rows
 ):
     step, b, which = step_place()
-    join_slots(step, (p0, p1, p2, p3, p4), spread)
+    join_slots(step, (p0, p1), spread)
     load_set(place, (own, received), rows)
     normed = (rows[...].astype(F32) * gain[group : group + 1, :]).astype(BF16)
     packed = spread[b, which].reshape(rows.shape[0], spread.shape[-1])
@@ -240,52 +232,64 @@
     put_grad(step, total, kept, (c1, c2, c3))
 
 
-def first_grad_kernel(
-    group, place, own, received, gain, top, p0, p1, p2, p3, p4, a0, a1, a2, a3, a4,
-    kept, c1, c2, c3, total, out_total, spread, active, rows,
-):
-    step, b, which = step_place()
-    join_slots(step, (p0, p1, p2, p3, p4), spread)
-    join_slots(step, (a0, a1, a2, a3, a4), active)
-    load_set(place, (own, received), rows)
-    normed = (rows[...].astype(F32) * gain[group : group + 1, :]).astype(BF16)
+def top_grad_kernel(place, top, p0, p1, kept, c1, c2, c3, total, spread, rows):
+    step, b, which = step_place()
+    join_slots(step, (p0, p1), spread)
+    load_top(0, place, top, rows)
     packed = spread[b, which].reshape(rows.shape[0], spread.shape[-1])
-    add_grad(step, total, packed[:, : total.shape[0]], normed)
-    load_top(0, place, top, rows)
-    add_grad(step, out_total, active[b, which].reshape(rows.shape[0], active.shape[-1]), rows[...])
-    put_grad(step, total, kept, (c1, c2, c3), 0)
-    put_grad(step, out_total, kept, (c1, c2, c3), 1)
-
-
-def out_grad_kernel(place, in0, in1, p0, p1, p2, p3, p4, kept, c1, c2, c3, total, spread, rows):
-    step, b, which = step_place()
-    join_slots(step, (p0, p1, p2, p3, p4), spread)
+    add_grad(step, total, packed, rows[...])
+    put_grad(step, total, kept, (c1, c2, c3))
+
+
+def out_grad_kernel(place, in0, in1, p0, p1, kept, c1, c2, c3, total, spread, rows):
+    step, b, which = step_place()
+    join_slots(step, (p0, p1), spread)
     load_set(place, (in0, in1), rows)
     packed = spread[b, which].reshape(rows.shape[0], spread.shape[-1])
     add_grad(step, total, packed, rows[...])
     put_grad(step, total, kept, (c1, c2, c3))
 
 
-def core_sum_kernel(kept, moved, own, chip, section, both):
-    def at(k):
-        return kept[k // 2, k % 2].astype(F32) + moved[k // 2, k % 2].astype(F32)
-
-    own[...] = at(0)
-    chip[...] = at(1).astype(BF16)
-    section[...] = at(2).astype(BF16)
-    both[...] = at(3).astype(BF16)
-
-
-def whole_sum(own, chip, section, both):
-    return own[...] + chip[...].astype(F32) + section[...].astype(F32) + both[...].astype(F32)
-
-
-def active_kernel(features, own, chip, section, both, hidden, activated):
-    total = whole_sum(own, chip, section, both)
-    hidden[...] = total
-    units = activated.shape[1]
-    terms = row_terms(total[:, :units], total[:, units : units + 1], features)
-    activated[...] = terms[3]
+def core_sum_kernel(count, *refs):
+    kept, moved, riders = refs[:count], refs[count : 2 * count], refs[2 * count : -4]
+    own, chip, section, both = refs[-4:]
+    start = 0
+    for left, right in zip(kept, moved):
+        width = left.shape[-1]
+        for k, out in enumerate((own, chip, section, both)):
+            value = left[k // 2, k % 2].astype(F32) + right[k // 2, k % 2].astype(F32)
+            out[:, start : start + width] = value.astype(out.dtype)
+        start += width
+    for rider in riders:
+        for out in (chip, section, both):
+            out[:, start:] = rider[...]
+
+
+def hop_sum_kernel(next_part, last_part, hop0, hop1, forth, back):
+    cut = hop0.shape[0]
+
+    def added(a, b):
+        return (a.astype(F32) + b.astype(F32)).astype(BF16)
+
+    forth[:cut] = added(next_part[:cut], hop0[...])
+    forth[cut:] = next_part[cut:]
+    back[:cut] = last_part[:cut]
+    back[cut:] = added(last_part[cut:], hop1[...])
+
+
+def whole_sum(own, parts):
+    width = own.shape[1]
+    total = own[...]
+    for part in parts:
+        total = total + part[:, :width].astype(F32)
+    return total
+
+
+def put_riders(four, rider, parts):
+    width = rider.shape[1]
+    four[0, 0] = rider[...]
+    for k, part in enumerate(parts):
+        four[(k + 1) // 2, (k + 1) % 2] = part[:, part.shape[1] - width :]
 
 
 def put_units(features, hidden, unit_grads, packed):
@@ -302,12 +306,24 @@
 
 def first_unit_kernel(features, own, chip, section, both, packed, activated):
     units = activated.shape[1]
-    total = whole_sum(own, chip, section, both)
+    total = whole_sum(own, (chip, section, both))
     activated[...] = put_units(features, total, total[:, units + PAD :], packed)
 
 
-def unit_kernel(features, hidden, own, chip, section, both, packed):
-    put_units(features, hidden, whole_sum(own, chip, section, both), packed)
+def active_kernel(features, own, chip, section, both, rider, hidden, activated, four):
+    parts = (chip, section, both)
+    total = whole_sum(own, parts)
+    hidden[...] = total
+    units = activated.shape[1]
+    terms = row_terms(total[:, :units], total[:, units : units + 1], features)
+    activated[...] = terms[3]
+    put_riders(four, rider, parts)
+
+
+def unit_kernel(features, hidden, own, chip, section, both, rider, packed, four):
+    parts = (chip, section, both)
+    put_units(features, hidden, whole_sum(own, parts), packed)
+    put_riders(four, rider, parts)
 
 
 def call(kernel, name, outs, args, scratch=(), specs=None, place=None, flops=0):
@@ -344,22 +360,30 @@
     return jax.ShapeDtypeStruct(shape, dtype)
 
 
-def pair_sum(sent, kept):
-    moved = swap_core(sent)
-    small = sent.shape[2:]
-    own, chip, section, both = call(
-        core_sum_kernel,
+def swap_chips(chip, section, both):
+    return swap_chip(chip), swap_section(section), swap_both(both)
+
+
+def core_sum(sent, kept, *riders):
+    tokens = sent[0].shape[2]
+    width = sum(part.shape[3] for part in sent)
+    wide = width + sum(rider.shape[1] for rider in riders)
+
+    def bound(*refs):
+        core_sum_kernel(len(sent), *refs)
+
+    return call(
+        bound,
         "core_sum",
-        [shape_of(small, F32)] + [shape_of(small)] * 3,
-        (kept, moved),
-    )
-    return own, swap_chip(chip), swap_section(section), swap_both(both)
+        [shape_of((tokens, width), F32)] + [shape_of((tokens, wide))] * 3,
+        tuple(kept) + tuple(swap_core(part) for part in sent) + riders,
+    )
 
 
 def pair_spread(block):
-    parts = (block, swap_chip(block), swap_section(block), swap_both(block))
+    parts = (block,) + swap_chips(block, block, block)
     four = jnp.stack(parts).reshape((2, 2) + block.shape)
-    return parts + (swap_core(four),)
+    return four, swap_core(four)
 
 
 def two_sections(saved_inputs, cotangent, weight_in, weight_out, gain, plan):
@@ -386,26 +410,18 @@
 
     received = swap_section(after(jnp.stack((sent_inputs(0), sent_inputs(1))), moved))
 
-    position = lax.axis_index("dp")
-
     def near(block):
         return rotate(block, 1), rotate(block, -1)
 
     def far(below, above):
-        inner = trade_inner(jnp.where(position == 1, below, above))
-        outward = trade_outward(jnp.where(position == 2, below, above))
-        return inner, outward
-
-    def joined(inner, outward):
-        return jnp.where((position == 1) | (position == 2), inner, outward)
+        return rotate(below[0], 1), rotate(above[1], -1)
 
     held0 = jnp.where(own == 1, mine, moved)
     held1 = jnp.where(own == 0, mine, moved)
     below, above = near(held0)
-    weights0 = (held0, above, joined(*far(below, above)), below)
+    weights0 = (held0, above, below) + far(below, above)
     below, above = near(after(held1, below, above))
-    far1 = far(below, above)
-    weights1 = (held1, above, joined(*far1), below)
+    weights1 = (held1, above, below) + far(below, above)
     units = 4 * mine.shape[-1]
     rows2 = 2 * tokens
     gain_spec = pl.BlockSpec((2, part), lambda i, s: (0, s[SECTION]))
@@ -418,13 +434,10 @@
     spread_scratch = ((2, 2, 2, tokens, units + PAD), BF16)
     act_scratch = ((2, 2, 2, tokens, units), BF16)
     grad_scratch = ((units, part), F32)
-    grad_shapes = [shape_of((1, units // 4, part), F32)] + [shape_of((1, units // 4, part))] * 3
+    grad_shapes = [shape_of((units // 4, part), F32)] + [shape_of((units // 4, part))] * 3
+    four_shape = shape_of((2, 2, tokens, units))
     one_dot = 2 * slots * tokens * part * units
 
-    both_grad_shapes = [shape_of((2, units // 4, part), F32)] + [
-        shape_of((2, units // 4, part))
-    ] * 3
-    first_shapes = [shape_of((2, 2, tokens, 2 * units + PAD))] * 2
 
     def received_spec(phase):
         return pl.BlockSpec((None, half, tokens, part), lambda i, s: (phase, 0, 0, 0))
@@ -440,109 +453,124 @@
 
         return bound
 
-    def scatter(parts):
-        kept, next_part, far_part, last_part = parts
-        inner, inward = trade_inner(far_part), trade_inward(far_part)
-        onward = jnp.where(position == 2, inner, inward)
-        backward = jnp.where(position == 1, inner, inward)
-        middle = (position == 1) | (position == 2)
-        zero = jnp.zeros((), F32)
-        forth = next_part.astype(F32) + jnp.where(middle, onward.astype(F32), zero)
-        back = last_part.astype(F32) + jnp.where(middle, backward.astype(F32), zero)
-        return kept, rotate(forth.astype(BF16), 1), rotate(back.astype(BF16), -1)
+    def first_hop(parts):
+        cut = parts[2].shape[0] // 2
+        return rotate(parts[2][:cut], 1), rotate(parts[2][cut:], -1)
+
+    def second_hop(parts, hop, *earlier):
+        kept, next_part, _, last_part = parts
+        forth, back = call(
+            hop_sum_kernel,
+            "hop_sum",
+            [shape_of(next_part.shape)] * 2,
+            (after(next_part, *earlier), last_part) + hop,
+        )
+        return kept, rotate(forth, 1), rotate(back, -1)
 
     def total(parts):
         return parts[0] + parts[1].astype(F32) + parts[2].astype(F32)
 
-    sent, kept = call(
+    sent, kept, sent1, kept1 = call(
         bind(first_part_kernel, 1),
         "first_part",
-        first_shapes,
+        hidden_shapes + partial_shapes,
         (stored, received, gain, cotangent) + weights0,
         [weight_scratch, weight_scratch, rows_scratch],
         {0: own_spec(0), 1: received_spec(0), 2: gain_spec, 3: top_spec},
         place,
         2 * one_dot,
     )
+    own_sum, *parts = core_sum((sent, sent1), (kept, kept1))
     scaled0, act0 = call(
         bind(first_unit_kernel, features),
         "first_units",
         [shape_of((tokens, units + PAD)), shape_of((tokens, units))],
-        pair_sum(sent, kept),
+        (own_sum,) + swap_chips(*parts),
     )
     scaled0 = pair_spread(scaled0)
-    act0 = pair_spread(act0)
+
+    sent, kept = call(
+        bind(hidden_kernel, 0),
+        "hidden_part",
+        hidden_shapes,
+        (stored, received, gain) + weights1,
+        [weight_scratch, rows_scratch],
+        {0: own_spec(1), 1: received_spec(1), 2: gain_spec},
+        place,
+        one_dot,
+    )
+    own_sum, *parts = core_sum((sent,), (kept,), act0)
+    in_grads0 = call(
+        bind(in_grad_kernel, 1),
+        "in_grad",
+        grad_shapes,
+        (stored, received, after(gain, own_sum)) + scaled0,
+        [grad_scratch, spread_scratch, rows_scratch],
+        {0: own_spec(0), 1: received_spec(0), 2: gain_spec},
+        place,
+        one_dot,
+    )
+    in_hop0 = first_hop(in_grads0)
     result0, result1, sent, kept = call(
         bind(first_back_kernel, 1),
         "first_back",
         [set_shape, set_shape] + partial_shapes,
-        (stored, received, gain, cotangent) + scaled0 + weights0 + weights1,
+        (stored, received, after(gain, in_grads0[0]), cotangent) + scaled0 + weights0 + weights1,
         [weight_scratch, weight_scratch, spread_scratch, rows_scratch, rows_scratch],
         {0: own_spec(0), 1: received_spec(0), 2: gain_spec, 3: top_spec},
         place,
         2 * one_dot,
     )
-    hidden1, act1 = call(
+    hidden1, act1, act0 = call(
         bind(active_kernel, features),
         "activated",
-        [shape_of((tokens, units + PAD), F32), shape_of((tokens, units))],
-        pair_sum(
-            *call(
-                bind(hidden_kernel, 0),
-                "hidden_part",
-                hidden_shapes,
-                (stored, received, gain) + weights1,
-                [weight_scratch, rows_scratch],
-                {0: own_spec(1), 1: received_spec(1), 2: gain_spec},
-                place,
-                one_dot,
-            )
-        ),
-    )
-    act1 = pair_spread(act1)
-    grads0 = call(
-        bind(first_grad_kernel, 1),
-        "first_grads",
-        both_grad_shapes,
-        (stored, received, gain, cotangent) + scaled0 + act0,
-        [grad_scratch, grad_scratch, spread_scratch, act_scratch, rows_scratch],
-        {0: own_spec(0), 1: received_spec(0), 2: gain_spec, 3: top_spec},
+        [shape_of((tokens, units + PAD), F32), shape_of((tokens, units)), four_shape],
+        (after(own_sum, kept),) + swap_chips(*parts) + (act0,),
+    )
+    own_sum, *parts = core_sum((sent,), (kept,), act1)
+    in_totals0 = second_hop(in_grads0, in_hop0, own_sum)
+    out_grads0 = call(
+        top_grad_kernel,
+        "top_grad",
+        grad_shapes,
+        (cotangent, after(act0, own_sum), swap_core(act0)),
+        [grad_scratch, act_scratch, rows_scratch],
+        {0: top_spec},
         place,
-        2 * one_dot,
-    )
-    sums = pair_sum(sent, kept)
-    scaled1 = call(
+        one_dot,
+    )
+    out_hop0 = first_hop(out_grads0)
+    scaled1, act1 = call(
         bind(unit_kernel, features),
         "unit_grads",
-        [shape_of((tokens, units + PAD))],
-        (after(hidden1, grads0[0]),) + sums,
-    )[0]
+        [shape_of((tokens, units + PAD)), four_shape],
+        (after(hidden1, out_grads0[0]), own_sum) + swap_chips(*parts) + (act1,),
+    )
+    out_totals0 = second_hop(out_grads0, out_hop0, scaled1)
     scaled1 = pair_spread(scaled1)
-    totals0 = scatter(grads0)
-    out_totals1 = scatter(
-        call(
-            out_grad_kernel,
-            "out_grad",
-            grad_shapes,
-            (result1, result0) + act1,
-            [grad_scratch, act_scratch, rows_scratch],
-            None,
-            place,
-            one_dot,
-        )
-    )
-    returned0 = swap_section(after(result1, scaled1[1]))
+    out_grads1 = call(
+        out_grad_kernel,
+        "out_grad",
+        grad_shapes,
+        (result1, result0, act1, swap_core(act1)),
+        [grad_scratch, act_scratch, rows_scratch],
+        None,
+        place,
+        one_dot,
+    )
+    out_hop1 = first_hop(out_grads1)
+    returned0 = swap_section(after(result1, scaled1[0]))
     in_grads1 = call(
         bind(in_grad_kernel, 0),
         "in_grad",
         grad_shapes,
-        (stored, received, gain) + scaled1,
+        (stored, received, after(gain, out_grads1[0])) + scaled1,
         [grad_scratch, spread_scratch, rows_scratch],
         {0: own_spec(1), 1: received_spec(1), 2: gain_spec},
         place,
         one_dot,
     )
-    in_totals1 = scatter(in_grads1)
+    in_hop1 = first_hop(in_grads1)
     result2, result3 = call(
         bind(last_back_kernel, 0),
         "last_back",
@@ -554,10 +582,10 @@
         one_dot,
     )
     returned1 = swap_section(result3)
-    total0 = total(totals0)
-    out_total1 = total(out_totals1)[0]
-    in_total1 = total(after(in_totals1, result3))[0]
-    in_total0, out_total0 = total0[0], total0[1]
+    in_totals1 = second_hop(in_grads1, in_hop1, result3)
+    out_totals1 = second_hop(out_grads1, out_hop1, in_grads1[0])
+    in_total0, out_total0, out_total1 = total(in_totals0), total(out_totals0), total(out_totals1)
+    in_total1 = total(in_totals1)
     outputs = jnp.zeros_like(stored)
     for phase, block, back in ((0, result0, returned0), (1, result2, returned1)):
         first = half * place[OWN + phase]

time: 275 us -> 251 us (0.913)
  waiting for transfers between devices: 117 us -> 105 us
  starting transfers between devices: 85.8 us -> 75.3 us
  other arithmetic: 9.77 us -> 3.79 us
    ppermute x10 -> x0, starting transfers between devices: 23.2 us -> none  [the longest x3 16.2 us: trade_inward(): return lax.ppermute(block, 'dp', [(3, 2), (0, 1)])]
    ppermute x10 -> x0, waiting for transfers between devices: 16.3 us -> none  [the longest x2 13.4 us: trade_outward(): return lax.ppermute(block, 'dp', [(2, 3), (1, 0)])]
    ppermute x10 -> x24, starting transfers between devices: 29.4 us -> 45.3 us  [rotate(): lax.ppermute(block, 'dp', [(i, (i + shift) % count) for i in range(count)])]
    ppermute x10 -> x24, waiting for transfers between devices: 51.7 us -> 63.2 us  [rotate(): lax.ppermute(block, 'dp', [(i, (i + shift) % count) for i in range(count)])]
    ppermute x7 -> x5, starting transfers between devices: 10 us -> 5.42 us  [swap_both(): lax.ppermute(block, ('section', 'mp'), [(i, i ^ 6) for i in range(8)])]
    select_n x6 -> x1, other arithmetic: 4.98 us -> 1.18 us  [two_sections(): held0 = jnp.where(own == 1, mine, moved)]
    ppermute x7 -> x5, waiting for transfers between devices: 7.75 us -> 4.39 us  [swap_both(): lax.ppermute(block, ('section', 'mp'), [(i, i ^ 6) for i in range(8)])]
    unnamed x20 -> x32, local copies, waits for them, and re-layouts: 4.8 us -> 8.14 us
  transfers between devices with their start and end apart: 54 -> 53, of which waited for: 21 -> 23; matrix products, arithmetic and copies ran while one was open for 7% -> 5% of each run, Pallas kernels for 14% -> 18%
where the time goes in v4:
time: 251 us; the launch traced here: 250 us
  waiting for transfers between devices  105 us (42%)
  starting transfers between devices  75.3 us (30%)
  Pallas kernels  46.3 us (18%)
  local copies, waits for them, and re-layouts  18.5 us (7%)
  other arithmetic  3.79 us (2%)
    ppermute x24, waiting for transfers between devices, rotate(): lax.ppermute(block, 'dp', [(i, (i + shift) % count) for i in range(count)])  63.2 us
    ppermute x24, starting transfers between devices, rotate(): lax.ppermute(block, 'dp', [(i, (i + shift) % count) for i in range(count)])  45.3 us
    pallas_call x8, Pallas kernels, call(): pl.pallas_call(kernel, out_shape=outs, grid_spec=pltpu.PrefetchScalarGrid...  44.6 us
    ppermute x11, waiting for transfers between devices, swap_section(): return lax.ppermute(block, 'section', [(0, 1), (1, 0)])  34.6 us
    ppermute x11, starting transfers between devices, swap_section(): return lax.ppermute(block, 'section', [(0, 1), (1, 0)])  16.8 us
    unnamed x32, local copies, waits for them, and re-layouts  8.14 us
    ppermute x5, starting transfers between devices, swap_chip(): return lax.ppermute(block, 'mp', [(i, i ^ 2) for i in range(4)])  6 us
    ppermute x5, starting transfers between devices, swap_both(): lax.ppermute(block, ('section', 'mp'), [(i, i ^ 6) for i in range(8)])  5.42 us
  transfers between devices with their start and end apart: 53, of which 23 were waited for; matrix products, arithmetic and copies ran while one was open for 5% of the time, Pallas kernels for 18%

profile of v4, /device:TPU:0, one launch (start us, length us, event | category | flops | bytes accessed | tf_op | source)
XLA Modules:
  0.0 250.5 jit_solution(14825582190498227218)
XLA Ops:
  8.9 8.8 %collective-permute-done = bf16[2,1024,128]{2,1,0:T(8,128)(2,1)} collective-permute-done((bf16[2,1024,128]{2,1,0:T(8,128)(2,1)S(1)}, bf16[2,1024,128]{2,1,0:T(8,128)(2,1)}, u32[]{:S(2)}, u32[]{:S(2)}) %collective-permute-start) | collective-permute-done | bytes 524320 | tf_op jit(solution)/shard_map/ppermute | solution.py:35
  20.6 3.7 %collective-permute-start.3 = (bf16[2,1024,128]{2,1,0:T(8,128)(2,1)S(1)}, bf16[2,1024,128]{2,1,0:T(8,128)(2,1)S(1)}, u32[]{:S(2)}, u32[]{:S(2)}) collective-permute-start(bf16[2,1024,128]{2,1,0:T(8,128)(2,1)S(1)} %get-tuple-element.150.refs_5_.refs_7_), channel_id=1, source_target_pairs={{0,3},{1,0},{2,1},{3,2},{4,7},{5,4},{6,5},{7,6},{8,11},{9,8},{10,9... | collective-permute-start | bytes 1572872 | tf_op jit(solution)/shard_map/ppermute | solution.py:16
  24.3 12.4 %collective-permute-done.3.refs_6_.refs_8_ = bf16[2,1024,128]{2,1,0:T(8,128)(2,1)S(1)} collective-permute-done((bf16[2,1024,128]{2,1,0:T(8,128)(2,1)S(1)}, bf16[2,1024,128]{2,1,0:T(8,128)(2,1)S(1)}, u32[]{:S(2)}, u32[]{:S(2)}) %collective-permute-start.3) | collective-permute-done | bytes 524320 | tf_op jit(solution)/shard_map/ppermute | solution.py:16
  37.5 4.3 %collective-permute-start.10 = (bf16[1024,128]{1,0:T(8,128)(2,1)}, bf16[1024,128]{1,0:T(8,128)(2,1)S(1)}, u32[]{:S(2)}, u32[]{:S(2)}) collective-permute-start(bf16[1024,128]{1,0:T(8,128)(2,1)} %slice_bitcast_fusion), channel_id=1, source_target_pairs={{0,3},{1,0},{2,1},{3,2},{4,7},{5,4},{6,5},{7,6},{8,11},{9,8},{10,9... | collective-permute-start | bytes 786440 | tf_op jit(solution)/shard_map/ppermute | solution.py:16
  41.8 7.1 %collective-permute-done.2.refs_7_.refs_9_ = bf16[2,1024,128]{2,1,0:T(8,128)(2,1)S(1)} collective-permute-done((bf16[2,1024,128]{2,1,0:T(8,128)(2,1)S(1)}, bf16[2,1024,128]{2,1,0:T(8,128)(2,1)S(1)}, u32[]{:S(2)}, u32[]{:S(2)}) %collective-permute-start.2) | collective-permute-done | bytes 524320 | tf_op jit(solution)/shard_map/ppermute | solution.py:16
  53.7 7.4 %collective-permute-done.9.refs_8_.refs_10_ = bf16[1024,128]{1,0:T(8,128)(2,1)} collective-permute-done((bf16[1024,128]{1,0:T(8,128)(2,1)}, bf16[1024,128]{1,0:T(8,128)(2,1)}, u32[]{:S(2)}, u32[]{:S(2)}) %collective-permute-start.9) | collective-permute-done | bytes 262176 | tf_op jit(solution)/shard_map/ppermute | solution.py:16
  68.1 7.2 %first_part.1 = (bf16[2,2,128,640]{3,2,1,0:T(8,128)(2,1)S(1)}, bf16[2,2,128,640]{3,2,1,0:T(8,128)(2,1)S(1)}, bf16[2,2,128,512]{3,2,1,0:T(8,128)(2,1)S(1)}, bf16[2,2,128,512]{3,2,1,0:T(8,128)(2,1)S(1)}) custom-call(s32[13]{0:T(128)S(1)} %concatenate.15.refs_0_.place, bf16[8,128,2048]{2,1,0:T(8,128)(2,1)} %bitcast.47, bf16[2,4,128,1024]{3,2,1,0:T(8,128)(2,1)} %copy-done, ...), custom_call_target="tpu_custom_call" | custom-call | flops 2147483648 | bytes 14958592 | tf_op jit(solution)/shard_map/first_part/pallas_call | solution.py:343
  83.4 8.4 %collective-permute-done.4.refs_5_.refs_13_.refs_9_ = bf16[2,1024,128]{2,1,0:T(8,128)(2,1)S(1)} collective-permute-done((bf16[2,1024,128]{2,1,0:T(8,128)(2,1)S(1)}, bf16[2,1024,128]{2,1,0:T(8,128)(2,1)S(1)}, u32[]{:S(2)}, u32[]{:S(2)}) %collective-permute-start.4) | collective-permute-done | bytes 524320 | tf_op jit(solution)/shard_map/ppermute | solution.py:16
  91.8 4.3 %collective-permute-start.7 = (bf16[1024,128]{1,0:T(8,128)(2,1)S(1)}, bf16[1024,128]{1,0:T(8,128)(2,1)S(1)}, u32[]{:S(2)}, u32[]{:S(2)}) collective-permute-start(bf16[1024,128]{1,0:T(8,128)(2,1)S(1)} %slice_bitcast_fusion.2), channel_id=1, source_target_pairs={{0,3},{1,0},{2,1},{3,2},{4,7},{5,4},{6,5},{7,6},{8,11},{9,8},{10,9... | collective-permute-start | bytes 786440 | tf_op jit(solution)/shard_map/ppermute | solution.py:16
  103.0 4.1 %hidden_part.1 = (bf16[2,2,128,640]{3,2,1,0:T(8,128)(2,1)S(1)}, bf16[2,2,128,640]{3,2,1,0:T(8,128)(2,1)S(1)}) custom-call(s32[13]{0:T(128)S(1)} %concatenate.15.refs_0_.place, bf16[8,128,2048]{2,1,0:T(8,128)(2,1)} %bitcast.48, bf16[2,4,128,1024]{3,2,1,0:T(8,128)(2,1)S(1)} %copy-done.1, f32[2,2048]{1,0:T(2,128)S(1)} %copy-done.12, ...), custom_call_target="tpu_custom_call" | custom-call | flops 1073741824 | bytes 9715712 | tf_op jit(solution)/shard_map/hidden_part/pallas_call | solution.py:343
  113.0 4.9 %in_grad.2 = (f32[128,1024]{1,0:T(8,128)S(1)}, bf16[128,1024]{1,0:T(8,128)(2,1)S(1)}, bf16[128,1024]{1,0:T(8,128)(2,1)S(1)}, bf16[128,1024]{1,0:T(8,128)(2,1)S(1)}) custom-call(s32[13]{0:T(128)S(1)} %concatenate.15.refs_0_.place, bf16[8,128,2048]{2,1,0:T(8,128)(2,1)} %bitcast.49, bf16[2,4,128,1024]{3,2,1,0:T(8,128)(2,1)S(1)} %copy-done.1, ...), custom_call_target="tpu_custom_call" | custom-call | flops 1073741824 | bytes 8929280 | tf_op jit(solution)/shard_map/in_grad/pallas_call | solution.py:343
  117.9 9.3 %first_back.1 = (bf16[4,128,1024]{2,1,0:T(8,128)(2,1)}, bf16[4,128,1024]{2,1,0:T(8,128)(2,1)}, bf16[2,2,128,512]{3,2,1,0:T(8,128)(2,1)S(1)}, bf16[2,2,128,512]{3,2,1,0:T(8,128)(2,1)S(1)}) custom-call(s32[13]{0:T(128)S(1)} %concatenate.15.refs_0_.place, bf16[8,128,2048]{2,1,0:T(8,128)(2,1)} %bitcast.50, bf16[2,4,128,1024]{3,2,1,0:T(8,128)(2,1)} %copy-done, ...), custom_call_target="tpu_custom_call" | custom-call | flops 2147483648 | bytes 19152896 | tf_op jit(solution)/shard_map/first_back/pallas_call | solution.py:343
  132.8 5.0 %top_grad.1 = (f32[128,1024]{1,0:T(8,128)S(1)}, bf16[128,1024]{1,0:T(8,128)(2,1)S(1)}, bf16[128,1024]{1,0:T(8,128)(2,1)S(1)}, bf16[128,1024]{1,0:T(8,128)(2,1)S(1)}) custom-call(s32[13]{0:T(128)S(1)} %concatenate.15.refs_0_.place, bf16[8,128,2048]{2,1,0:T(8,128)(2,1)} %top.1, bf16[2,2,128,512]{3,2,1,0:T(8,128)(2,1)S(1)} %get-tuple-element.102.p0, ...), custom_call_target="tpu_custom_call" | custom-call | flops 1073741824 | bytes 6553600 | tf_op jit(solution)/shard_map/top_grad/pallas_call | solution.py:343
  138.5 6.0 %collective-permute-done.26.refs_3_ = bf16[128,1024]{1,0:T(8,128)(2,1)S(1)} collective-permute-done((bf16[128,1024]{1,0:T(8,128)(2,1)S(1)}, bf16[128,1024]{1,0:T(8,128)(2,1)S(1)}, u32[]{:S(2)}, u32[]{:S(2)}) %collective-permute-start.26) | collective-permute-done | bytes 262176 | tf_op jit(solution)/shard_map/ppermute | solution.py:35
  148.4 4.4 %collective-permute-done.31 = bf16[128,640]{1,0:T(8,128)(2,1)S(1)} collective-permute-done((bf16[128,640]{1,0:T(8,128)(2,1)S(1)}, bf16[128,640]{1,0:T(8,128)(2,1)S(1)}, u32[]{:S(2)}, u32[]{:S(2)}) %collective-permute-start.31) | collective-permute-done | bytes 163872 | tf_op jit(solution)/shard_map/ppermute | solution.py:47
  166.0 4.9 %in_grad.3 = (f32[128,1024]{1,0:T(8,128)S(1)}, bf16[128,1024]{1,0:T(8,128)(2,1)S(1)}, bf16[128,1024]{1,0:T(8,128)(2,1)S(1)}, bf16[128,1024]{1,0:T(8,128)(2,1)S(1)}) custom-call(s32[13]{0:T(128)S(1)} %concatenate.15.refs_0_.place, bf16[8,128,2048]{2,1,0:T(8,128)(2,1)} %bitcast.51, bf16[2,4,128,1024]{3,2,1,0:T(8,128)(2,1)S(1)} %copy-done.2, ...), custom_call_target="tpu_custom_call" | custom-call | flops 1073741824 | bytes 8929280 | tf_op jit(solution)/shard_map/in_grad/pallas_call | solution.py:343
  171.0 3.9 %collective-permute-start.34 = (bf16[64,1024]{1,0:T(8,128)(2,1)S(1)}, bf16[64,1024]{1,0:T(8,128)(2,1)S(1)}, u32[]{:S(2)}, u32[]{:S(2)}) collective-permute-start(bf16[64,1024]{1,0:T(8,128)(2,1)S(1)} %get-tuple-element.162), channel_id=1, source_target_pairs={{0,3},{1,0},{2,1},{3,2},{4,7},{5,4},{6,5},{7,6},{8,11},{9,8},{10,9... | collective-permute-start | bytes 393224 | tf_op jit(solution)/shard_map/ppermute | solution.py:16
  179.1 4.8 %collective-permute-start.49 = (bf16[128,1024]{1,0:T(8,128)(2,1)S(1)}, bf16[128,1024]{1,0:T(8,128)(2,1)S(1)}, u32[]{:S(2)}, u32[]{:S(2)}) collective-permute-start(bf16[128,1024]{1,0:T(8,128)(2,1)S(1)} %get-tuple-element.138), channel_id=1, source_target_pairs={{0,3},{1,0},{2,1},{3,2},{4,7},{5,4},{6,5},{7,6},{8,11},{9,8},{10,9... | collective-permute-start | bytes 786440 | tf_op jit(solution)/shard_map/ppermute | solution.py:16
  183.9 4.7 %collective-permute-start.44 = (bf16[128,1024]{1,0:T(8,128)(2,1)S(1)}, bf16[128,1024]{1,0:T(8,128)(2,1)S(1)}, u32[]{:S(2)}, u32[]{:S(2)}) collective-permute-start(bf16[128,1024]{1,0:T(8,128)(2,1)S(1)} %get-tuple-element.131), channel_id=1, source_target_pairs={{0,1},{1,2},{2,3},{3,0},{4,5},{5,6},{6,7},{7,4},{8,9},{9,10},{10,1... | collective-permute-start | bytes 786440 | tf_op jit(solution)/shard_map/ppermute | solution.py:16
  191.4 5.7 %last_back.1 = (bf16[4,128,1024]{2,1,0:T(8,128)(2,1)S(1)}, bf16[4,128,1024]{2,1,0:T(8,128)(2,1)S(1)}) custom-call(s32[13]{0:T(128)S(1)} %concatenate.15.refs_0_.place, bf16[8,128,2048]{2,1,0:T(8,128)(2,1)} %bitcast.52, bf16[2,4,128,1024]{3,2,1,0:T(8,128)(2,1)} %copy-done, f32[2,2048]{1,0:T(2,128)S(1)} %copy-done.12, ...), custom_call_target="tpu_custom_call" | custom-call | flops 1073741824 | bytes 13910016 | tf_op jit(solution)/shard_map/last_back/pallas_call | solution.py:343
  201.7 5.7 %collective-permute-done.45 = bf16[128,1024]{1,0:T(8,128)(2,1)S(1)} collective-permute-done((bf16[128,1024]{1,0:T(8,128)(2,1)S(1)}, bf16[128,1024]{1,0:T(8,128)(2,1)S(1)}, u32[]{:S(2)}, u32[]{:S(2)}) %collective-permute-start.45) | collective-permute-done | bytes 262176 | tf_op jit(solution)/shard_map/ppermute | solution.py:16
  214.3 4.3 %collective-permute-done.40 = bf16[128,1024]{1,0:T(8,128)(2,1)S(1)} collective-permute-done((bf16[128,1024]{1,0:T(8,128)(2,1)S(1)}, bf16[128,1024]{1,0:T(8,128)(2,1)S(1)}, u32[]{:S(2)}, u32[]{:S(2)}) %collective-permute-start.40) | collective-permute-done | bytes 262176 | tf_op jit(solution)/shard_map/ppermute | solution.py:16
  220.0 4.2 %collective-permute-done.35 = bf16[128,1024]{1,0:T(8,128)(2,1)S(1)} collective-permute-done((bf16[128,1024]{1,0:T(8,128)(2,1)S(1)}, bf16[128,1024]{1,0:T(8,128)(2,1)S(1)}, u32[]{:S(2)}, u32[]{:S(2)}) %collective-permute-start.35) | collective-permute-done | bytes 262176 | tf_op jit(solution)/shard_map/ppermute | solution.py:16
  230.7 13.2 %collective-permute-done.50 = bf16[128,1024]{1,0:T(8,128)(2,1)S(1)} collective-permute-done((bf16[128,1024]{1,0:T(8,128)(2,1)S(1)}, bf16[128,1024]{1,0:T(8,128)(2,1)S(1)}, u32[]{:S(2)}, u32[]{:S(2)}) %collective-permute-start.50) | collective-permute-done | bytes 262176 | tf_op jit(solution)/shard_map/ppermute | solution.py:35
  (159 shorter events, 100.9 us)
Async XLA Ops:
  2.7 15.1 %collective-permute-start = (bf16[2,1024,128]{2,1,0:T(8,128)(2,1)S(1)}, bf16[2,1024,128]{2,1,0:T(8,128)(2,1)}, u32[]{:S(2)}, u32[]{:S(2)}) collective-permute-start(bf16[2,1024,128]{2,1,0:T(8,128)(2,1)S(1)} %pad_maximum_fusion.3), channel_id=1, source_target_pairs={{0,16},{16,0},{1,17},{17,1},{2,18},{18,2},{3,19},{19,3},{4,20},{20... | collective-permute-start | bytes 1572872 | tf_op jit(solution)/shard_map/ppermute | solution.py:35
  17.7 47.0 %collective-permute-start.1 = (bf16[2,4,128,1024]{3,2,1,0:T(8,128)(2,1)}, bf16[2,4,128,1024]{3,2,1,0:T(8,128)(2,1)S(1)}, u32[]{:S(2)}, u32[]{:S(2)}) collective-permute-start(bf16[2,4,128,1024]{3,2,1,0:T(8,128)(2,1)} %pad_maximum_fusion), channel_id=1, source_target_pairs={{0,16},{16,0},{1,17},{17,1},{2,18},{18,2},{3,19},{19,3},{4,20},{20... | collective-permute-start | bytes 6291464 | tf_op jit(solution)/shard_map/ppermute | solution.py:35
  20.6 16.0 %collective-permute-start.3 = (bf16[2,1024,128]{2,1,0:T(8,128)(2,1)S(1)}, bf16[2,1024,128]{2,1,0:T(8,128)(2,1)S(1)}, u32[]{:S(2)}, u32[]{:S(2)}) collective-permute-start(bf16[2,1024,128]{2,1,0:T(8,128)(2,1)S(1)} %get-tuple-element.150.refs_5_.refs_7_), channel_id=1, source_target_pairs={{0,3},{1,0},{2,1},{3,2},{4,7},{5,4},{6,5},{7,6},{8,11},{9,8},{10,9... | collective-permute-start | bytes 1572872 | tf_op jit(solution)/shard_map/ppermute | solution.py:16
  24.3 24.6 %collective-permute-start.2 = (bf16[2,1024,128]{2,1,0:T(8,128)(2,1)S(1)}, bf16[2,1024,128]{2,1,0:T(8,128)(2,1)S(1)}, u32[]{:S(2)}, u32[]{:S(2)}) collective-permute-start(bf16[2,1024,128]{2,1,0:T(8,128)(2,1)S(1)} %get-tuple-element.150.refs_5_.refs_7_), channel_id=1, source_target_pairs={{0,1},{1,2},{2,3},{3,0},{4,5},{5,6},{6,7},{7,4},{8,9},{9,10},{10,1... | collective-permute-start | bytes 1572872 | tf_op jit(solution)/shard_map/ppermute | solution.py:16
  37.5 16.2 %collective-permute-start.10 = (bf16[1024,128]{1,0:T(8,128)(2,1)}, bf16[1024,128]{1,0:T(8,128)(2,1)S(1)}, u32[]{:S(2)}, u32[]{:S(2)}) collective-permute-start(bf16[1024,128]{1,0:T(8,128)(2,1)} %slice_bitcast_fusion), channel_id=1, source_target_pairs={{0,3},{1,0},{2,1},{3,2},{4,7},{5,4},{6,5},{7,6},{8,11},{9,8},{10,9... | collective-permute-start | bytes 786440 | tf_op jit(solution)/shard_map/ppermute | solution.py:16
  51.4 28.0 %collective-permute-start.5 = (bf16[2,1024,128]{2,1,0:T(8,128)(2,1)S(1)}, bf16[2,1024,128]{2,1,0:T(8,128)(2,1)S(1)}, u32[]{:S(2)}, u32[]{:S(2)}) collective-permute-start(bf16[2,1024,128]{2,1,0:T(8,128)(2,1)S(1)} %get-tuple-element.73.refs_4_.refs_12_.refs_8_), channel_id=1, source_target_pairs={{0,1},{1,2},{2,3},{3,0},{4,5},{5,6},{6,7},{7,4},{8,9},{9,10},{10,1... | collective-permute-start | bytes 1572872 | tf_op jit(solution)/shard_map/ppermute | solution.py:16
  75.9 15.8 %collective-permute-start.4 = (bf16[2,1024,128]{2,1,0:T(8,128)(2,1)S(1)}, bf16[2,1024,128]{2,1,0:T(8,128)(2,1)S(1)}, u32[]{:S(2)}, u32[]{:S(2)}) collective-permute-start(bf16[2,1024,128]{2,1,0:T(8,128)(2,1)S(1)} %get-tuple-element.73.refs_4_.refs_12_.refs_8_), channel_id=1, source_target_pairs={{0,3},{1,0},{2,1},{3,2},{4,7},{5,4},{6,5},{7,6},{8,11},{9,8},{10,9... | collective-permute-start | bytes 1572872 | tf_op jit(solution)/shard_map/ppermute | solution.py:16
  79.4 20.6 %collective-permute-start.6 = (bf16[1024,128]{1,0:T(8,128)(2,1)S(1)}, bf16[1024,128]{1,0:T(8,128)(2,1)S(1)}, u32[]{:S(2)}, u32[]{:S(2)}) collective-permute-start(bf16[1024,128]{1,0:T(8,128)(2,1)S(1)} %slice_bitcast_fusion.3), channel_id=1, source_target_pairs={{0,1},{1,2},{2,3},{3,0},{4,5},{5,6},{6,7},{7,4},{8,9},{9,10},{10,1... | collective-permute-start | bytes 786440 | tf_op jit(solution)/shard_map/ppermute | solution.py:16
  79.8 16.3 %collective-permute-start.13 = (bf16[128,1152]{1,0:T(8,128)(2,1)S(1)}, bf16[128,1152]{1,0:T(8,128)(2,1)S(1)}, u32[]{:S(2)}, u32[]{:S(2)}) collective-permute-start(bf16[128,1152]{1,0:T(8,128)(2,1)S(1)} %get-tuple-element.81), channel_id=1, source_target_pairs={{0,8},{4,12},{8,0},{12,4},{1,9},{5,13},{9,1},{13,5},{2,10},{6,14},... | collective-permute-start | bytes 884744 | tf_op jit(solution)/shard_map/ppermute | solution.py:43
  109.4 17.8 %collective-permute-start.20 = (bf16[128,1152]{1,0:T(8,128)(2,1)S(1)}, bf16[128,1152]{1,0:T(8,128)(2,1)S(1)}, u32[]{:S(2)}, u32[]{:S(2)}) collective-permute-start(bf16[128,1152]{1,0:T(8,128)(2,1)S(1)} %get-tuple-element.94), channel_id=1, source_target_pairs={{0,8},{4,12},{8,0},{12,4},{1,9},{5,13},{9,1},{13,5},{2,10},{6,14},... | collective-permute-start | bytes 884744 | tf_op jit(solution)/shard_map/ppermute | solution.py:43
  111.0 16.2 %collective-permute-start.21 = (bf16[128,1152]{1,0:T(8,128)(2,1)S(1)}, bf16[128,1152]{1,0:T(8,128)(2,1)S(1)}, u32[]{:S(2)}, u32[]{:S(2)}) collective-permute-start(bf16[128,1152]{1,0:T(8,128)(2,1)S(1)} %get-tuple-element.95), channel_id=1, source_target_pairs={{0,16},{16,0},{1,17},{17,1},{2,18},{18,2},{3,19},{19,3},{4,20},{20... | collective-permute-start | bytes 884744 | tf_op jit(solution)/shard_map/ppermute | solution.py:35
  154.7 21.8 %collective-permute-start.38 = (bf16[64,1024]{1,0:T(8,128)(2,1)S(1)}, bf16[64,1024]{1,0:T(8,128)(2,1)S(1)}, u32[]{:S(2)}, u32[]{:S(2)}) collective-permute-start(bf16[64,1024]{1,0:T(8,128)(2,1)S(1)} %get-tuple-element.160), channel_id=1, source_target_pairs={{0,3},{1,0},{2,1},{3,2},{4,7},{5,4},{6,5},{7,6},{8,11},{9,8},{10,9... | collective-permute-start | bytes 393224 | tf_op jit(solution)/shard_map/ppermute | solution.py:16
  174.8 53.8 %collective-permute-start.51 = (bf16[4,128,1024]{2,1,0:T(8,128)(2,1)S(1)}, bf16[4,128,1024]{2,1,0:T(8,128)(2,1)S(1)}, u32[]{:S(2)}, u32[]{:S(2)}) collective-permute-start(bf16[4,128,1024]{2,1,0:T(8,128)(2,1)S(1)} %copy-done.11), channel_id=1, source_target_pairs={{0,16},{16,0},{1,17},{17,1},{2,18},{18,2},{3,19},{19,3},{4,20},{20... | collective-permute-start | bytes 3145736 | tf_op jit(solution)/shard_map/ppermute | solution.py:35
  176.5 20.7 %collective-permute-start.48 = (bf16[128,1024]{1,0:T(8,128)(2,1)S(1)}, bf16[128,1024]{1,0:T(8,128)(2,1)S(1)}, u32[]{:S(2)}, u32[]{:S(2)}) collective-permute-start(bf16[128,1024]{1,0:T(8,128)(2,1)S(1)} %get-tuple-element.137), channel_id=1, source_target_pairs={{0,1},{1,2},{2,3},{3,0},{4,5},{5,6},{6,7},{7,4},{8,9},{9,10},{10,1... | collective-permute-start | bytes 786440 | tf_op jit(solution)/shard_map/ppermute | solution.py:16
  179.1 20.1 %collective-permute-start.49 = (bf16[128,1024]{1,0:T(8,128)(2,1)S(1)}, bf16[128,1024]{1,0:T(8,128)(2,1)S(1)}, u32[]{:S(2)}, u32[]{:S(2)}) collective-permute-start(bf16[128,1024]{1,0:T(8,128)(2,1)S(1)} %get-tuple-element.138), channel_id=1, source_target_pairs={{0,3},{1,0},{2,1},{3,2},{4,7},{5,4},{6,5},{7,6},{8,11},{9,8},{10,9... | collective-permute-start | bytes 786440 | tf_op jit(solution)/shard_map/ppermute | solution.py:16
  183.9 17.7 %collective-permute-start.44 = (bf16[128,1024]{1,0:T(8,128)(2,1)S(1)}, bf16[128,1024]{1,0:T(8,128)(2,1)S(1)}, u32[]{:S(2)}, u32[]{:S(2)}) collective-permute-start(bf16[128,1024]{1,0:T(8,128)(2,1)S(1)} %get-tuple-element.131), channel_id=1, source_target_pairs={{0,1},{1,2},{2,3},{3,0},{4,5},{5,6},{6,7},{7,4},{8,9},{9,10},{10,1... | collective-permute-start | bytes 786440 | tf_op jit(solution)/shard_map/ppermute | solution.py:16
  188.7 18.7 %collective-permute-start.45 = (bf16[128,1024]{1,0:T(8,128)(2,1)S(1)}, bf16[128,1024]{1,0:T(8,128)(2,1)S(1)}, u32[]{:S(2)}, u32[]{:S(2)}) collective-permute-start(bf16[128,1024]{1,0:T(8,128)(2,1)S(1)} %get-tuple-element.132), channel_id=1, source_target_pairs={{0,3},{1,0},{2,1},{3,2},{4,7},{5,4},{6,5},{7,6},{8,11},{9,8},{10,9... | collective-permute-start | bytes 786440 | tf_op jit(solution)/shard_map/ppermute | solution.py:16
  197.2 15.8 %collective-permute-start.39 = (bf16[128,1024]{1,0:T(8,128)(2,1)S(1)}, bf16[128,1024]{1,0:T(8,128)(2,1)S(1)}, u32[]{:S(2)}, u32[]{:S(2)}) collective-permute-start(bf16[128,1024]{1,0:T(8,128)(2,1)S(1)} %get-tuple-element.125), channel_id=1, source_target_pairs={{0,1},{1,2},{2,3},{3,0},{4,5},{5,6},{6,7},{7,4},{8,9},{9,10},{10,1... | collective-permute-start | bytes 786440 | tf_op jit(solution)/shard_map/ppermute | solution.py:16
  199.2 19.4 %collective-permute-start.40 = (bf16[128,1024]{1,0:T(8,128)(2,1)S(1)}, bf16[128,1024]{1,0:T(8,128)(2,1)S(1)}, u32[]{:S(2)}, u32[]{:S(2)}) collective-permute-start(bf16[128,1024]{1,0:T(8,128)(2,1)S(1)} %get-tuple-element.126), channel_id=1, source_target_pairs={{0,3},{1,0},{2,1},{3,2},{4,7},{5,4},{6,5},{7,6},{8,11},{9,8},{10,9... | collective-permute-start | bytes 786440 | tf_op jit(solution)/shard_map/ppermute | solution.py:16
  201.7 22.6 %collective-permute-start.35 = (bf16[128,1024]{1,0:T(8,128)(2,1)S(1)}, bf16[128,1024]{1,0:T(8,128)(2,1)S(1)}, u32[]{:S(2)}, u32[]{:S(2)}) collective-permute-start(bf16[128,1024]{1,0:T(8,128)(2,1)S(1)} %get-tuple-element.119), channel_id=1, source_target_pairs={{0,1},{1,2},{2,3},{3,0},{4,5},{5,6},{6,7},{7,4},{8,9},{9,10},{10,1... | collective-permute-start | bytes 786440 | tf_op jit(solution)/shard_map/ppermute | solution.py:16
  207.4 19.6 %collective-permute-start.36 = (bf16[128,1024]{1,0:T(8,128)(2,1)S(1)}, bf16[128,1024]{1,0:T(8,128)(2,1)S(1)}, u32[]{:S(2)}, u32[]{:S(2)}) collective-permute-start(bf16[128,1024]{1,0:T(8,128)(2,1)S(1)} %get-tuple-element.120), channel_id=1, source_target_pairs={{0,3},{1,0},{2,1},{3,2},{4,7},{5,4},{6,5},{7,6},{8,11},{9,8},{10,9... | collective-permute-start | bytes 786440 | tf_op jit(solution)/shard_map/ppermute | solution.py:16
  212.9 35.3 %collective-permute-start.52 = (bf16[4,128,1024]{2,1,0:T(8,128)(2,1)S(1)}, bf16[4,128,1024]{2,1,0:T(8,128)(2,1)}, u32[]{:S(2)}, u32[]{:S(2)}) collective-permute-start(bf16[4,128,1024]{2,1,0:T(8,128)(2,1)S(1)} %get-tuple-element.115), channel_id=1, source_target_pairs={{0,16},{16,0},{1,17},{17,1},{2,18},{18,2},{3,19},{19,3},{4,20},{20... | collective-permute-start | bytes 3145736 | tf_op jit(solution)/shard_map/ppermute | solution.py:35
  218.6 25.3 %collective-permute-start.50 = (bf16[128,1024]{1,0:T(8,128)(2,1)S(1)}, bf16[128,1024]{1,0:T(8,128)(2,1)S(1)}, u32[]{:S(2)}, u32[]{:S(2)}) collective-permute-start(bf16[128,1024]{1,0:T(8,128)(2,1)S(1)} %get-tuple-element.146), channel_id=1, source_target_pairs={{0,16},{16,0},{1,17},{17,1},{2,18},{18,2},{3,19},{19,3},{4,20},{20... | collective-permute-start | bytes 786440 | tf_op jit(solution)/shard_map/ppermute | solution.py:35
  227.2 19.5 %collective-permute-start.41 = (bf16[128,1024]{1,0:T(8,128)(2,1)S(1)}, bf16[128,1024]{1,0:T(8,128)(2,1)S(1)}, u32[]{:S(2)}, u32[]{:S(2)}) collective-permute-start(bf16[128,1024]{1,0:T(8,128)(2,1)S(1)} %get-tuple-element.148), channel_id=1, source_target_pairs={{0,16},{16,0},{1,17},{17,1},{2,18},{18,2},{3,19},{19,3},{4,20},{20... | collective-permute-start | bytes 786440 | tf_op jit(solution)/shard_map/ppermute | solution.py:35
  (44 other events, 530.6 us)

commit v5 on v4

--- a/solution.py
+++ b/solution.py
@@ -380,9 +380,9 @@
     )
 
 
-def pair_spread(block):
+def pair_spread(block, *earlier):
     parts = (block,) + swap_chips(block, block, block)
-    four = jnp.stack(parts).reshape((2, 2) + block.shape)
+    four = after(jnp.stack(parts).reshape((2, 2) + block.shape), *earlier)
     return four, swap_core(four)
 
 
@@ -527,7 +527,7 @@
         [shape_of((tokens, units + PAD), F32), shape_of((tokens, units)), four_shape],
         (after(own_sum, kept),) + swap_chips(*parts) + (act0,),
     )
-    own_sum, *parts = core_sum((sent,), (kept,), act1)
+    own_sum, *parts = core_sum((after(sent, *in_hop0),), (kept,), act1)
     in_totals0 = second_hop(in_grads0, in_hop0, own_sum)
     out_grads0 = call(
         top_grad_kernel,
@@ -544,10 +544,10 @@
         bind(unit_kernel, features),
         "unit_grads",
         [shape_of((tokens, units + PAD)), four_shape],
-        (after(hidden1, out_grads0[0]), own_sum) + swap_chips(*parts) + (act1,),
+        (after(hidden1, out_grads0[0], *in_totals0[1:]), own_sum) + swap_chips(*parts) + (act1,),
     )
     out_totals0 = second_hop(out_grads0, out_hop0, scaled1)
-    scaled1 = pair_spread(scaled1)
+    scaled1 = pair_spread(scaled1, *out_hop0)
     out_grads1 = call(
         out_grad_kernel,
         "out_grad",
@@ -560,29 +560,29 @@
     )
     out_hop1 = first_hop(out_grads1)
     returned0 = swap_section(after(result1, scaled1[0]))
+    result2, result3 = call(
+        bind(last_back_kernel, 0),
+        "last_back",
+        [set_shape, set_shape],
+        (stored, received, gain, result1, result0) + scaled1 + weights1,
+        [weight_scratch, spread_scratch, rows_scratch, rows_scratch],
+        {0: own_spec(1), 1: received_spec(1), 2: gain_spec},
+        place,
+        one_dot,
+    )
+    returned1 = swap_section(result3)
     in_grads1 = call(
         bind(in_grad_kernel, 0),
         "in_grad",
         grad_shapes,
-        (stored, received, after(gain, out_grads1[0])) + scaled1,
+        (stored, received, after(gain, out_grads1[0], result3)) + scaled1,
         [grad_scratch, spread_scratch, rows_scratch],
         {0: own_spec(1), 1: received_spec(1), 2: gain_spec},
         place,
         one_dot,
     )
     in_hop1 = first_hop(in_grads1)
-    result2, result3 = call(
-        bind(last_back_kernel, 0),
-        "last_back",
-        [set_shape, set_shape],
-        (stored, received, gain, result1, after(result0, in_grads1[0])) + scaled1 + weights1,
-        [weight_scratch, spread_scratch, rows_scratch, rows_scratch],
-        {0: own_spec(1), 1: received_spec(1), 2: gain_spec},
-        place,
-        one_dot,
-    )
-    returned1 = swap_section(result3)
-    in_totals1 = second_hop(in_grads1, in_hop1, result3)
+    in_totals1 = second_hop(in_grads1, in_hop1, returned0)
     out_totals1 = second_hop(out_grads1, out_hop1, in_grads1[0])
     in_total0, out_total0, out_total1 = total(in_totals0), total(out_totals0), total(out_totals1)
     in_total1 = total(in_totals1)

time: 251 us -> 233 us (0.928)
  waiting for transfers between devices: 105 us -> 95.9 us
  starting transfers between devices: 75.3 us -> 69.2 us
    ppermute x11, waiting for transfers between devices: 34.6 us -> 20.5 us  [swap_section(): return lax.ppermute(block, 'section', [(0, 1), (1, 0)])]
    ppermute x24, waiting for transfers between devices: 63.2 us -> 70.5 us  [rotate(): lax.ppermute(block, 'dp', [(i, (i + shift) % count) for i in range(count)])]
    ppermute x24, starting transfers between devices: 45.3 us -> 40.2 us  [rotate(): lax.ppermute(block, 'dp', [(i, (i + shift) % count) for i in range(count)])]
    unnamed x32 -> x34, local copies, waits for them, and re-layouts: 8.14 us -> 8.14 us
  transfers between devices with their start and end apart: 53 -> 53, of which waited for: 23 -> 24; matrix products, arithmetic and copies ran while one was open for 5% -> 5% of each run, Pallas kernels for 18% -> 20%
where the time goes in v5:
time: 233 us
  waiting for transfers between devices  95.9 us (41%)
  starting transfers between devices  69.2 us (30%)
  Pallas kernels  46.2 us (20%)
  local copies, waits for them, and re-layouts  16.6 us (7%)
  other arithmetic  3.81 us (2%)
    ppermute x24, waiting for transfers between devices, rotate(): lax.ppermute(block, 'dp', [(i, (i + shift) % count) for i in range(count)])  70.5 us
    pallas_call x8, Pallas kernels, call(): pl.pallas_call(kernel, out_shape=outs, grid_spec=pltpu.PrefetchScalarGrid...  44.5 us
    ppermute x24, starting transfers between devices, rotate(): lax.ppermute(block, 'dp', [(i, (i + shift) % count) for i in range(count)])  40.2 us
    ppermute x11, waiting for transfers between devices, swap_section(): return lax.ppermute(block, 'section', [(0, 1), (1, 0)])  20.5 us
    ppermute x11, starting transfers between devices, swap_section(): return lax.ppermute(block, 'section', [(0, 1), (1, 0)])  15.9 us
    unnamed x34, local copies, waits for them, and re-layouts  8.14 us
    ppermute x5, starting transfers between devices, swap_chip(): return lax.ppermute(block, 'mp', [(i, i ^ 2) for i in range(4)])  5.94 us
    ppermute x5, starting transfers between devices, swap_both(): lax.ppermute(block, ('section', 'mp'), [(i, i ^ 6) for i in range(8)])  5.41 us
  transfers between devices with their start and end apart: 53, of which 24 were waited for; matrix products, arithmetic and copies ran while one was open for 5% of the time, Pallas kernels for 20%

profile of v5, /device:TPU:0, one launch (start us, length us, event | category | flops | bytes accessed | tf_op | source)
XLA Modules:
  0.0 233.0 jit_solution(8367128507310482491)
XLA Ops:
  8.9 8.8 %collective-permute-done = bf16[2,1024,128]{2,1,0:T(8,128)(2,1)} collective-permute-done((bf16[2,1024,128]{2,1,0:T(8,128)(2,1)S(1)}, bf16[2,1024,128]{2,1,0:T(8,128)(2,1)}, u32[]{:S(2)}, u32[]{:S(2)}) %collective-permute-start) | collective-permute-done | bytes 524320 | tf_op jit(solution)/shard_map/ppermute | solution.py:35
  24.3 12.4 %collective-permute-done.3.refs_6_.refs_8_ = bf16[2,1024,128]{2,1,0:T(8,128)(2,1)S(1)} collective-permute-done((bf16[2,1024,128]{2,1,0:T(8,128)(2,1)S(1)}, bf16[2,1024,128]{2,1,0:T(8,128)(2,1)S(1)}, u32[]{:S(2)}, u32[]{:S(2)}) %collective-permute-start.3) | collective-permute-done | bytes 524320 | tf_op jit(solution)/shard_map/ppermute | solution.py:16
  37.5 4.3 %collective-permute-start.10 = (bf16[1024,128]{1,0:T(8,128)(2,1)}, bf16[1024,128]{1,0:T(8,128)(2,1)S(1)}, u32[]{:S(2)}, u32[]{:S(2)}) collective-permute-start(bf16[1024,128]{1,0:T(8,128)(2,1)} %slice_bitcast_fusion), channel_id=1, source_target_pairs={{0,3},{1,0},{2,1},{3,2},{4,7},{5,4},{6,5},{7,6},{8,11},{9,8},{10,9... | collective-permute-start | bytes 786440 | tf_op jit(solution)/shard_map/ppermute | solution.py:16
  41.7 7.1 %collective-permute-done.2.refs_7_.refs_9_ = bf16[2,1024,128]{2,1,0:T(8,128)(2,1)S(1)} collective-permute-done((bf16[2,1024,128]{2,1,0:T(8,128)(2,1)S(1)}, bf16[2,1024,128]{2,1,0:T(8,128)(2,1)S(1)}, u32[]{:S(2)}, u32[]{:S(2)}) %collective-permute-start.2) | collective-permute-done | bytes 524320 | tf_op jit(solution)/shard_map/ppermute | solution.py:16
  53.7 7.4 %collective-permute-done.9.refs_8_.refs_10_ = bf16[1024,128]{1,0:T(8,128)(2,1)} collective-permute-done((bf16[1024,128]{1,0:T(8,128)(2,1)}, bf16[1024,128]{1,0:T(8,128)(2,1)}, u32[]{:S(2)}, u32[]{:S(2)}) %collective-permute-start.9) | collective-permute-done | bytes 262176 | tf_op jit(solution)/shard_map/ppermute | solution.py:16
  68.2 7.2 %first_part.1 = (bf16[2,2,128,640]{3,2,1,0:T(8,128)(2,1)S(1)}, bf16[2,2,128,640]{3,2,1,0:T(8,128)(2,1)S(1)}, bf16[2,2,128,512]{3,2,1,0:T(8,128)(2,1)S(1)}, bf16[2,2,128,512]{3,2,1,0:T(8,128)(2,1)S(1)}) custom-call(s32[13]{0:T(128)S(1)} %concatenate.15.refs_0_.place, bf16[8,128,2048]{2,1,0:T(8,128)(2,1)} %bitcast.47, bf16[2,4,128,1024]{3,2,1,0:T(8,128)(2,1)} %copy-done, ...), custom_call_target="tpu_custom_call" | custom-call | flops 2147483648 | bytes 14958592 | tf_op jit(solution)/shard_map/first_part/pallas_call | solution.py:343
  83.4 8.4 %collective-permute-done.4.refs_5_.refs_13_.refs_9_ = bf16[2,1024,128]{2,1,0:T(8,128)(2,1)S(1)} collective-permute-done((bf16[2,1024,128]{2,1,0:T(8,128)(2,1)S(1)}, bf16[2,1024,128]{2,1,0:T(8,128)(2,1)S(1)}, u32[]{:S(2)}, u32[]{:S(2)}) %collective-permute-start.4) | collective-permute-done | bytes 524320 | tf_op jit(solution)/shard_map/ppermute | solution.py:16
  91.8 4.3 %collective-permute-start.7 = (bf16[1024,128]{1,0:T(8,128)(2,1)S(1)}, bf16[1024,128]{1,0:T(8,128)(2,1)S(1)}, u32[]{:S(2)}, u32[]{:S(2)}) collective-permute-start(bf16[1024,128]{1,0:T(8,128)(2,1)S(1)} %slice_bitcast_fusion.2), channel_id=1, source_target_pairs={{0,3},{1,0},{2,1},{3,2},{4,7},{5,4},{6,5},{7,6},{8,11},{9,8},{10,9... | collective-permute-start | bytes 786440 | tf_op jit(solution)/shard_map/ppermute | solution.py:16
  103.0 4.1 %hidden_part.1 = (bf16[2,2,128,640]{3,2,1,0:T(8,128)(2,1)S(1)}, bf16[2,2,128,640]{3,2,1,0:T(8,128)(2,1)S(1)}) custom-call(s32[13]{0:T(128)S(1)} %concatenate.15.refs_0_.place, bf16[8,128,2048]{2,1,0:T(8,128)(2,1)} %bitcast.48, bf16[2,4,128,1024]{3,2,1,0:T(8,128)(2,1)S(1)} %copy-done.1, f32[2,2048]{1,0:T(2,128)S(1)} %copy-done.13, ...), custom_call_target="tpu_custom_call" | custom-call | flops 1073741824 | bytes 9715712 | tf_op jit(solution)/shard_map/hidden_part/pallas_call | solution.py:343
  113.0 4.9 %in_grad.2 = (f32[128,1024]{1,0:T(8,128)S(1)}, bf16[128,1024]{1,0:T(8,128)(2,1)S(1)}, bf16[128,1024]{1,0:T(8,128)(2,1)S(1)}, bf16[128,1024]{1,0:T(8,128)(2,1)S(1)}) custom-call(s32[13]{0:T(128)S(1)} %concatenate.15.refs_0_.place, bf16[8,128,2048]{2,1,0:T(8,128)(2,1)} %bitcast.49, bf16[2,4,128,1024]{3,2,1,0:T(8,128)(2,1)S(1)} %copy-done.1, ...), custom_call_target="tpu_custom_call" | custom-call | flops 1073741824 | bytes 8929280 | tf_op jit(solution)/shard_map/in_grad/pallas_call | solution.py:343
  121.4 9.3 %first_back.1 = (bf16[4,128,1024]{2,1,0:T(8,128)(2,1)}, bf16[4,128,1024]{2,1,0:T(8,128)(2,1)}, bf16[2,2,128,512]{3,2,1,0:T(8,128)(2,1)S(1)}, bf16[2,2,128,512]{3,2,1,0:T(8,128)(2,1)S(1)}) custom-call(s32[13]{0:T(128)S(1)} %concatenate.15.refs_0_.place, bf16[8,128,2048]{2,1,0:T(8,128)(2,1)} %bitcast.50, bf16[2,4,128,1024]{3,2,1,0:T(8,128)(2,1)} %copy-done, ...), custom_call_target="tpu_custom_call" | custom-call | flops 2147483648 | bytes 19152896 | tf_op jit(solution)/shard_map/first_back/pallas_call | solution.py:343
  133.0 3.9 %collective-permute-start.28 = (bf16[128,1024]{1,0:T(8,128)(2,1)S(1)}, bf16[128,1024]{1,0:T(8,128)(2,1)S(1)}, u32[]{:S(2)}, u32[]{:S(2)}) collective-permute-start(bf16[128,1024]{1,0:T(8,128)(2,1)S(1)} %get-tuple-element.111), channel_id=1, source_target_pairs={{0,3},{1,0},{2,1},{3,2},{4,7},{5,4},{6,5},{7,6},{8,11},{9,8},{10,9... | collective-permute-start | bytes 786440 | tf_op jit(solution)/shard_map/ppermute | solution.py:16
  140.3 5.0 %top_grad.1 = (f32[128,1024]{1,0:T(8,128)S(1)}, bf16[128,1024]{1,0:T(8,128)(2,1)S(1)}, bf16[128,1024]{1,0:T(8,128)(2,1)S(1)}, bf16[128,1024]{1,0:T(8,128)(2,1)S(1)}) custom-call(s32[13]{0:T(128)S(1)} %concatenate.15.refs_0_.place, bf16[8,128,2048]{2,1,0:T(8,128)(2,1)} %top.1, bf16[2,2,128,512]{3,2,1,0:T(8,128)(2,1)S(1)} %get-tuple-element.105.p0, ...), custom_call_target="tpu_custom_call" | custom-call | flops 1073741824 | bytes 6553600 | tf_op jit(solution)/shard_map/top_grad/pallas_call | solution.py:343
  147.0 4.7 %collective-permute-done.30.refs_3_ = bf16[128,1024]{1,0:T(8,128)(2,1)S(1)} collective-permute-done((bf16[128,1024]{1,0:T(8,128)(2,1)S(1)}, bf16[128,1024]{1,0:T(8,128)(2,1)S(1)}, u32[]{:S(2)}, u32[]{:S(2)}) %collective-permute-start.30) | collective-permute-done | bytes 262176 | tf_op jit(solution)/shard_map/ppermute | solution.py:35
  161.6 4.9 %collective-permute-done.36.hop0 = bf16[64,1024]{1,0:T(8,128)(2,1)S(1)} collective-permute-done((bf16[64,1024]{1,0:T(8,128)(2,1)S(1)}, bf16[64,1024]{1,0:T(8,128)(2,1)S(1)}, u32[]{:S(2)}, u32[]{:S(2)}) %collective-permute-start.36) | collective-permute-done | bytes 131104 | tf_op jit(solution)/shard_map/ppermute | solution.py:16
  166.6 3.8 %collective-permute-start.50 = (bf16[128,1024]{1,0:T(8,128)(2,1)S(1)}, bf16[128,1024]{1,0:T(8,128)(2,1)S(1)}, u32[]{:S(2)}, u32[]{:S(2)}) collective-permute-start(bf16[128,1024]{1,0:T(8,128)(2,1)S(1)} %get-tuple-element.141), channel_id=1, source_target_pairs={{0,3},{1,0},{2,1},{3,2},{4,7},{5,4},{6,5},{7,6},{8,11},{9,8},{10,9... | collective-permute-start | bytes 786440 | tf_op jit(solution)/shard_map/ppermute | solution.py:16
  177.3 5.7 %last_back.1 = (bf16[4,128,1024]{2,1,0:T(8,128)(2,1)S(1)}, bf16[4,128,1024]{2,1,0:T(8,128)(2,1)S(1)}) custom-call(s32[13]{0:T(128)S(1)} %concatenate.15.refs_0_.place, bf16[8,128,2048]{2,1,0:T(8,128)(2,1)} %bitcast.51, bf16[2,4,128,1024]{3,2,1,0:T(8,128)(2,1)} %copy-done, f32[2,2048]{1,0:T(2,128)S(1)} %copy-done.13, ...), custom_call_target="tpu_custom_call" | custom-call | flops 1073741824 | bytes 13910016 | tf_op jit(solution)/shard_map/last_back/pallas_call | solution.py:343
  183.0 4.9 %in_grad.3 = (f32[128,1024]{1,0:T(8,128)S(1)}, bf16[128,1024]{1,0:T(8,128)(2,1)S(1)}, bf16[128,1024]{1,0:T(8,128)(2,1)S(1)}, bf16[128,1024]{1,0:T(8,128)(2,1)S(1)}) custom-call(s32[13]{0:T(128)S(1)} %concatenate.15.refs_0_.place, bf16[8,128,2048]{2,1,0:T(8,128)(2,1)} %bitcast.52, bf16[2,4,128,1024]{3,2,1,0:T(8,128)(2,1)S(1)} %copy-done.2, ...), custom_call_target="tpu_custom_call" | custom-call | flops 1073741824 | bytes 8929280 | tf_op jit(solution)/shard_map/in_grad/pallas_call | solution.py:343
  188.6 3.8 %collective-permute-start.48 = (bf16[128,1024]{1,0:T(8,128)(2,1)S(1)}, bf16[128,1024]{1,0:T(8,128)(2,1)S(1)}, u32[]{:S(2)}, u32[]{:S(2)}) collective-permute-start(bf16[128,1024]{1,0:T(8,128)(2,1)S(1)} %get-tuple-element.136), channel_id=1, source_target_pairs={{0,3},{1,0},{2,1},{3,2},{4,7},{5,4},{6,5},{7,6},{8,11},{9,8},{10,9... | collective-permute-start | bytes 786440 | tf_op jit(solution)/shard_map/ppermute | solution.py:16
  194.3 5.3 %collective-permute-done.47 = bf16[128,1024]{1,0:T(8,128)(2,1)S(1)} collective-permute-done((bf16[128,1024]{1,0:T(8,128)(2,1)S(1)}, bf16[128,1024]{1,0:T(8,128)(2,1)S(1)}, u32[]{:S(2)}, u32[]{:S(2)}) %collective-permute-start.47) | collective-permute-done | bytes 262176 | tf_op jit(solution)/shard_map/ppermute | solution.py:16
  199.6 3.9 %collective-permute-done.48 = bf16[128,1024]{1,0:T(8,128)(2,1)S(1)} collective-permute-done((bf16[128,1024]{1,0:T(8,128)(2,1)S(1)}, bf16[128,1024]{1,0:T(8,128)(2,1)S(1)}, u32[]{:S(2)}, u32[]{:S(2)}) %collective-permute-start.48) | collective-permute-done | bytes 262176 | tf_op jit(solution)/shard_map/ppermute | solution.py:16
  205.0 4.6 %collective-permute-done.40.hop0 = bf16[64,1024]{1,0:T(8,128)(2,1)S(1)} collective-permute-done((bf16[64,1024]{1,0:T(8,128)(2,1)S(1)}, bf16[64,1024]{1,0:T(8,128)(2,1)S(1)}, u32[]{:S(2)}, u32[]{:S(2)}) %collective-permute-start.40) | collective-permute-done | bytes 131104 | tf_op jit(solution)/shard_map/ppermute | solution.py:16
  209.7 3.8 %collective-permute-start.43 = (bf16[128,1024]{1,0:T(8,128)(2,1)S(1)}, bf16[128,1024]{1,0:T(8,128)(2,1)S(1)}, u32[]{:S(2)}, u32[]{:S(2)}) collective-permute-start(bf16[128,1024]{1,0:T(8,128)(2,1)S(1)} %get-tuple-element.130), channel_id=1, source_target_pairs={{0,3},{1,0},{2,1},{3,2},{4,7},{5,4},{6,5},{7,6},{8,11},{9,8},{10,9... | collective-permute-start | bytes 786440 | tf_op jit(solution)/shard_map/ppermute | solution.py:16
  213.6 7.1 %collective-permute-done.42 = bf16[128,1024]{1,0:T(8,128)(2,1)S(1)} collective-permute-done((bf16[128,1024]{1,0:T(8,128)(2,1)S(1)}, bf16[128,1024]{1,0:T(8,128)(2,1)S(1)}, u32[]{:S(2)}, u32[]{:S(2)}) %collective-permute-start.42) | collective-permute-done | bytes 262176 | tf_op jit(solution)/shard_map/ppermute | solution.py:16
  (161 shorter events, 92.3 us)
Async XLA Ops:
  2.7 15.1 %collective-permute-start = (bf16[2,1024,128]{2,1,0:T(8,128)(2,1)S(1)}, bf16[2,1024,128]{2,1,0:T(8,128)(2,1)}, u32[]{:S(2)}, u32[]{:S(2)}) collective-permute-start(bf16[2,1024,128]{2,1,0:T(8,128)(2,1)S(1)} %pad_maximum_fusion.3), channel_id=1, source_target_pairs={{0,16},{16,0},{1,17},{17,1},{2,18},{18,2},{3,19},{19,3},{4,20},{20... | collective-permute-start | bytes 1572872 | tf_op jit(solution)/shard_map/ppermute | solution.py:35
  17.7 47.0 %collective-permute-start.1 = (bf16[2,4,128,1024]{3,2,1,0:T(8,128)(2,1)}, bf16[2,4,128,1024]{3,2,1,0:T(8,128)(2,1)S(1)}, u32[]{:S(2)}, u32[]{:S(2)}) collective-permute-start(bf16[2,4,128,1024]{3,2,1,0:T(8,128)(2,1)} %pad_maximum_fusion), channel_id=1, source_target_pairs={{0,16},{16,0},{1,17},{17,1},{2,18},{18,2},{3,19},{19,3},{4,20},{20... | collective-permute-start | bytes 6291464 | tf_op jit(solution)/shard_map/ppermute | solution.py:35
  20.6 16.0 %collective-permute-start.3 = (bf16[2,1024,128]{2,1,0:T(8,128)(2,1)S(1)}, bf16[2,1024,128]{2,1,0:T(8,128)(2,1)S(1)}, u32[]{:S(2)}, u32[]{:S(2)}) collective-permute-start(bf16[2,1024,128]{2,1,0:T(8,128)(2,1)S(1)} %get-tuple-element.152.refs_5_.refs_7_), channel_id=1, source_target_pairs={{0,3},{1,0},{2,1},{3,2},{4,7},{5,4},{6,5},{7,6},{8,11},{9,8},{10,9... | collective-permute-start | bytes 1572872 | tf_op jit(solution)/shard_map/ppermute | solution.py:16
  24.3 24.6 %collective-permute-start.2 = (bf16[2,1024,128]{2,1,0:T(8,128)(2,1)S(1)}, bf16[2,1024,128]{2,1,0:T(8,128)(2,1)S(1)}, u32[]{:S(2)}, u32[]{:S(2)}) collective-permute-start(bf16[2,1024,128]{2,1,0:T(8,128)(2,1)S(1)} %get-tuple-element.152.refs_5_.refs_7_), channel_id=1, source_target_pairs={{0,1},{1,2},{2,3},{3,0},{4,5},{5,6},{6,7},{7,4},{8,9},{9,10},{10,1... | collective-permute-start | bytes 1572872 | tf_op jit(solution)/shard_map/ppermute | solution.py:16
  37.5 16.2 %collective-permute-start.10 = (bf16[1024,128]{1,0:T(8,128)(2,1)}, bf16[1024,128]{1,0:T(8,128)(2,1)S(1)}, u32[]{:S(2)}, u32[]{:S(2)}) collective-permute-start(bf16[1024,128]{1,0:T(8,128)(2,1)} %slice_bitcast_fusion), channel_id=1, source_target_pairs={{0,3},{1,0},{2,1},{3,2},{4,7},{5,4},{6,5},{7,6},{8,11},{9,8},{10,9... | collective-permute-start | bytes 786440 | tf_op jit(solution)/shard_map/ppermute | solution.py:16
  51.4 28.1 %collective-permute-start.5 = (bf16[2,1024,128]{2,1,0:T(8,128)(2,1)S(1)}, bf16[2,1024,128]{2,1,0:T(8,128)(2,1)S(1)}, u32[]{:S(2)}, u32[]{:S(2)}) collective-permute-start(bf16[2,1024,128]{2,1,0:T(8,128)(2,1)S(1)} %get-tuple-element.74.refs_4_.refs_12_.refs_8_), channel_id=1, source_target_pairs={{0,1},{1,2},{2,3},{3,0},{4,5},{5,6},{6,7},{7,4},{8,9},{9,10},{10,1... | collective-permute-start | bytes 1572872 | tf_op jit(solution)/shard_map/ppermute | solution.py:16
  75.9 15.9 %collective-permute-start.4 = (bf16[2,1024,128]{2,1,0:T(8,128)(2,1)S(1)}, bf16[2,1024,128]{2,1,0:T(8,128)(2,1)S(1)}, u32[]{:S(2)}, u32[]{:S(2)}) collective-permute-start(bf16[2,1024,128]{2,1,0:T(8,128)(2,1)S(1)} %get-tuple-element.74.refs_4_.refs_12_.refs_8_), channel_id=1, source_target_pairs={{0,3},{1,0},{2,1},{3,2},{4,7},{5,4},{6,5},{7,6},{8,11},{9,8},{10,9... | collective-permute-start | bytes 1572872 | tf_op jit(solution)/shard_map/ppermute | solution.py:16
  79.5 20.6 %collective-permute-start.6 = (bf16[1024,128]{1,0:T(8,128)(2,1)S(1)}, bf16[1024,128]{1,0:T(8,128)(2,1)S(1)}, u32[]{:S(2)}, u32[]{:S(2)}) collective-permute-start(bf16[1024,128]{1,0:T(8,128)(2,1)S(1)} %slice_bitcast_fusion.3), channel_id=1, source_target_pairs={{0,1},{1,2},{2,3},{3,0},{4,5},{5,6},{6,7},{7,4},{8,9},{9,10},{10,1... | collective-permute-start | bytes 786440 | tf_op jit(solution)/shard_map/ppermute | solution.py:16
  79.8 16.3 %collective-permute-start.13 = (bf16[128,1152]{1,0:T(8,128)(2,1)S(1)}, bf16[128,1152]{1,0:T(8,128)(2,1)S(1)}, u32[]{:S(2)}, u32[]{:S(2)}) collective-permute-start(bf16[128,1152]{1,0:T(8,128)(2,1)S(1)} %get-tuple-element.82), channel_id=1, source_target_pairs={{0,8},{4,12},{8,0},{12,4},{1,9},{5,13},{9,1},{13,5},{2,10},{6,14},... | collective-permute-start | bytes 884744 | tf_op jit(solution)/shard_map/ppermute | solution.py:43
  81.4 14.8 %collective-permute-start.14 = (bf16[128,1152]{1,0:T(8,128)(2,1)S(1)}, bf16[128,1152]{1,0:T(8,128)(2,1)S(1)}, u32[]{:S(2)}, u32[]{:S(2)}) collective-permute-start(bf16[128,1152]{1,0:T(8,128)(2,1)S(1)} %get-tuple-element.83), channel_id=1, source_target_pairs={{0,16},{16,0},{1,17},{17,1},{2,18},{18,2},{3,19},{19,3},{4,20},{20... | collective-permute-start | bytes 884744 | tf_op jit(solution)/shard_map/ppermute | solution.py:35
  82.9 13.2 %collective-permute-start.15 = (bf16[128,1152]{1,0:T(8,128)(2,1)S(1)}, bf16[128,1152]{1,0:T(8,128)(2,1)S(1)}, u32[]{:S(2)}, u32[]{:S(2)}) collective-permute-start(bf16[128,1152]{1,0:T(8,128)(2,1)S(1)} %get-tuple-element.84), channel_id=1, source_target_pairs={{0,24},{4,28},{8,16},{12,20},{16,8},{20,12},{24,0},{28,4},{1,25},{... | collective-permute-start | bytes 884744 | tf_op jit(solution)/shard_map/ppermute | solution.py:47
  109.5 21.3 %collective-permute-start.20 = (bf16[128,1152]{1,0:T(8,128)(2,1)S(1)}, bf16[128,1152]{1,0:T(8,128)(2,1)S(1)}, u32[]{:S(2)}, u32[]{:S(2)}) collective-permute-start(bf16[128,1152]{1,0:T(8,128)(2,1)S(1)} %get-tuple-element.95), channel_id=1, source_target_pairs={{0,8},{4,12},{8,0},{12,4},{1,9},{5,13},{9,1},{13,5},{2,10},{6,14},... | collective-permute-start | bytes 884744 | tf_op jit(solution)/shard_map/ppermute | solution.py:43
  111.0 19.8 %collective-permute-start.21 = (bf16[128,1152]{1,0:T(8,128)(2,1)S(1)}, bf16[128,1152]{1,0:T(8,128)(2,1)S(1)}, u32[]{:S(2)}, u32[]{:S(2)}) collective-permute-start(bf16[128,1152]{1,0:T(8,128)(2,1)S(1)} %get-tuple-element.96), channel_id=1, source_target_pairs={{0,16},{16,0},{1,17},{17,1},{2,18},{18,2},{3,19},{19,3},{4,20},{20... | collective-permute-start | bytes 884744 | tf_op jit(solution)/shard_map/ppermute | solution.py:35
  112.6 18.3 %collective-permute-start.22 = (bf16[128,1152]{1,0:T(8,128)(2,1)S(1)}, bf16[128,1152]{1,0:T(8,128)(2,1)S(1)}, u32[]{:S(2)}, u32[]{:S(2)}) collective-permute-start(bf16[128,1152]{1,0:T(8,128)(2,1)S(1)} %get-tuple-element.97), channel_id=1, source_target_pairs={{0,24},{4,28},{8,16},{12,20},{16,8},{20,12},{24,0},{28,4},{1,25},{... | collective-permute-start | bytes 884744 | tf_op jit(solution)/shard_map/ppermute | solution.py:47
  133.0 14.0 %collective-permute-start.28 = (bf16[128,1024]{1,0:T(8,128)(2,1)S(1)}, bf16[128,1024]{1,0:T(8,128)(2,1)S(1)}, u32[]{:S(2)}, u32[]{:S(2)}) collective-permute-start(bf16[128,1024]{1,0:T(8,128)(2,1)S(1)} %get-tuple-element.111), channel_id=1, source_target_pairs={{0,3},{1,0},{2,1},{3,2},{4,7},{5,4},{6,5},{7,6},{8,11},{9,8},{10,9... | collective-permute-start | bytes 786440 | tf_op jit(solution)/shard_map/ppermute | solution.py:16
  138.3 13.4 %collective-permute-start.30 = (bf16[128,1024]{1,0:T(8,128)(2,1)S(1)}, bf16[128,1024]{1,0:T(8,128)(2,1)S(1)}, u32[]{:S(2)}, u32[]{:S(2)}) collective-permute-start(bf16[128,1024]{1,0:T(8,128)(2,1)S(1)} %get-tuple-element.114), channel_id=1, source_target_pairs={{0,16},{16,0},{1,17},{17,1},{2,18},{18,2},{3,19},{19,3},{4,20},{20... | collective-permute-start | bytes 786440 | tf_op jit(solution)/shard_map/ppermute | solution.py:35
  155.6 16.0 %collective-permute-start.32 = (bf16[2,2,128,512]{3,2,1,0:T(8,128)(2,1)S(1)}, bf16[2,2,128,512]{3,2,1,0:T(8,128)(2,1)S(1)}, u32[]{:S(2)}, u32[]{:S(2)}) collective-permute-start(bf16[2,2,128,512]{3,2,1,0:T(8,128)(2,1)S(1)} %get-tuple-element.116.p0), channel_id=1, source_target_pairs={{0,4},{4,0},{8,12},{12,8},{1,5},{5,1},{9,13},{13,9},{2,6},{6,2},{1... | collective-permute-start | bytes 1572872 | tf_op jit(solution)/shard_map/ppermute | solution.py:39
  166.6 26.5 %collective-permute-start.49 = (bf16[128,1024]{1,0:T(8,128)(2,1)S(1)}, bf16[128,1024]{1,0:T(8,128)(2,1)S(1)}, u32[]{:S(2)}, u32[]{:S(2)}) collective-permute-start(bf16[128,1024]{1,0:T(8,128)(2,1)S(1)} %get-tuple-element.140), channel_id=1, source_target_pairs={{0,1},{1,2},{2,3},{3,0},{4,5},{5,6},{6,7},{7,4},{8,9},{9,10},{10,1... | collective-permute-start | bytes 786440 | tf_op jit(solution)/shard_map/ppermute | solution.py:16
  166.6 27.6 %collective-permute-start.50 = (bf16[128,1024]{1,0:T(8,128)(2,1)S(1)}, bf16[128,1024]{1,0:T(8,128)(2,1)S(1)}, u32[]{:S(2)}, u32[]{:S(2)}) collective-permute-start(bf16[128,1024]{1,0:T(8,128)(2,1)S(1)} %get-tuple-element.141), channel_id=1, source_target_pairs={{0,3},{1,0},{2,1},{3,2},{4,7},{5,4},{6,5},{7,6},{8,11},{9,8},{10,9... | collective-permute-start | bytes 786440 | tf_op jit(solution)/shard_map/ppermute | solution.py:16
  170.4 34.4 %collective-permute-start.39 = (bf16[4,128,1024]{2,1,0:T(8,128)(2,1)S(1)}, bf16[4,128,1024]{2,1,0:T(8,128)(2,1)S(1)}, u32[]{:S(2)}, u32[]{:S(2)}) collective-permute-start(bf16[4,128,1024]{2,1,0:T(8,128)(2,1)S(1)} %copy-done.12), channel_id=1, source_target_pairs={{0,16},{16,0},{1,17},{17,1},{2,18},{18,2},{3,19},{19,3},{4,20},{20... | collective-permute-start | bytes 3145736 | tf_op jit(solution)/shard_map/ppermute | solution.py:35
  175.3 13.1 %collective-permute-start.45 = (bf16[64,1024]{1,0:T(8,128)(2,1)S(1)}, bf16[64,1024]{1,0:T(8,128)(2,1)S(1)}, u32[]{:S(2)}, u32[]{:S(2)}) collective-permute-start(bf16[64,1024]{1,0:T(8,128)(2,1)S(1)} %get-tuple-element.159), channel_id=1, source_target_pairs={{0,1},{1,2},{2,3},{3,0},{4,5},{5,6},{6,7},{7,4},{8,9},{9,10},{10,1... | collective-permute-start | bytes 393224 | tf_op jit(solution)/shard_map/ppermute | solution.py:16
  188.6 14.9 %collective-permute-start.48 = (bf16[128,1024]{1,0:T(8,128)(2,1)S(1)}, bf16[128,1024]{1,0:T(8,128)(2,1)S(1)}, u32[]{:S(2)}, u32[]{:S(2)}) collective-permute-start(bf16[128,1024]{1,0:T(8,128)(2,1)S(1)} %get-tuple-element.136), channel_id=1, source_target_pairs={{0,3},{1,0},{2,1},{3,2},{4,7},{5,4},{6,5},{7,6},{8,11},{9,8},{10,9... | collective-permute-start | bytes 786440 | tf_op jit(solution)/shard_map/ppermute | solution.py:16
  193.1 37.6 %collective-permute-start.52 = (bf16[4,128,1024]{2,1,0:T(8,128)(2,1)S(1)}, bf16[4,128,1024]{2,1,0:T(8,128)(2,1)}, u32[]{:S(2)}, u32[]{:S(2)}) collective-permute-start(bf16[4,128,1024]{2,1,0:T(8,128)(2,1)S(1)} %get-tuple-element.121), channel_id=1, source_target_pairs={{0,16},{16,0},{1,17},{17,1},{2,18},{18,2},{3,19},{19,3},{4,20},{20... | collective-permute-start | bytes 3145736 | tf_op jit(solution)/shard_map/ppermute | solution.py:35
  203.7 20.4 %collective-permute-start.51 = (bf16[128,1024]{1,0:T(8,128)(2,1)S(1)}, bf16[128,1024]{1,0:T(8,128)(2,1)S(1)}, u32[]{:S(2)}, u32[]{:S(2)}) collective-permute-start(bf16[128,1024]{1,0:T(8,128)(2,1)S(1)} %get-tuple-element.148), channel_id=1, source_target_pairs={{0,16},{16,0},{1,17},{17,1},{2,18},{18,2},{3,19},{19,3},{4,20},{20... | collective-permute-start | bytes 786440 | tf_op jit(solution)/shard_map/ppermute | solution.py:35
  (45 other events, 507.0 us)

commit v6 on v5

--- a/solution.py
+++ b/solution.py
@@ -73,6 +73,13 @@
         width = held.shape[-1]
         for k, part in enumerate((held.at[which], above.at[which], far[which], below.at[which])):
             whole[:, k * width : (k + 1) * width] = part[...]
+
+
+def join_whole(step, parts, whole):
+    @pl.when(step == 0)
+    def _():
+        for k, part in enumerate(parts):
+            whole[:, k * part.shape[1] : (k + 1) * part.shape[1]] = part[...]
 
 
 def join_slots(step, parts, whole):
@@ -126,12 +133,12 @@
 
 
 def first_part_kernel(
-    group, place, own, received, gain, top, w0, w1, w2, w3, w4, sent0, kept0, sent1, kept1,
+    group, place, own, received, gain, top, w0, w1, w2, w3, w4, w5, w6, w7, sent0, kept0, sent1, kept1,
     weights, outward, rows,
 ):
     step, b, which = step_place()
-    join_units(step, 0, (w0, w1, w2, w3, w4), weights)
-    join_units(step, 1, (w0, w1, w2, w3, w4), outward)
+    join_whole(step, (w0, w1, w2, w3), weights)
+    join_whole(step, (w4, w5, w6, w7), outward)
     load_set(place, (own, received), rows)
     wide = rows[...].astype(F32)
     normed = (wide * gain[group : group + 1, :]).astype(BF16)
@@ -173,11 +180,11 @@
 
 
 def first_back_kernel(
-    group, place, own, received, gain, top, p0, p1, w0, w1, w2, w3, w4, v0, v1, v2, v3, v4,
+    group, place, own, received, gain, top, p0, p1, w0, w1, w2, w3, v0, v1, v2, v3, v4,
     result0, result1, sent, kept, weights, outward, spread, rows, grads,
 ):
     step, b, which = step_place()
-    join_units(step, 0, (w0, w1, w2, w3, w4), weights)
+    join_whole(step, (w0, w1, w2, w3), weights)
     join_units(step, 1, (v0, v1, v2, v3, v4), outward)
     join_slots(step, (p0, p1), spread)
     load_top(0, place, top, grads)
@@ -199,55 +206,58 @@
     put_result(place, result, (result0, result1))
 
 
-def add_grad(step, total, units, rows):
-    part = lax.dot_general(units, rows, (((0,), (0,)), ((), ())), preferred_element_type=F32)
-
-    @pl.when(step == 0)
+def flip_slots(parts, flipped):
+    @pl.when(pl.program_id(0) == 0)
     def _():
-        total[...] = part
-
-    @pl.when(step > 0)
-    def _():
-        total[...] += part
-
-
-def put_grad(step, total, kept, parts):
-    @pl.when(step == STEPS - 1)
-    def _():
-        height = kept.shape[0]
-        kept[...] = total[:height]
-        for k, part in enumerate(parts):
-            part[...] = total[(k + 1) * height : (k + 2) * height].astype(BF16)
+        units = flipped.shape[0]
+        for k in range(8):
+            block = parts[k // 4][k // 2 % 2, k % 2]
+            tokens = block.shape[0]
+            flipped[:, k * tokens : (k + 1) * tokens] = block[:, :units].T
+
+
+def fill_rows(place, load, rows):
+    for k in range(8):
+        block = load(k // 2 % 2, slot_at(place, k % 2, k // 4))
+        tokens = block.shape[0]
+        rows[k * tokens : (k + 1) * tokens] = block
+
+
+def put_grad(flipped, rows, kept, parts):
+    value = jnp.dot(flipped[...], rows[...], preferred_element_type=F32)
+    height = kept.shape[0]
+    kept[...] = value[:height]
+    for k, part in enumerate(parts):
+        part[...] = value[(k + 1) * height : (k + 2) * height].astype(BF16)
 
 
 def in_grad_kernel(
-    group, place, own, received, gain, p0, p1, kept, c1, c2, c3, total, spread, rows
+    group, place, own, received, gain, p0, p1, kept, c1, c2, c3, flipped, rows
 ):
-    step, b, which = step_place()
-    join_slots(step, (p0, p1), spread)
-    load_set(place, (own, received), rows)
-    normed = (rows[...].astype(F32) * gain[group : group + 1, :]).astype(BF16)
-    packed = spread[b, which].reshape(rows.shape[0], spread.shape[-1])
-    add_grad(step, total, packed[:, : total.shape[0]], normed)
-    put_grad(step, total, kept, (c1, c2, c3))
-
-
-def top_grad_kernel(place, top, p0, p1, kept, c1, c2, c3, total, spread, rows):
-    step, b, which = step_place()
-    join_slots(step, (p0, p1), spread)
-    load_top(0, place, top, rows)
-    packed = spread[b, which].reshape(rows.shape[0], spread.shape[-1])
-    add_grad(step, total, packed, rows[...])
-    put_grad(step, total, kept, (c1, c2, c3))
-
-
-def out_grad_kernel(place, in0, in1, p0, p1, kept, c1, c2, c3, total, spread, rows):
-    step, b, which = step_place()
-    join_slots(step, (p0, p1), spread)
-    load_set(place, (in0, in1), rows)
-    packed = spread[b, which].reshape(rows.shape[0], spread.shape[-1])
-    add_grad(step, total, packed, rows[...])
-    put_grad(step, total, kept, (c1, c2, c3))
+    def load(which, slot):
+        block = (own, received)[which][slot].astype(F32)
+        return (block * gain[group : group + 1, :]).astype(BF16)
+
+    flip_slots((p0, p1), flipped)
+    fill_rows(place, load, rows)
+    put_grad(flipped, rows, kept, (c1, c2, c3))
+
+
+def top_grad_kernel(place, top, p0, p1, kept, c1, c2, c3, flipped, rows):
+    half = top.shape[0] // 2
+
+    def load(which, slot):
+        return top[place[PLAN + half * (place[OWN] ^ which) + slot]]
+
+    flip_slots((p0, p1), flipped)
+    fill_rows(place, load, rows)
+    put_grad(flipped, rows, kept, (c1, c2, c3))
+
+
+def out_grad_kernel(place, in0, in1, p0, p1, kept, c1, c2, c3, flipped, rows):
+    flip_slots((p0, p1), flipped)
+    fill_rows(place, lambda which, slot: (in0, in1)[which][slot], rows)
+    put_grad(flipped, rows, kept, (c1, c2, c3))
 
 
 def core_sum_kernel(count, *refs):
@@ -326,7 +336,7 @@
     put_riders(four, rider, parts)
 
 
-def call(kernel, name, outs, args, scratch=(), specs=None, place=None, flops=0):
+def call(kernel, name, outs, args, scratch=(), specs=None, place=None, flops=0, out_spec=None):
     size = sum(a.size * a.dtype.itemsize for a in args)
     size += sum(o.size * o.dtype.itemsize for o in outs)
     cost = pl.CostEstimate(flops=flops, bytes_accessed=size, transcendentals=0)
@@ -347,7 +357,7 @@
             num_scalar_prefetch=1,
             grid=(STEPS,),
             in_specs=[specs.get(k, whole(a.shape)) for k, a in enumerate(args)],
-            out_specs=[whole(o.shape) for o in outs],
+            out_specs=[out_spec or whole(o.shape) for o in outs],
             scratch_shapes=[pltpu.VMEM(shape, dtype) for shape, dtype in scratch],
         ),
         compiler_params=params,
@@ -401,28 +411,30 @@
     def rows(array, section):
         return lax.dynamic_slice_in_dim(array, section * part, part, 0)
 
-    mine = jnp.stack((rows(weight_in[0], own), rows(weight_out[0], own)))
-    moved = swap_section(jnp.stack((rows(weight_in[0], other), rows(weight_out[0], other))))
+    mine = (rows(weight_in[0], own), rows(weight_out[0], own))
+    moved_in = swap_section(rows(weight_in[0], other))
+    moved_out = swap_section(rows(weight_out[0], other))
+    moved = (moved_in, moved_out)
 
     def sent_inputs(phase):
         first = half * place[OWN + phase]
         return lax.dynamic_slice(stored, (first, 0, other * part), (half, tokens, part))
 
-    received = swap_section(after(jnp.stack((sent_inputs(0), sent_inputs(1))), moved))
 
     def near(block):
         return rotate(block, 1), rotate(block, -1)
 
-    def far(below, above):
-        return rotate(below[0], 1), rotate(above[1], -1)
-
-    held0 = jnp.where(own == 1, mine, moved)
-    held1 = jnp.where(own == 0, mine, moved)
-    below, above = near(held0)
-    weights0 = (held0, above, below) + far(below, above)
-    below, above = near(after(held1, below, above))
-    weights1 = (held1, above, below) + far(below, above)
-    units = 4 * mine.shape[-1]
+    held0 = [jnp.where(own == 1, a, b) for a, b in zip(mine, moved)]
+    held1 = jnp.where(own == 0, jnp.stack(mine), jnp.stack(moved))
+    below_in, above_in = near(held0[0])
+    below_out, above_out = near(held0[1])
+    far_in, far_out = rotate(below_in, 1), rotate(above_out, -1)
+    weights0 = (held0[0], above_in, far_in, below_in, held0[1], above_out, far_out, below_out)
+    received = [swap_section(after(sent_inputs(0), moved_out)), None]
+    received[1] = swap_section(after(sent_inputs(1), below_out))
+    below, above = near(after(held1, below_out, above_out))
+    weights1 = (held1, above, below, rotate(below[0], 1), rotate(above[1], -1))
+    units = 4 * mine[0].shape[-1]
     rows2 = 2 * tokens
     gain_spec = pl.BlockSpec((2, part), lambda i, s: (0, s[SECTION]))
     top_spec = pl.BlockSpec((slots, tokens, part), lambda i, s: (0, 0, s[SECTION]))
@@ -432,15 +444,22 @@
     weight_scratch = ((part, units), BF16)
     rows_scratch = ((rows2, part), BF16)
     spread_scratch = ((2, 2, 2, tokens, units + PAD), BF16)
-    act_scratch = ((2, 2, 2, tokens, units), BF16)
-    grad_scratch = ((units, part), F32)
     grad_shapes = [shape_of((units // 4, part), F32)] + [shape_of((units // 4, part))] * 3
     four_shape = shape_of((2, 2, tokens, units))
     one_dot = 2 * slots * tokens * part * units
 
 
-    def received_spec(phase):
-        return pl.BlockSpec((None, half, tokens, part), lambda i, s: (phase, 0, 0, 0))
+    tile = part // STEPS
+    tile_top = pl.BlockSpec((slots, tokens, tile), lambda i, s: (0, 0, STEPS * s[SECTION] + i))
+    tile_gain = pl.BlockSpec((2, tile), lambda i, s: (0, STEPS * s[SECTION] + i))
+    tile_set = pl.BlockSpec((half, tokens, tile), lambda i, s: (0, 0, i))
+    tile_grad = pl.BlockSpec((units // 4, tile), lambda i, s: (0, i))
+    grad_scratch = [((units, slots * tokens), BF16), ((slots * tokens, tile), BF16)]
+
+    def tile_own(phase):
+        return pl.BlockSpec(
+            (half, tokens, tile), lambda i, s: (s[OWN + phase], 0, STEPS * s[SECTION] + i)
+        )
 
     def own_spec(phase):
         return pl.BlockSpec(
@@ -474,13 +493,13 @@
         bind(first_part_kernel, 1),
         "first_part",
         hidden_shapes + partial_shapes,
-        (stored, received, gain, cotangent) + weights0,
+        (stored, received[0], gain, cotangent) + weights0,
         [weight_scratch, weight_scratch, rows_scratch],
-        {0: own_spec(0), 1: received_spec(0), 2: gain_spec, 3: top_spec},
+        {0: own_spec(0), 2: gain_spec, 3: top_spec},
         place,
         2 * one_dot,
     )
-    own_sum, *parts = core_sum((sent, sent1), (kept, kept1))
+    own_sum, *parts = core_sum((sent, sent1), (after(kept, received[1]), kept1))
     scaled0, act0 = call(
         bind(first_unit_kernel, features),
         "first_units",
@@ -493,9 +512,9 @@
         bind(hidden_kernel, 0),
         "hidden_part",
         hidden_shapes,
-        (stored, received, gain) + weights1,
+        (stored, received[1], gain) + weights1,
         [weight_scratch, rows_scratch],
-        {0: own_spec(1), 1: received_spec(1), 2: gain_spec},
+        {0: own_spec(1), 2: gain_spec},
         place,
         one_dot,
     )
@@ -504,20 +523,21 @@
         bind(in_grad_kernel, 1),
         "in_grad",
         grad_shapes,
-        (stored, received, after(gain, own_sum)) + scaled0,
-        [grad_scratch, spread_scratch, rows_scratch],
-        {0: own_spec(0), 1: received_spec(0), 2: gain_spec},
+        (stored, received[0], after(gain, own_sum)) + scaled0,
+        grad_scratch,
+        {0: tile_own(0), 1: tile_set, 2: tile_gain},
         place,
         one_dot,
+        tile_grad,
     )
     in_hop0 = first_hop(in_grads0)
     result0, result1, sent, kept = call(
         bind(first_back_kernel, 1),
         "first_back",
         [set_shape, set_shape] + partial_shapes,
-        (stored, received, after(gain, in_grads0[0]), cotangent) + scaled0 + weights0 + weights1,
+        (stored, received[0], after(gain, in_grads0[0]), cotangent) + scaled0 + weights0[:4] + weights1,
         [weight_scratch, weight_scratch, spread_scratch, rows_scratch, rows_scratch],
-        {0: own_spec(0), 1: received_spec(0), 2: gain_spec, 3: top_spec},
+        {0: own_spec(0), 2: gain_spec, 3: top_spec},
         place,
         2 * one_dot,
     )
@@ -534,10 +554,11 @@
         "top_grad",
         grad_shapes,
         (cotangent, after(act0, own_sum), swap_core(act0)),
-        [grad_scratch, act_scratch, rows_scratch],
-        {0: top_spec},
+        grad_scratch,
+        {0: tile_top},
         place,
         one_dot,
+        tile_grad,
     )
     out_hop0 = first_hop(out_grads0)
     scaled1, act1 = call(
@@ -553,10 +574,11 @@
         "out_grad",
         grad_shapes,
         (result1, result0, act1, swap_core(act1)),
-        [grad_scratch, act_scratch, rows_scratch],
-        None,
+        grad_scratch,
+        {0: tile_set, 1: tile_set},
         place,
         one_dot,
+        tile_grad,
     )
     out_hop1 = first_hop(out_grads1)
     returned0 = swap_section(after(result1, scaled1[0]))
@@ -564,9 +586,9 @@
         bind(last_back_kernel, 0),
         "last_back",
         [set_shape, set_shape],
-        (stored, received, gain, result1, result0) + scaled1 + weights1,
+        (stored, received[1], gain, result1, result0) + scaled1 + weights1,
         [weight_scratch, spread_scratch, rows_scratch, rows_scratch],
-        {0: own_spec(1), 1: received_spec(1), 2: gain_spec},
+        {0: own_spec(1), 2: gain_spec},
         place,
         one_dot,
     )
@@ -575,11 +597,12 @@
         bind(in_grad_kernel, 0),
         "in_grad",
         grad_shapes,
-        (stored, received, after(gain, out_grads1[0], result3)) + scaled1,
-        [grad_scratch, spread_scratch, rows_scratch],
-        {0: own_spec(1), 1: received_spec(1), 2: gain_spec},
+        (stored, received[1], after(gain, out_grads1[0], result3)) + scaled1,
+        grad_scratch,
+        {0: tile_own(1), 1: tile_set, 2: tile_gain},
         place,
         one_dot,
+        tile_grad,
     )
     in_hop1 = first_hop(in_grads1)
     in_totals1 = second_hop(in_grads1, in_hop1, returned0)
@@ -595,7 +618,7 @@
     def whole(total0, total1):
         kept = jnp.where(own == 1, total0, total1)
         given = jnp.where(own == 1, total1, total0).astype(BF16)
-        back = swap_section(given).astype(F32)
+        back = after(swap_section(given), returned1).astype(F32)
         return jnp.where(
             own == 1,
             jnp.concatenate((back, kept), 1),

time: 233 us -> 220 us (0.944)
  waiting for transfers between devices: 95.9 us -> 82.7 us
  starting transfers between devices: 69.2 us -> 74.7 us
  local copies, waits for them, and re-layouts: 16.6 us -> 13.6 us
  Pallas kernels: 46.2 us -> 43.8 us
    ppermute x24 -> x26, waiting for transfers between devices: 70.5 us -> 61.6 us  [rotate(): lax.ppermute(block, 'dp', [(i, (i + shift) % count) for i in range(count)])]
    ppermute x11 -> x13, waiting for transfers between devices: 20.5 us -> 15.9 us  [swap_section(): return lax.ppermute(block, 'section', [(0, 1), (1, 0)])]
    ppermute x24 -> x26, starting transfers between devices: 40.2 us -> 43.4 us  [rotate(): lax.ppermute(block, 'dp', [(i, (i + shift) % count) for i in range(count)])]
    ppermute x11 -> x13, starting transfers between devices: 15.9 us -> 18.9 us  [swap_section(): return lax.ppermute(block, 'section', [(0, 1), (1, 0)])]
    pallas_call x8, Pallas kernels: 44.5 us -> 42.1 us  [call(): pl.pallas_call(kernel, out_shape=outs, grid_spec=pltpu.PrefetchScalarGrid...]
    unnamed x34 -> x32, local copies, waits for them, and re-layouts: 8.14 us -> 6.44 us
  transfers between devices with their start and end apart: 53 -> 57, of which waited for: 24 -> 29; matrix products, arithmetic and copies ran while one was open for 5% -> 5% of each run, Pallas kernels for 20% -> 20%
where the time goes in v6:
time: 220 us
  waiting for transfers between devices  82.7 us (38%)
  starting transfers between devices  74.7 us (34%)
  Pallas kernels  43.8 us (20%)
  local copies, waits for them, and re-layouts  13.6 us (6%)
  other arithmetic  3.9 us (2%)
    ppermute x26, waiting for transfers between devices, rotate(): lax.ppermute(block, 'dp', [(i, (i + shift) % count) for i in range(count)])  61.6 us
    ppermute x26, starting transfers between devices, rotate(): lax.ppermute(block, 'dp', [(i, (i + shift) % count) for i in range(count)])  43.4 us
    pallas_call x8, Pallas kernels, call(): pl.pallas_call(kernel, out_shape=outs, grid_spec=pltpu.PrefetchScalarGrid...  42.1 us
    ppermute x13, starting transfers between devices, swap_section(): return lax.ppermute(block, 'section', [(0, 1), (1, 0)])  18.9 us
    ppermute x13, waiting for transfers between devices, swap_section(): return lax.ppermute(block, 'section', [(0, 1), (1, 0)])  15.9 us
    ppermute x5, starting transfers between devices, swap_chip(): return lax.ppermute(block, 'mp', [(i, i ^ 2) for i in range(4)])  6.7 us
    unnamed x32, local copies, waits for them, and re-layouts  6.44 us
  transfers between devices with their start and end apart: 57, of which 29 were waited for; matrix products, arithmetic and copies ran while one was open for 5% of the time, Pallas kernels for 20%

profile of v6, /device:TPU:0, one launch (start us, length us, event | category | flops | bytes accessed | tf_op | source)
XLA Modules:
  0.0 219.8 jit_solution(6712903636404246810)
XLA Ops:
  14.0 3.6 %collective-permute-done.4 = bf16[1024,128]{1,0:T(8,128)(2,1)S(1)} collective-permute-done((bf16[1024,128]{1,0:T(8,128)(2,1)S(1)}, bf16[1024,128]{1,0:T(8,128)(2,1)S(1)}, u32[]{:S(2)}, u32[]{:S(2)}) %collective-permute-start.4) | collective-permute-done | bytes 262176 | tf_op jit(solution)/shard_map/ppermute | solution.py:35
  23.3 3.8 %collective-permute-start.11 = (bf16[1024,128]{1,0:T(8,128)(2,1)S(1)}, bf16[1024,128]{1,0:T(8,128)(2,1)S(1)}, u32[]{:S(2)}, u32[]{:S(2)}) collective-permute-start(bf16[1024,128]{1,0:T(8,128)(2,1)S(1)} %get-tuple-element.154.refs_5_.refs_7_), channel_id=1, source_target_pairs={{0,3},{1,0},{2,1},{3,2},{4,7},{5,4},{6,5},{7,6},{8,11},{9,8},{10,9... | collective-permute-start | bytes 786440 | tf_op jit(solution)/shard_map/ppermute | solution.py:16
  29.7 3.9 %collective-permute-start.13 = (bf16[1024,128]{1,0:T(8,128)(2,1)S(1)}, bf16[1024,128]{1,0:T(8,128)(2,1)S(1)}, u32[]{:S(2)}, u32[]{:S(2)}) collective-permute-start(bf16[1024,128]{1,0:T(8,128)(2,1)S(1)} %collective-permute-done.12.refs_8_.refs_10_), channel_id=1, source_target_pairs={{0,1},{1,2},{2,3},{3,0},{4,5},{5,6},{6,7},{7,4},{8,9},{9,10},{10,1... | collective-permute-start | bytes 786440 | tf_op jit(solution)/shard_map/ppermute | solution.py:16
  52.2 5.7 %collective-permute-done.14.refs_11_ = bf16[1024,128]{1,0:T(8,128)(2,1)} collective-permute-done((bf16[1024,128]{1,0:T(8,128)(2,1)}, bf16[1024,128]{1,0:T(8,128)(2,1)}, u32[]{:S(2)}, u32[]{:S(2)}) %collective-permute-start.14) | collective-permute-done | bytes 262176 | tf_op jit(solution)/shard_map/ppermute | solution.py:16
  59.0 6.9 %first_part.1 = (bf16[2,2,128,640]{3,2,1,0:T(8,128)(2,1)S(1)}, bf16[2,2,128,640]{3,2,1,0:T(8,128)(2,1)S(1)}, bf16[2,2,128,512]{3,2,1,0:T(8,128)(2,1)S(1)}, bf16[2,2,128,512]{3,2,1,0:T(8,128)(2,1)S(1)}) custom-call(s32[13]{0:T(128)S(1)} %concatenate.15.refs_0_.place, bf16[8,128,2048]{2,1,0:T(8,128)(2,1)} %bitcast.57, ...), custom_call_target="tpu_custom_call" | custom-call | flops 2147483648 | bytes 13910016 | tf_op jit(solution)/shard_map/first_part/pallas_call | solution.py:353
  72.7 8.6 %collective-permute-done.6.refs_5_.refs_12_.refs_9_ = bf16[2,1024,128]{2,1,0:T(8,128)(2,1)S(1)} collective-permute-done((bf16[2,1024,128]{2,1,0:T(8,128)(2,1)S(1)}, bf16[2,1024,128]{2,1,0:T(8,128)(2,1)S(1)}, u32[]{:S(2)}, u32[]{:S(2)}) %collective-permute-start.6) | collective-permute-done | bytes 524320 | tf_op jit(solution)/shard_map/ppermute | solution.py:16
  81.3 3.7 %collective-permute-start.9 = (bf16[1024,128]{1,0:T(8,128)(2,1)S(1)}, bf16[1024,128]{1,0:T(8,128)(2,1)S(1)}, u32[]{:S(2)}, u32[]{:S(2)}) collective-permute-start(bf16[1024,128]{1,0:T(8,128)(2,1)S(1)} %slice_bitcast_fusion), channel_id=1, source_target_pairs={{0,3},{1,0},{2,1},{3,2},{4,7},{5,4},{6,5},{7,6},{8,11},{9,8},{10,9... | collective-permute-start | bytes 786440 | tf_op jit(solution)/shard_map/ppermute | solution.py:16
  91.7 4.1 %hidden_part.1 = (bf16[2,2,128,640]{3,2,1,0:T(8,128)(2,1)S(1)}, bf16[2,2,128,640]{3,2,1,0:T(8,128)(2,1)S(1)}) custom-call(s32[13]{0:T(128)S(1)} %concatenate.15.refs_0_.place, bf16[8,128,2048]{2,1,0:T(8,128)(2,1)} %bitcast.58, bf16[4,128,1024]{2,1,0:T(8,128)(2,1)S(1)} %collective-permute-done.2.refs_2_, f32[2,2048]{1,0:T(2,128)S(1)} %copy-done.6, ...), custom_call_target="tpu_custom_call" | custom-call | flops 1073741824 | bytes 8667136 | tf_op jit(solution)/shard_map/hidden_part/pallas_call | solution.py:353
  101.7 4.4 %in_grad.2 = (f32[128,1024]{1,0:T(8,128)S(1)}, bf16[128,1024]{1,0:T(8,128)(2,1)S(1)}, bf16[128,1024]{1,0:T(8,128)(2,1)S(1)}, bf16[128,1024]{1,0:T(8,128)(2,1)S(1)}) custom-call(s32[13]{0:T(128)S(1)} %concatenate.15.refs_0_.place, bf16[8,128,2048]{2,1,0:T(8,128)(2,1)} %bitcast.59, bf16[4,128,1024]{2,1,0:T(8,128)(2,1)S(1)} %collective-permute-done.3.refs_2_, ...), custom_call_target="tpu_custom_call" | custom-call | flops 1073741824 | bytes 7880704 | tf_op jit(solution)/shard_map/in_grad/pallas_call | solution.py:353
  106.1 3.6 %collective-permute-start.28 = (bf16[64,1024]{1,0:T(8,128)(2,1)S(1)}, bf16[64,1024]{1,0:T(8,128)(2,1)S(1)}, u32[]{:S(2)}, u32[]{:S(2)}) collective-permute-start(bf16[64,1024]{1,0:T(8,128)(2,1)S(1)} %get-tuple-element.170), channel_id=1, source_target_pairs={{0,3},{1,0},{2,1},{3,2},{4,7},{5,4},{6,5},{7,6},{8,11},{9,8},{10,9... | collective-permute-start | bytes 393224 | tf_op jit(solution)/shard_map/ppermute | solution.py:16
  109.8 9.0 %first_back.1 = (bf16[4,128,1024]{2,1,0:T(8,128)(2,1)}, bf16[4,128,1024]{2,1,0:T(8,128)(2,1)}, bf16[2,2,128,512]{3,2,1,0:T(8,128)(2,1)S(1)}, bf16[2,2,128,512]{3,2,1,0:T(8,128)(2,1)S(1)}) custom-call(s32[13]{0:T(128)S(1)} %concatenate.15.refs_0_.place, bf16[8,128,2048]{2,1,0:T(8,128)(2,1)} %bitcast.60, bf16[4,128,1024]{2,1,0:T(8,128)(2,1)} %copy-done, ...), custom_call_target="tpu_custom_call" | custom-call | flops 2147483648 | bytes 17055744 | tf_op jit(solution)/shard_map/first_back/pallas_call | solution.py:353
  121.0 3.9 %collective-permute-start.32 = (bf16[128,1024]{1,0:T(8,128)(2,1)S(1)}, bf16[128,1024]{1,0:T(8,128)(2,1)S(1)}, u32[]{:S(2)}, u32[]{:S(2)}) collective-permute-start(bf16[128,1024]{1,0:T(8,128)(2,1)S(1)} %get-tuple-element.117), channel_id=1, source_target_pairs={{0,3},{1,0},{2,1},{3,2},{4,7},{5,4},{6,5},{7,6},{8,11},{9,8},{10,9... | collective-permute-start | bytes 786440 | tf_op jit(solution)/shard_map/ppermute | solution.py:16
  128.4 4.5 %top_grad.1 = (f32[128,1024]{1,0:T(8,128)S(1)}, bf16[128,1024]{1,0:T(8,128)(2,1)S(1)}, bf16[128,1024]{1,0:T(8,128)(2,1)S(1)}, bf16[128,1024]{1,0:T(8,128)(2,1)S(1)}) custom-call(s32[13]{0:T(128)S(1)} %concatenate.15.refs_0_.place, bf16[8,128,2048]{2,1,0:T(8,128)(2,1)} %top.1, bf16[2,2,128,512]{3,2,1,0:T(8,128)(2,1)S(1)} %get-tuple-element.111.p0, ...), custom_call_target="tpu_custom_call" | custom-call | flops 1073741824 | bytes 6553600 | tf_op jit(solution)/shard_map/top_grad/pallas_call | solution.py:353
  135.0 4.8 %collective-permute-done.34.refs_3_ = bf16[128,1024]{1,0:T(8,128)(2,1)S(1)} collective-permute-done((bf16[128,1024]{1,0:T(8,128)(2,1)S(1)}, bf16[128,1024]{1,0:T(8,128)(2,1)S(1)}, u32[]{:S(2)}, u32[]{:S(2)}) %collective-permute-start.34) | collective-permute-done | bytes 262176 | tf_op jit(solution)/shard_map/ppermute | solution.py:35
  149.7 4.9 %collective-permute-done.40.hop0 = bf16[64,1024]{1,0:T(8,128)(2,1)S(1)} collective-permute-done((bf16[64,1024]{1,0:T(8,128)(2,1)S(1)}, bf16[64,1024]{1,0:T(8,128)(2,1)S(1)}, u32[]{:S(2)}, u32[]{:S(2)}) %collective-permute-start.40) | collective-permute-done | bytes 131104 | tf_op jit(solution)/shard_map/ppermute | solution.py:16
  154.7 3.8 %collective-permute-start.55 = (bf16[128,1024]{1,0:T(8,128)(2,1)S(1)}, bf16[128,1024]{1,0:T(8,128)(2,1)S(1)}, u32[]{:S(2)}, u32[]{:S(2)}) collective-permute-start(bf16[128,1024]{1,0:T(8,128)(2,1)S(1)} %get-tuple-element.148), channel_id=1, source_target_pairs={{0,3},{1,0},{2,1},{3,2},{4,7},{5,4},{6,5},{7,6},{8,11},{9,8},{10,9... | collective-permute-start | bytes 786440 | tf_op jit(solution)/shard_map/ppermute | solution.py:16
  165.0 5.7 %last_back.1 = (bf16[4,128,1024]{2,1,0:T(8,128)(2,1)S(1)}, bf16[4,128,1024]{2,1,0:T(8,128)(2,1)S(1)}) custom-call(s32[13]{0:T(128)S(1)} %concatenate.15.refs_0_.place, bf16[8,128,2048]{2,1,0:T(8,128)(2,1)} %bitcast.61, bf16[4,128,1024]{2,1,0:T(8,128)(2,1)} %copy-done.1, f32[2,2048]{1,0:T(2,128)S(1)} %copy-done.6, ...), custom_call_target="tpu_custom_call" | custom-call | flops 1073741824 | bytes 12861440 | tf_op jit(solution)/shard_map/last_back/pallas_call | solution.py:353
  170.7 4.4 %in_grad.3 = (f32[128,1024]{1,0:T(8,128)S(1)}, bf16[128,1024]{1,0:T(8,128)(2,1)S(1)}, bf16[128,1024]{1,0:T(8,128)(2,1)S(1)}, bf16[128,1024]{1,0:T(8,128)(2,1)S(1)}) custom-call(s32[13]{0:T(128)S(1)} %concatenate.15.refs_0_.place, bf16[8,128,2048]{2,1,0:T(8,128)(2,1)} %bitcast.62, bf16[4,128,1024]{2,1,0:T(8,128)(2,1)S(1)} %copy-done.2, ...), custom_call_target="tpu_custom_call" | custom-call | flops 1073741824 | bytes 7880704 | tf_op jit(solution)/shard_map/in_grad/pallas_call | solution.py:353
  176.7 3.8 %collective-permute-start.53 = (bf16[128,1024]{1,0:T(8,128)(2,1)S(1)}, bf16[128,1024]{1,0:T(8,128)(2,1)S(1)}, u32[]{:S(2)}, u32[]{:S(2)}) collective-permute-start(bf16[128,1024]{1,0:T(8,128)(2,1)S(1)} %get-tuple-element.143), channel_id=1, source_target_pairs={{0,3},{1,0},{2,1},{3,2},{4,7},{5,4},{6,5},{7,6},{8,11},{9,8},{10,9... | collective-permute-start | bytes 786440 | tf_op jit(solution)/shard_map/ppermute | solution.py:16
  182.4 5.3 %collective-permute-done.52 = bf16[128,1024]{1,0:T(8,128)(2,1)S(1)} collective-permute-done((bf16[128,1024]{1,0:T(8,128)(2,1)S(1)}, bf16[128,1024]{1,0:T(8,128)(2,1)S(1)}, u32[]{:S(2)}, u32[]{:S(2)}) %collective-permute-start.52) | collective-permute-done | bytes 262176 | tf_op jit(solution)/shard_map/ppermute | solution.py:16
  187.7 3.9 %collective-permute-done.53 = bf16[128,1024]{1,0:T(8,128)(2,1)S(1)} collective-permute-done((bf16[128,1024]{1,0:T(8,128)(2,1)S(1)}, bf16[128,1024]{1,0:T(8,128)(2,1)S(1)}, u32[]{:S(2)}, u32[]{:S(2)}) %collective-permute-start.53) | collective-permute-done | bytes 262176 | tf_op jit(solution)/shard_map/ppermute | solution.py:16
  193.1 4.6 %collective-permute-done.44.hop0 = bf16[64,1024]{1,0:T(8,128)(2,1)S(1)} collective-permute-done((bf16[64,1024]{1,0:T(8,128)(2,1)S(1)}, bf16[64,1024]{1,0:T(8,128)(2,1)S(1)}, u32[]{:S(2)}, u32[]{:S(2)}) %collective-permute-start.44) | collective-permute-done | bytes 131104 | tf_op jit(solution)/shard_map/ppermute | solution.py:16
  197.8 3.8 %collective-permute-start.47 = (bf16[128,1024]{1,0:T(8,128)(2,1)S(1)}, bf16[128,1024]{1,0:T(8,128)(2,1)S(1)}, u32[]{:S(2)}, u32[]{:S(2)}) collective-permute-start(bf16[128,1024]{1,0:T(8,128)(2,1)S(1)} %get-tuple-element.136), channel_id=1, source_target_pairs={{0,3},{1,0},{2,1},{3,2},{4,7},{5,4},{6,5},{7,6},{8,11},{9,8},{10,9... | collective-permute-start | bytes 786440 | tf_op jit(solution)/shard_map/ppermute | solution.py:16
  201.7 7.1 %collective-permute-done.46 = bf16[128,1024]{1,0:T(8,128)(2,1)S(1)} collective-permute-done((bf16[128,1024]{1,0:T(8,128)(2,1)S(1)}, bf16[128,1024]{1,0:T(8,128)(2,1)S(1)}, u32[]{:S(2)}, u32[]{:S(2)}) %collective-permute-start.46) | collective-permute-done | bytes 262176 | tf_op jit(solution)/shard_map/ppermute | solution.py:16
  (166 shorter events, 100.9 us)
Async XLA Ops:
  11.9 46.0 %collective-permute-start.3 = (bf16[4,128,1024]{2,1,0:T(8,128)(2,1)}, bf16[4,128,1024]{2,1,0:T(8,128)(2,1)S(1)}, u32[]{:S(2)}, u32[]{:S(2)}) collective-permute-start(bf16[4,128,1024]{2,1,0:T(8,128)(2,1)} %get-tuple-element.78), channel_id=1, source_target_pairs={{0,16},{16,0},{1,17},{17,1},{2,18},{18,2},{3,19},{19,3},{4,20},{20... | collective-permute-start | bytes 3145736 | tf_op jit(solution)/shard_map/ppermute | solution.py:35
  21.2 15.0 %collective-permute-start.5 = (bf16[1024,128]{1,0:T(8,128)(2,1)S(1)}, bf16[1024,128]{1,0:T(8,128)(2,1)}, u32[]{:S(2)}, u32[]{:S(2)}) collective-permute-start(bf16[1024,128]{1,0:T(8,128)(2,1)S(1)} %get-tuple-element.156.refs_9_), channel_id=1, source_target_pairs={{0,3},{1,0},{2,1},{3,2},{4,7},{5,4},{6,5},{7,6},{8,11},{9,8},{10,9... | collective-permute-start | bytes 786440 | tf_op jit(solution)/shard_map/ppermute | solution.py:16
  23.3 17.7 %collective-permute-start.1 = (bf16[1024,128]{1,0:T(8,128)(2,1)S(1)}, bf16[1024,128]{1,0:T(8,128)(2,1)S(1)}, u32[]{:S(2)}, u32[]{:S(2)}) collective-permute-start(bf16[1024,128]{1,0:T(8,128)(2,1)S(1)} %get-tuple-element.156.refs_9_), channel_id=1, source_target_pairs={{0,1},{1,2},{2,3},{3,0},{4,5},{5,6},{6,7},{7,4},{8,9},{9,10},{10,1... | collective-permute-start | bytes 786440 | tf_op jit(solution)/shard_map/ppermute | solution.py:16
  23.3 24.1 %collective-permute-start.11 = (bf16[1024,128]{1,0:T(8,128)(2,1)S(1)}, bf16[1024,128]{1,0:T(8,128)(2,1)S(1)}, u32[]{:S(2)}, u32[]{:S(2)}) collective-permute-start(bf16[1024,128]{1,0:T(8,128)(2,1)S(1)} %get-tuple-element.154.refs_5_.refs_7_), channel_id=1, source_target_pairs={{0,3},{1,0},{2,1},{3,2},{4,7},{5,4},{6,5},{7,6},{8,11},{9,8},{10,9... | collective-permute-start | bytes 786440 | tf_op jit(solution)/shard_map/ppermute | solution.py:16
  29.7 22.5 %collective-permute-start.13 = (bf16[1024,128]{1,0:T(8,128)(2,1)S(1)}, bf16[1024,128]{1,0:T(8,128)(2,1)S(1)}, u32[]{:S(2)}, u32[]{:S(2)}) collective-permute-start(bf16[1024,128]{1,0:T(8,128)(2,1)S(1)} %collective-permute-done.12.refs_8_.refs_10_), channel_id=1, source_target_pairs={{0,1},{1,2},{2,3},{3,0},{4,5},{5,6},{6,7},{7,4},{8,9},{9,10},{10,1... | collective-permute-start | bytes 786440 | tf_op jit(solution)/shard_map/ppermute | solution.py:16
  36.2 21.6 %collective-permute-start.14 = (bf16[1024,128]{1,0:T(8,128)(2,1)}, bf16[1024,128]{1,0:T(8,128)(2,1)}, u32[]{:S(2)}, u32[]{:S(2)}) collective-permute-start(bf16[1024,128]{1,0:T(8,128)(2,1)} %collective-permute-done.5.refs_10_), channel_id=1, source_target_pairs={{0,3},{1,0},{2,1},{3,2},{4,7},{5,4},{6,5},{7,6},{8,11},{9,8},{10,9... | collective-permute-start | bytes 786440 | tf_op jit(solution)/shard_map/ppermute | solution.py:16
  41.7 26.9 %collective-permute-start.2 = (bf16[4,128,1024]{2,1,0:T(8,128)(2,1)}, bf16[4,128,1024]{2,1,0:T(8,128)(2,1)S(1)}, u32[]{:S(2)}, u32[]{:S(2)}) collective-permute-start(bf16[4,128,1024]{2,1,0:T(8,128)(2,1)} %get-tuple-element.77), channel_id=1, source_target_pairs={{0,16},{16,0},{1,17},{17,1},{2,18},{18,2},{3,19},{19,3},{4,20},{20... | collective-permute-start | bytes 3145736 | tf_op jit(solution)/shard_map/ppermute | solution.py:35
  47.4 20.9 %collective-permute-start.7 = (bf16[2,1024,128]{2,1,0:T(8,128)(2,1)S(1)}, bf16[2,1024,128]{2,1,0:T(8,128)(2,1)S(1)}, u32[]{:S(2)}, u32[]{:S(2)}) collective-permute-start(bf16[2,1024,128]{2,1,0:T(8,128)(2,1)S(1)} %maximum_select_fusion.2.refs_4_.refs_11_.refs_8_), channel_id=1, source_target_pairs={{0,1},{1,2},{2,3},{3,0},{4,5},{5,6},{6,7},{7,4},{8,9},{9,10},{10,1... | collective-permute-start | bytes 1572872 | tf_op jit(solution)/shard_map/ppermute | solution.py:16
  66.5 14.7 %collective-permute-start.6 = (bf16[2,1024,128]{2,1,0:T(8,128)(2,1)S(1)}, bf16[2,1024,128]{2,1,0:T(8,128)(2,1)S(1)}, u32[]{:S(2)}, u32[]{:S(2)}) collective-permute-start(bf16[2,1024,128]{2,1,0:T(8,128)(2,1)S(1)} %maximum_select_fusion.2.refs_4_.refs_11_.refs_8_), channel_id=1, source_target_pairs={{0,3},{1,0},{2,1},{3,2},{4,7},{5,4},{6,5},{7,6},{8,11},{9,8},{10,9... | collective-permute-start | bytes 1572872 | tf_op jit(solution)/shard_map/ppermute | solution.py:16
  68.3 21.6 %collective-permute-start.8 = (bf16[1024,128]{1,0:T(8,128)(2,1)S(1)}, bf16[1024,128]{1,0:T(8,128)(2,1)S(1)}, u32[]{:S(2)}, u32[]{:S(2)}) collective-permute-start(bf16[1024,128]{1,0:T(8,128)(2,1)S(1)} %slice_bitcast_fusion.1), channel_id=1, source_target_pairs={{0,1},{1,2},{2,3},{3,0},{4,5},{5,6},{6,7},{7,4},{8,9},{9,10},{10,1... | collective-permute-start | bytes 786440 | tf_op jit(solution)/shard_map/ppermute | solution.py:16
  69.1 15.9 %collective-permute-start.17 = (bf16[128,1152]{1,0:T(8,128)(2,1)S(1)}, bf16[128,1152]{1,0:T(8,128)(2,1)S(1)}, u32[]{:S(2)}, u32[]{:S(2)}) collective-permute-start(bf16[128,1152]{1,0:T(8,128)(2,1)S(1)} %get-tuple-element.88), channel_id=1, source_target_pairs={{0,8},{4,12},{8,0},{12,4},{1,9},{5,13},{9,1},{13,5},{2,10},{6,14},... | collective-permute-start | bytes 884744 | tf_op jit(solution)/shard_map/ppermute | solution.py:43
  70.9 15.1 %collective-permute-start.18 = (bf16[128,1152]{1,0:T(8,128)(2,1)S(1)}, bf16[128,1152]{1,0:T(8,128)(2,1)S(1)}, u32[]{:S(2)}, u32[]{:S(2)}) collective-permute-start(bf16[128,1152]{1,0:T(8,128)(2,1)S(1)} %get-tuple-element.89), channel_id=1, source_target_pairs={{0,16},{16,0},{1,17},{17,1},{2,18},{18,2},{3,19},{19,3},{4,20},{20... | collective-permute-start | bytes 884744 | tf_op jit(solution)/shard_map/ppermute | solution.py:35
  72.4 13.6 %collective-permute-start.19 = (bf16[128,1152]{1,0:T(8,128)(2,1)S(1)}, bf16[128,1152]{1,0:T(8,128)(2,1)S(1)}, u32[]{:S(2)}, u32[]{:S(2)}) collective-permute-start(bf16[128,1152]{1,0:T(8,128)(2,1)S(1)} %get-tuple-element.90), channel_id=1, source_target_pairs={{0,24},{4,28},{8,16},{12,20},{16,8},{20,12},{24,0},{28,4},{1,25},{... | collective-permute-start | bytes 884744 | tf_op jit(solution)/shard_map/ppermute | solution.py:47
  98.1 20.7 %collective-permute-start.24 = (bf16[128,1152]{1,0:T(8,128)(2,1)S(1)}, bf16[128,1152]{1,0:T(8,128)(2,1)S(1)}, u32[]{:S(2)}, u32[]{:S(2)}) collective-permute-start(bf16[128,1152]{1,0:T(8,128)(2,1)S(1)} %get-tuple-element.101), channel_id=1, source_target_pairs={{0,8},{4,12},{8,0},{12,4},{1,9},{5,13},{9,1},{13,5},{2,10},{6,14},... | collective-permute-start | bytes 884744 | tf_op jit(solution)/shard_map/ppermute | solution.py:43
  99.9 19.0 %collective-permute-start.25 = (bf16[128,1152]{1,0:T(8,128)(2,1)S(1)}, bf16[128,1152]{1,0:T(8,128)(2,1)S(1)}, u32[]{:S(2)}, u32[]{:S(2)}) collective-permute-start(bf16[128,1152]{1,0:T(8,128)(2,1)S(1)} %get-tuple-element.102), channel_id=1, source_target_pairs={{0,16},{16,0},{1,17},{17,1},{2,18},{18,2},{3,19},{19,3},{4,20},{20... | collective-permute-start | bytes 884744 | tf_op jit(solution)/shard_map/ppermute | solution.py:35
  101.4 17.4 %collective-permute-start.26 = (bf16[128,1152]{1,0:T(8,128)(2,1)S(1)}, bf16[128,1152]{1,0:T(8,128)(2,1)S(1)}, u32[]{:S(2)}, u32[]{:S(2)}) collective-permute-start(bf16[128,1152]{1,0:T(8,128)(2,1)S(1)} %get-tuple-element.103), channel_id=1, source_target_pairs={{0,24},{4,28},{8,16},{12,20},{16,8},{20,12},{24,0},{28,4},{1,25},{... | collective-permute-start | bytes 884744 | tf_op jit(solution)/shard_map/ppermute | solution.py:47
  121.0 14.0 %collective-permute-start.32 = (bf16[128,1024]{1,0:T(8,128)(2,1)S(1)}, bf16[128,1024]{1,0:T(8,128)(2,1)S(1)}, u32[]{:S(2)}, u32[]{:S(2)}) collective-permute-start(bf16[128,1024]{1,0:T(8,128)(2,1)S(1)} %get-tuple-element.117), channel_id=1, source_target_pairs={{0,3},{1,0},{2,1},{3,2},{4,7},{5,4},{6,5},{7,6},{8,11},{9,8},{10,9... | collective-permute-start | bytes 786440 | tf_op jit(solution)/shard_map/ppermute | solution.py:16
  143.7 16.0 %collective-permute-start.36 = (bf16[2,2,128,512]{3,2,1,0:T(8,128)(2,1)S(1)}, bf16[2,2,128,512]{3,2,1,0:T(8,128)(2,1)S(1)}, u32[]{:S(2)}, u32[]{:S(2)}) collective-permute-start(bf16[2,2,128,512]{3,2,1,0:T(8,128)(2,1)S(1)} %get-tuple-element.122.p0), channel_id=1, source_target_pairs={{0,4},{4,0},{8,12},{12,8},{1,5},{5,1},{9,13},{13,9},{2,6},{6,2},{1... | collective-permute-start | bytes 1572872 | tf_op jit(solution)/shard_map/ppermute | solution.py:39
  154.7 26.5 %collective-permute-start.54 = (bf16[128,1024]{1,0:T(8,128)(2,1)S(1)}, bf16[128,1024]{1,0:T(8,128)(2,1)S(1)}, u32[]{:S(2)}, u32[]{:S(2)}) collective-permute-start(bf16[128,1024]{1,0:T(8,128)(2,1)S(1)} %get-tuple-element.147), channel_id=1, source_target_pairs={{0,1},{1,2},{2,3},{3,0},{4,5},{5,6},{6,7},{7,4},{8,9},{9,10},{10,1... | collective-permute-start | bytes 786440 | tf_op jit(solution)/shard_map/ppermute | solution.py:16
  154.7 27.7 %collective-permute-start.55 = (bf16[128,1024]{1,0:T(8,128)(2,1)S(1)}, bf16[128,1024]{1,0:T(8,128)(2,1)S(1)}, u32[]{:S(2)}, u32[]{:S(2)}) collective-permute-start(bf16[128,1024]{1,0:T(8,128)(2,1)S(1)} %get-tuple-element.148), channel_id=1, source_target_pairs={{0,3},{1,0},{2,1},{3,2},{4,7},{5,4},{6,5},{7,6},{8,11},{9,8},{10,9... | collective-permute-start | bytes 786440 | tf_op jit(solution)/shard_map/ppermute | solution.py:16
  158.5 34.5 %collective-permute-start.43 = (bf16[4,128,1024]{2,1,0:T(8,128)(2,1)S(1)}, bf16[4,128,1024]{2,1,0:T(8,128)(2,1)S(1)}, u32[]{:S(2)}, u32[]{:S(2)}) collective-permute-start(bf16[4,128,1024]{2,1,0:T(8,128)(2,1)S(1)} %copy-done.5), channel_id=1, source_target_pairs={{0,16},{16,0},{1,17},{17,1},{2,18},{18,2},{3,19},{19,3},{4,20},{20... | collective-permute-start | bytes 3145736 | tf_op jit(solution)/shard_map/ppermute | solution.py:35
  176.7 14.9 %collective-permute-start.53 = (bf16[128,1024]{1,0:T(8,128)(2,1)S(1)}, bf16[128,1024]{1,0:T(8,128)(2,1)S(1)}, u32[]{:S(2)}, u32[]{:S(2)}) collective-permute-start(bf16[128,1024]{1,0:T(8,128)(2,1)S(1)} %get-tuple-element.143), channel_id=1, source_target_pairs={{0,3},{1,0},{2,1},{3,2},{4,7},{5,4},{6,5},{7,6},{8,11},{9,8},{10,9... | collective-permute-start | bytes 786440 | tf_op jit(solution)/shard_map/ppermute | solution.py:16
  181.2 31.0 %collective-permute-start.49 = (bf16[4,128,1024]{2,1,0:T(8,128)(2,1)S(1)}, bf16[4,128,1024]{2,1,0:T(8,128)(2,1)S(1)}, u32[]{:S(2)}, u32[]{:S(2)}) collective-permute-start(bf16[4,128,1024]{2,1,0:T(8,128)(2,1)S(1)} %get-tuple-element.127), channel_id=1, source_target_pairs={{0,16},{16,0},{1,17},{17,1},{2,18},{18,2},{3,19},{19,3},{4,20},{20... | collective-permute-start | bytes 3145736 | tf_op jit(solution)/shard_map/ppermute | solution.py:35
  191.8 20.4 %collective-permute-start.56 = (bf16[128,1024]{1,0:T(8,128)(2,1)S(1)}, bf16[128,1024]{1,0:T(8,128)(2,1)S(1)}, u32[]{:S(2)}, u32[]{:S(2)}) collective-permute-start(bf16[128,1024]{1,0:T(8,128)(2,1)S(1)} %get-tuple-element.160), channel_id=1, source_target_pairs={{0,16},{16,0},{1,17},{17,1},{2,18},{18,2},{3,19},{19,3},{4,20},{20... | collective-permute-start | bytes 786440 | tf_op jit(solution)/shard_map/ppermute | solution.py:35
  (48 other events, 595.7 us)

commit v7 on v6

--- a/solution.py
+++ b/solution.py
@@ -53,7 +53,7 @@
 
 CORE, CHIP, SECTION, OWN, PLAN = 0, 1, 2, 3, 5
 STEPS = 4
-VMEM_BYTES = 48 * 1024 * 1024
+VMEM_BYTES = 44 * 1024 * 1024
 
 
 def step_place():
@@ -604,7 +604,7 @@
         one_dot,
         tile_grad,
     )
-    in_hop1 = first_hop(in_grads1)
+    in_hop1 = first_hop(after(in_grads1, *out_totals0[1:]))
     in_totals1 = second_hop(in_grads1, in_hop1, returned0)
     out_totals1 = second_hop(out_grads1, out_hop1, in_grads1[0])
     in_total0, out_total0, out_total1 = total(in_totals0), total(out_totals0), total(out_totals1)

time: 220 us -> 220 us (level)
  Pallas kernels: 43.8 us -> 39 us
    pallas_call x8, Pallas kernels: 42.1 us -> 37.4 us  [call(): pl.pallas_call(kernel, out_shape=outs, grid_spec=pltpu.PrefetchScalarGrid...]
    unnamed x32 -> x28, local copies, waits for them, and re-layouts: 6.44 us -> 8.39 us
  transfers between devices with their start and end apart: 57 -> 57, of which waited for: 29 -> 30; matrix products, arithmetic and copies ran while one was open for 5% -> 5% of each run, Pallas kernels for 20% -> 18%
where the time goes in v7:
time: 220 us; the launch traced here: 219 us
  waiting for transfers between devices  84.4 us (38%)
  starting transfers between devices  74.2 us (34%)
  Pallas kernels  39 us (18%)
  local copies, waits for them, and re-layouts  15.5 us (7%)
  other arithmetic  4.87 us (2%)
    ppermute x26, waiting for transfers between devices, rotate(): lax.ppermute(block, 'dp', [(i, (i + shift) % count) for i in range(count)])  62.7 us
    ppermute x26, starting transfers between devices, rotate(): lax.ppermute(block, 'dp', [(i, (i + shift) % count) for i in range(count)])  43.5 us
    pallas_call x8, Pallas kernels, call(): pl.pallas_call(kernel, out_shape=outs, grid_spec=pltpu.PrefetchScalarGrid...  37.4 us
    ppermute x13, starting transfers between devices, swap_section(): return lax.ppermute(block, 'section', [(0, 1), (1, 0)])  18.8 us
    ppermute x13, waiting for transfers between devices, swap_section(): return lax.ppermute(block, 'section', [(0, 1), (1, 0)])  17.3 us
    unnamed x28, local copies, waits for them, and re-layouts  8.39 us
    ppermute x5, starting transfers between devices, swap_chip(): return lax.ppermute(block, 'mp', [(i, i ^ 2) for i in range(4)])  6.63 us
  transfers between devices with their start and end apart: 57, of which 30 were waited for; matrix products, arithmetic and copies ran while one was open for 5% of the time, Pallas kernels for 18%

profile of v7, /device:TPU:0, one launch (start us, length us, event | category | flops | bytes accessed | tf_op | source)
XLA Modules:
  0.0 219.1 jit_solution(4758612944370680643)
XLA Ops:
  14.0 3.6 %collective-permute-done.4 = bf16[1024,128]{1,0:T(8,128)(2,1)S(1)} collective-permute-done((bf16[1024,128]{1,0:T(8,128)(2,1)S(1)}, bf16[1024,128]{1,0:T(8,128)(2,1)S(1)}, u32[]{:S(2)}, u32[]{:S(2)}) %collective-permute-start.4) | collective-permute-done | bytes 262176 | tf_op jit(solution)/shard_map/ppermute | solution.py:35
  23.3 3.8 %collective-permute-start.11 = (bf16[1024,128]{1,0:T(8,128)(2,1)S(1)}, bf16[1024,128]{1,0:T(8,128)(2,1)S(1)}, u32[]{:S(2)}, u32[]{:S(2)}) collective-permute-start(bf16[1024,128]{1,0:T(8,128)(2,1)S(1)} %get-tuple-element.156.refs_5_.refs_7_), channel_id=1, source_target_pairs={{0,3},{1,0},{2,1},{3,2},{4,7},{5,4},{6,5},{7,6},{8,11},{9,8},{10,9... | collective-permute-start | bytes 786440 | tf_op jit(solution)/shard_map/ppermute | solution.py:16
  29.7 3.9 %collective-permute-start.13 = (bf16[1024,128]{1,0:T(8,128)(2,1)S(1)}, bf16[1024,128]{1,0:T(8,128)(2,1)S(1)}, u32[]{:S(2)}, u32[]{:S(2)}) collective-permute-start(bf16[1024,128]{1,0:T(8,128)(2,1)S(1)} %collective-permute-done.12.refs_8_.refs_10_), channel_id=1, source_target_pairs={{0,1},{1,2},{2,3},{3,0},{4,5},{5,6},{6,7},{7,4},{8,9},{9,10},{10,1... | collective-permute-start | bytes 786440 | tf_op jit(solution)/shard_map/ppermute | solution.py:16
  37.5 3.5 %collective-permute-done.1.refs_12_ = bf16[1024,128]{1,0:T(8,128)(2,1)S(1)} collective-permute-done((bf16[1024,128]{1,0:T(8,128)(2,1)S(1)}, bf16[1024,128]{1,0:T(8,128)(2,1)S(1)}, u32[]{:S(2)}, u32[]{:S(2)}) %collective-permute-start.1) | collective-permute-done | bytes 262176 | tf_op jit(solution)/shard_map/ppermute | solution.py:16
  52.2 5.7 %collective-permute-done.14.refs_11_ = bf16[1024,128]{1,0:T(8,128)(2,1)} collective-permute-done((bf16[1024,128]{1,0:T(8,128)(2,1)}, bf16[1024,128]{1,0:T(8,128)(2,1)}, u32[]{:S(2)}, u32[]{:S(2)}) %collective-permute-start.14) | collective-permute-done | bytes 262176 | tf_op jit(solution)/shard_map/ppermute | solution.py:16
  61.0 6.7 %first_part.1 = (bf16[2,2,128,640]{3,2,1,0:T(8,128)(2,1)S(1)}, bf16[2,2,128,640]{3,2,1,0:T(8,128)(2,1)S(1)}, bf16[2,2,128,512]{3,2,1,0:T(8,128)(2,1)S(1)}, bf16[2,2,128,512]{3,2,1,0:T(8,128)(2,1)S(1)}) custom-call(s32[13]{0:T(128)S(1)} %concatenate.15.refs_0_.place, bf16[8,128,2048]{2,1,0:T(8,128)(2,1)S(1)} %bitcast.51, ...), custom_call_target="tpu_custom_call" | custom-call | flops 2147483648 | bytes 13910016 | tf_op jit(solution)/shard_map/first_part/pallas_call | solution.py:353
  74.5 8.6 %collective-permute-done.6.refs_5_.refs_12_.refs_9_ = bf16[2,1024,128]{2,1,0:T(8,128)(2,1)S(1)} collective-permute-done((bf16[2,1024,128]{2,1,0:T(8,128)(2,1)S(1)}, bf16[2,1024,128]{2,1,0:T(8,128)(2,1)S(1)}, u32[]{:S(2)}, u32[]{:S(2)}) %collective-permute-start.6) | collective-permute-done | bytes 524320 | tf_op jit(solution)/shard_map/ppermute | solution.py:16
  83.1 3.7 %collective-permute-start.9 = (bf16[1024,128]{1,0:T(8,128)(2,1)S(1)}, bf16[1024,128]{1,0:T(8,128)(2,1)S(1)}, u32[]{:S(2)}, u32[]{:S(2)}) collective-permute-start(bf16[1024,128]{1,0:T(8,128)(2,1)S(1)} %slice_bitcast_fusion), channel_id=1, source_target_pairs={{0,3},{1,0},{2,1},{3,2},{4,7},{5,4},{6,5},{7,6},{8,11},{9,8},{10,9... | collective-permute-start | bytes 786440 | tf_op jit(solution)/shard_map/ppermute | solution.py:16
  102.4 3.3 %in_grad.2 = (f32[128,1024]{1,0:T(8,128)S(1)}, bf16[128,1024]{1,0:T(8,128)(2,1)S(1)}, bf16[128,1024]{1,0:T(8,128)(2,1)S(1)}, bf16[128,1024]{1,0:T(8,128)(2,1)S(1)}) custom-call(s32[13]{0:T(128)S(1)} %concatenate.15.refs_0_.place, bf16[8,128,2048]{2,1,0:T(8,128)(2,1)S(1)} %bitcast.53, bf16[4,128,1024]{2,1,0:T(8,128)(2,1)S(1)} %collective-permute-done.3.refs_2_, ...), custom_call_target="tpu_custom_call" | custom-call | flops 1073741824 | bytes 7880704 | tf_op jit(solution)/shard_map/in_grad/pallas_call | solution.py:353
  105.7 3.6 %collective-permute-start.28 = (bf16[64,1024]{1,0:T(8,128)(2,1)S(1)}, bf16[64,1024]{1,0:T(8,128)(2,1)S(1)}, u32[]{:S(2)}, u32[]{:S(2)}) collective-permute-start(bf16[64,1024]{1,0:T(8,128)(2,1)S(1)} %get-tuple-element.172), channel_id=1, source_target_pairs={{0,3},{1,0},{2,1},{3,2},{4,7},{5,4},{6,5},{7,6},{8,11},{9,8},{10,9... | collective-permute-start | bytes 393224 | tf_op jit(solution)/shard_map/ppermute | solution.py:16
  109.3 8.7 %first_back.1 = (bf16[4,128,1024]{2,1,0:T(8,128)(2,1)S(1)}, bf16[4,128,1024]{2,1,0:T(8,128)(2,1)}, bf16[2,2,128,512]{3,2,1,0:T(8,128)(2,1)S(1)}, bf16[2,2,128,512]{3,2,1,0:T(8,128)(2,1)S(1)}) custom-call(s32[13]{0:T(128)S(1)} %concatenate.15.refs_0_.place, bf16[8,128,2048]{2,1,0:T(8,128)(2,1)} %bitcast.49, ...), custom_call_target="tpu_custom_call" | custom-call | flops 2147483648 | bytes 17055744 | tf_op jit(solution)/shard_map/first_back/pallas_call | solution.py:353
  120.1 3.9 %collective-permute-start.32 = (bf16[128,1024]{1,0:T(8,128)(2,1)S(1)}, bf16[128,1024]{1,0:T(8,128)(2,1)S(1)}, u32[]{:S(2)}, u32[]{:S(2)}) collective-permute-start(bf16[128,1024]{1,0:T(8,128)(2,1)S(1)} %get-tuple-element.118), channel_id=1, source_target_pairs={{0,3},{1,0},{2,1},{3,2},{4,7},{5,4},{6,5},{7,6},{8,11},{9,8},{10,9... | collective-permute-start | bytes 786440 | tf_op jit(solution)/shard_map/ppermute | solution.py:16
  134.2 4.7 %collective-permute-done.34.refs_3_ = bf16[128,1024]{1,0:T(8,128)(2,1)S(1)} collective-permute-done((bf16[128,1024]{1,0:T(8,128)(2,1)S(1)}, bf16[128,1024]{1,0:T(8,128)(2,1)S(1)}, u32[]{:S(2)}, u32[]{:S(2)}) %collective-permute-start.34) | collective-permute-done | bytes 262176 | tf_op jit(solution)/shard_map/ppermute | solution.py:35
  148.8 4.9 %collective-permute-done.40.hop0 = bf16[64,1024]{1,0:T(8,128)(2,1)S(1)} collective-permute-done((bf16[64,1024]{1,0:T(8,128)(2,1)S(1)}, bf16[64,1024]{1,0:T(8,128)(2,1)S(1)}, u32[]{:S(2)}, u32[]{:S(2)}) %collective-permute-start.40) | collective-permute-done | bytes 131104 | tf_op jit(solution)/shard_map/ppermute | solution.py:16
  153.8 3.8 %collective-permute-start.45 = (bf16[128,1024]{1,0:T(8,128)(2,1)S(1)}, bf16[128,1024]{1,0:T(8,128)(2,1)}, u32[]{:S(2)}, u32[]{:S(2)}) collective-permute-start(bf16[128,1024]{1,0:T(8,128)(2,1)S(1)} %get-tuple-element.140), channel_id=1, source_target_pairs={{0,3},{1,0},{2,1},{3,2},{4,7},{5,4},{6,5},{7,6},{8,11},{9,8},{10,9... | collective-permute-start | bytes 786440 | tf_op jit(solution)/shard_map/ppermute | solution.py:16
  158.8 4.3 %out_grad.1 = (f32[128,1024]{1,0:T(8,128)S(1)}, bf16[128,1024]{1,0:T(8,128)(2,1)S(1)}, bf16[128,1024]{1,0:T(8,128)(2,1)S(1)}, bf16[128,1024]{1,0:T(8,128)(2,1)S(1)}) custom-call(s32[13]{0:T(128)S(1)} %concatenate.15.refs_0_.place, bf16[4,128,1024]{2,1,0:T(8,128)(2,1)} %get-tuple-element.132.in0.refs_4_, ...), custom_call_target="tpu_custom_call" | custom-call | flops 1073741824 | bytes 4456448 | tf_op jit(solution)/shard_map/out_grad/pallas_call | solution.py:353
  165.2 5.0 %last_back.1 = (bf16[4,128,1024]{2,1,0:T(8,128)(2,1)S(1)}, bf16[4,128,1024]{2,1,0:T(8,128)(2,1)S(1)}) custom-call(s32[13]{0:T(128)S(1)} %concatenate.15.refs_0_.place, bf16[8,128,2048]{2,1,0:T(8,128)(2,1)} %bitcast.50, bf16[4,128,1024]{2,1,0:T(8,128)(2,1)S(1)} %collective-permute-done.2.refs_2_, f32[2,2048]{1,0:T(2,128)S(1)} %copy-done.4, ...), custom_call_target="tpu_custom_call" | custom-call | flops 1073741824 | bytes 12861440 | tf_op jit(solution)/shard_map/last_back/pallas_call | solution.py:353
  170.2 3.3 %in_grad.3 = (f32[128,1024]{1,0:T(8,128)S(1)}, bf16[128,1024]{1,0:T(8,128)(2,1)S(1)}, bf16[128,1024]{1,0:T(8,128)(2,1)S(1)}, bf16[128,1024]{1,0:T(8,128)(2,1)S(1)}) custom-call(s32[13]{0:T(128)S(1)} %concatenate.15.refs_0_.place, bf16[8,128,2048]{2,1,0:T(8,128)(2,1)S(1)} %bitcast.54, bf16[4,128,1024]{2,1,0:T(8,128)(2,1)S(1)} %collective-permute-done.2.refs_2_, ...), custom_call_target="tpu_custom_call" | custom-call | flops 1073741824 | bytes 7880704 | tf_op jit(solution)/shard_map/in_grad/pallas_call | solution.py:353
  175.7 3.8 %collective-permute-start.55 = (bf16[128,1024]{1,0:T(8,128)(2,1)S(1)}, bf16[128,1024]{1,0:T(8,128)(2,1)S(1)}, u32[]{:S(2)}, u32[]{:S(2)}) collective-permute-start(bf16[128,1024]{1,0:T(8,128)(2,1)S(1)} %get-tuple-element.150), channel_id=1, source_target_pairs={{0,3},{1,0},{2,1},{3,2},{4,7},{5,4},{6,5},{7,6},{8,11},{9,8},{10,9... | collective-permute-start | bytes 786440 | tf_op jit(solution)/shard_map/ppermute | solution.py:16
  181.5 5.2 %collective-permute-done.54 = bf16[128,1024]{1,0:T(8,128)(2,1)S(1)} collective-permute-done((bf16[128,1024]{1,0:T(8,128)(2,1)S(1)}, bf16[128,1024]{1,0:T(8,128)(2,1)S(1)}, u32[]{:S(2)}, u32[]{:S(2)}) %collective-permute-start.54) | collective-permute-done | bytes 262176 | tf_op jit(solution)/shard_map/ppermute | solution.py:16
  186.7 3.9 %collective-permute-done.55 = bf16[128,1024]{1,0:T(8,128)(2,1)S(1)} collective-permute-done((bf16[128,1024]{1,0:T(8,128)(2,1)S(1)}, bf16[128,1024]{1,0:T(8,128)(2,1)S(1)}, u32[]{:S(2)}, u32[]{:S(2)}) %collective-permute-start.55) | collective-permute-done | bytes 262176 | tf_op jit(solution)/shard_map/ppermute | solution.py:16
  193.0 3.7 %collective-permute-done.46.hop0 = bf16[64,1024]{1,0:T(8,128)(2,1)S(1)} collective-permute-done((bf16[64,1024]{1,0:T(8,128)(2,1)S(1)}, bf16[64,1024]{1,0:T(8,128)(2,1)S(1)}, u32[]{:S(2)}, u32[]{:S(2)}) %collective-permute-start.46) | collective-permute-done | bytes 131104 | tf_op jit(solution)/shard_map/ppermute | solution.py:16
  196.9 3.8 %collective-permute-start.49 = (bf16[128,1024]{1,0:T(8,128)(2,1)S(1)}, bf16[128,1024]{1,0:T(8,128)(2,1)S(1)}, u32[]{:S(2)}, u32[]{:S(2)}) collective-permute-start(bf16[128,1024]{1,0:T(8,128)(2,1)S(1)} %get-tuple-element.143), channel_id=1, source_target_pairs={{0,3},{1,0},{2,1},{3,2},{4,7},{5,4},{6,5},{7,6},{8,11},{9,8},{10,9... | collective-permute-start | bytes 786440 | tf_op jit(solution)/shard_map/ppermute | solution.py:16
  200.8 7.1 %collective-permute-done.48 = bf16[128,1024]{1,0:T(8,128)(2,1)S(1)} collective-permute-done((bf16[128,1024]{1,0:T(8,128)(2,1)S(1)}, bf16[128,1024]{1,0:T(8,128)(2,1)S(1)}, u32[]{:S(2)}, u32[]{:S(2)}) %collective-permute-start.48) | collective-permute-done | bytes 262176 | tf_op jit(solution)/shard_map/ppermute | solution.py:16
  (162 shorter events, 105.5 us)
Async XLA Ops:
  11.9 46.0 %collective-permute-start.3 = (bf16[4,128,1024]{2,1,0:T(8,128)(2,1)}, bf16[4,128,1024]{2,1,0:T(8,128)(2,1)S(1)}, u32[]{:S(2)}, u32[]{:S(2)}) collective-permute-start(bf16[4,128,1024]{2,1,0:T(8,128)(2,1)} %get-tuple-element.79), channel_id=1, source_target_pairs={{0,16},{16,0},{1,17},{17,1},{2,18},{18,2},{3,19},{19,3},{4,20},{20... | collective-permute-start | bytes 3145736 | tf_op jit(solution)/shard_map/ppermute | solution.py:35
  21.2 15.0 %collective-permute-start.5 = (bf16[1024,128]{1,0:T(8,128)(2,1)S(1)}, bf16[1024,128]{1,0:T(8,128)(2,1)}, u32[]{:S(2)}, u32[]{:S(2)}) collective-permute-start(bf16[1024,128]{1,0:T(8,128)(2,1)S(1)} %get-tuple-element.158.refs_9_), channel_id=1, source_target_pairs={{0,3},{1,0},{2,1},{3,2},{4,7},{5,4},{6,5},{7,6},{8,11},{9,8},{10,9... | collective-permute-start | bytes 786440 | tf_op jit(solution)/shard_map/ppermute | solution.py:16
  23.3 17.7 %collective-permute-start.1 = (bf16[1024,128]{1,0:T(8,128)(2,1)S(1)}, bf16[1024,128]{1,0:T(8,128)(2,1)S(1)}, u32[]{:S(2)}, u32[]{:S(2)}) collective-permute-start(bf16[1024,128]{1,0:T(8,128)(2,1)S(1)} %get-tuple-element.158.refs_9_), channel_id=1, source_target_pairs={{0,1},{1,2},{2,3},{3,0},{4,5},{5,6},{6,7},{7,4},{8,9},{9,10},{10,1... | collective-permute-start | bytes 786440 | tf_op jit(solution)/shard_map/ppermute | solution.py:16
  23.3 24.1 %collective-permute-start.11 = (bf16[1024,128]{1,0:T(8,128)(2,1)S(1)}, bf16[1024,128]{1,0:T(8,128)(2,1)S(1)}, u32[]{:S(2)}, u32[]{:S(2)}) collective-permute-start(bf16[1024,128]{1,0:T(8,128)(2,1)S(1)} %get-tuple-element.156.refs_5_.refs_7_), channel_id=1, source_target_pairs={{0,3},{1,0},{2,1},{3,2},{4,7},{5,4},{6,5},{7,6},{8,11},{9,8},{10,9... | collective-permute-start | bytes 786440 | tf_op jit(solution)/shard_map/ppermute | solution.py:16
  29.7 22.5 %collective-permute-start.13 = (bf16[1024,128]{1,0:T(8,128)(2,1)S(1)}, bf16[1024,128]{1,0:T(8,128)(2,1)S(1)}, u32[]{:S(2)}, u32[]{:S(2)}) collective-permute-start(bf16[1024,128]{1,0:T(8,128)(2,1)S(1)} %collective-permute-done.12.refs_8_.refs_10_), channel_id=1, source_target_pairs={{0,1},{1,2},{2,3},{3,0},{4,5},{5,6},{6,7},{7,4},{8,9},{9,10},{10,1... | collective-permute-start | bytes 786440 | tf_op jit(solution)/shard_map/ppermute | solution.py:16
  36.3 21.6 %collective-permute-start.14 = (bf16[1024,128]{1,0:T(8,128)(2,1)}, bf16[1024,128]{1,0:T(8,128)(2,1)}, u32[]{:S(2)}, u32[]{:S(2)}) collective-permute-start(bf16[1024,128]{1,0:T(8,128)(2,1)} %collective-permute-done.5.refs_10_), channel_id=1, source_target_pairs={{0,3},{1,0},{2,1},{3,2},{4,7},{5,4},{6,5},{7,6},{8,11},{9,8},{10,9... | collective-permute-start | bytes 786440 | tf_op jit(solution)/shard_map/ppermute | solution.py:16
  41.7 28.7 %collective-permute-start.2 = (bf16[4,128,1024]{2,1,0:T(8,128)(2,1)}, bf16[4,128,1024]{2,1,0:T(8,128)(2,1)S(1)}, u32[]{:S(2)}, u32[]{:S(2)}) collective-permute-start(bf16[4,128,1024]{2,1,0:T(8,128)(2,1)} %get-tuple-element.78), channel_id=1, source_target_pairs={{0,16},{16,0},{1,17},{17,1},{2,18},{18,2},{3,19},{19,3},{4,20},{20... | collective-permute-start | bytes 3145736 | tf_op jit(solution)/shard_map/ppermute | solution.py:35
  47.4 22.7 %collective-permute-start.7 = (bf16[2,1024,128]{2,1,0:T(8,128)(2,1)S(1)}, bf16[2,1024,128]{2,1,0:T(8,128)(2,1)S(1)}, u32[]{:S(2)}, u32[]{:S(2)}) collective-permute-start(bf16[2,1024,128]{2,1,0:T(8,128)(2,1)S(1)} %maximum_select_fusion.2.refs_4_.refs_11_.refs_8_), channel_id=1, source_target_pairs={{0,1},{1,2},{2,3},{3,0},{4,5},{5,6},{6,7},{7,4},{8,9},{9,10},{10,1... | collective-permute-start | bytes 1572872 | tf_op jit(solution)/shard_map/ppermute | solution.py:16
  68.3 14.7 %collective-permute-start.6 = (bf16[2,1024,128]{2,1,0:T(8,128)(2,1)S(1)}, bf16[2,1024,128]{2,1,0:T(8,128)(2,1)S(1)}, u32[]{:S(2)}, u32[]{:S(2)}) collective-permute-start(bf16[2,1024,128]{2,1,0:T(8,128)(2,1)S(1)} %maximum_select_fusion.2.refs_4_.refs_11_.refs_8_), channel_id=1, source_target_pairs={{0,3},{1,0},{2,1},{3,2},{4,7},{5,4},{6,5},{7,6},{8,11},{9,8},{10,9... | collective-permute-start | bytes 1572872 | tf_op jit(solution)/shard_map/ppermute | solution.py:16
  70.1 21.6 %collective-permute-start.8 = (bf16[1024,128]{1,0:T(8,128)(2,1)S(1)}, bf16[1024,128]{1,0:T(8,128)(2,1)S(1)}, u32[]{:S(2)}, u32[]{:S(2)}) collective-permute-start(bf16[1024,128]{1,0:T(8,128)(2,1)S(1)} %slice_bitcast_fusion.1), channel_id=1, source_target_pairs={{0,1},{1,2},{2,3},{3,0},{4,5},{5,6},{6,7},{7,4},{8,9},{9,10},{10,1... | collective-permute-start | bytes 786440 | tf_op jit(solution)/shard_map/ppermute | solution.py:16
  70.9 15.9 %collective-permute-start.17 = (bf16[128,1152]{1,0:T(8,128)(2,1)S(1)}, bf16[128,1152]{1,0:T(8,128)(2,1)S(1)}, u32[]{:S(2)}, u32[]{:S(2)}) collective-permute-start(bf16[128,1152]{1,0:T(8,128)(2,1)S(1)} %get-tuple-element.89), channel_id=1, source_target_pairs={{0,8},{4,12},{8,0},{12,4},{1,9},{5,13},{9,1},{13,5},{2,10},{6,14},... | collective-permute-start | bytes 884744 | tf_op jit(solution)/shard_map/ppermute | solution.py:43
  72.7 15.1 %collective-permute-start.18 = (bf16[128,1152]{1,0:T(8,128)(2,1)S(1)}, bf16[128,1152]{1,0:T(8,128)(2,1)S(1)}, u32[]{:S(2)}, u32[]{:S(2)}) collective-permute-start(bf16[128,1152]{1,0:T(8,128)(2,1)S(1)} %get-tuple-element.90), channel_id=1, source_target_pairs={{0,16},{16,0},{1,17},{17,1},{2,18},{18,2},{3,19},{19,3},{4,20},{20... | collective-permute-start | bytes 884744 | tf_op jit(solution)/shard_map/ppermute | solution.py:35
  74.2 13.6 %collective-permute-start.19 = (bf16[128,1152]{1,0:T(8,128)(2,1)S(1)}, bf16[128,1152]{1,0:T(8,128)(2,1)S(1)}, u32[]{:S(2)}, u32[]{:S(2)}) collective-permute-start(bf16[128,1152]{1,0:T(8,128)(2,1)S(1)} %get-tuple-element.91), channel_id=1, source_target_pairs={{0,24},{4,28},{8,16},{12,20},{16,8},{20,12},{24,0},{28,4},{1,25},{... | collective-permute-start | bytes 884744 | tf_op jit(solution)/shard_map/ppermute | solution.py:47
  98.8 19.2 %collective-permute-start.24 = (bf16[128,1152]{1,0:T(8,128)(2,1)S(1)}, bf16[128,1152]{1,0:T(8,128)(2,1)S(1)}, u32[]{:S(2)}, u32[]{:S(2)}) collective-permute-start(bf16[128,1152]{1,0:T(8,128)(2,1)S(1)} %get-tuple-element.102), channel_id=1, source_target_pairs={{0,8},{4,12},{8,0},{12,4},{1,9},{5,13},{9,1},{13,5},{2,10},{6,14},... | collective-permute-start | bytes 884744 | tf_op jit(solution)/shard_map/ppermute | solution.py:43
  100.6 17.4 %collective-permute-start.25 = (bf16[128,1152]{1,0:T(8,128)(2,1)S(1)}, bf16[128,1152]{1,0:T(8,128)(2,1)S(1)}, u32[]{:S(2)}, u32[]{:S(2)}) collective-permute-start(bf16[128,1152]{1,0:T(8,128)(2,1)S(1)} %get-tuple-element.103), channel_id=1, source_target_pairs={{0,16},{16,0},{1,17},{17,1},{2,18},{18,2},{3,19},{19,3},{4,20},{20... | collective-permute-start | bytes 884744 | tf_op jit(solution)/shard_map/ppermute | solution.py:35
  102.1 15.9 %collective-permute-start.26 = (bf16[128,1152]{1,0:T(8,128)(2,1)S(1)}, bf16[128,1152]{1,0:T(8,128)(2,1)S(1)}, u32[]{:S(2)}, u32[]{:S(2)}) collective-permute-start(bf16[128,1152]{1,0:T(8,128)(2,1)S(1)} %get-tuple-element.104), channel_id=1, source_target_pairs={{0,24},{4,28},{8,16},{12,20},{16,8},{20,12},{24,0},{28,4},{1,25},{... | collective-permute-start | bytes 884744 | tf_op jit(solution)/shard_map/ppermute | solution.py:47
  120.1 14.0 %collective-permute-start.32 = (bf16[128,1024]{1,0:T(8,128)(2,1)S(1)}, bf16[128,1024]{1,0:T(8,128)(2,1)S(1)}, u32[]{:S(2)}, u32[]{:S(2)}) collective-permute-start(bf16[128,1024]{1,0:T(8,128)(2,1)S(1)} %get-tuple-element.118), channel_id=1, source_target_pairs={{0,3},{1,0},{2,1},{3,2},{4,7},{5,4},{6,5},{7,6},{8,11},{9,8},{10,9... | collective-permute-start | bytes 786440 | tf_op jit(solution)/shard_map/ppermute | solution.py:16
  142.8 16.0 %collective-permute-start.36 = (bf16[2,2,128,512]{3,2,1,0:T(8,128)(2,1)S(1)}, bf16[2,2,128,512]{3,2,1,0:T(8,128)(2,1)S(1)}, u32[]{:S(2)}, u32[]{:S(2)}) collective-permute-start(bf16[2,2,128,512]{3,2,1,0:T(8,128)(2,1)S(1)} %get-tuple-element.123.p0), channel_id=1, source_target_pairs={{0,4},{4,0},{8,12},{12,8},{1,5},{5,1},{9,13},{13,9},{2,6},{6,2},{1... | collective-permute-start | bytes 1572872 | tf_op jit(solution)/shard_map/ppermute | solution.py:39
  153.7 26.4 %collective-permute-start.44 = (bf16[128,1024]{1,0:T(8,128)(2,1)S(1)}, bf16[128,1024]{1,0:T(8,128)(2,1)S(1)}, u32[]{:S(2)}, u32[]{:S(2)}) collective-permute-start(bf16[128,1024]{1,0:T(8,128)(2,1)S(1)} %get-tuple-element.139), channel_id=1, source_target_pairs={{0,1},{1,2},{2,3},{3,0},{4,5},{5,6},{6,7},{7,4},{8,9},{9,10},{10,1... | collective-permute-start | bytes 786440 | tf_op jit(solution)/shard_map/ppermute | solution.py:16
  153.8 27.6 %collective-permute-start.45 = (bf16[128,1024]{1,0:T(8,128)(2,1)S(1)}, bf16[128,1024]{1,0:T(8,128)(2,1)}, u32[]{:S(2)}, u32[]{:S(2)}) collective-permute-start(bf16[128,1024]{1,0:T(8,128)(2,1)S(1)} %get-tuple-element.140), channel_id=1, source_target_pairs={{0,3},{1,0},{2,1},{3,2},{4,7},{5,4},{6,5},{7,6},{8,11},{9,8},{10,9... | collective-permute-start | bytes 786440 | tf_op jit(solution)/shard_map/ppermute | solution.py:16
  157.6 35.4 %collective-permute-start.43 = (bf16[4,128,1024]{2,1,0:T(8,128)(2,1)}, bf16[4,128,1024]{2,1,0:T(8,128)(2,1)S(1)}, u32[]{:S(2)}, u32[]{:S(2)}) collective-permute-start(bf16[4,128,1024]{2,1,0:T(8,128)(2,1)} %get-tuple-element.132.in0.refs_4_), channel_id=1, source_target_pairs={{0,16},{16,0},{1,17},{17,1},{2,18},{18,2},{3,19},{19,3},{4,20},{20... | collective-permute-start | bytes 3145736 | tf_op jit(solution)/shard_map/ppermute | solution.py:35
  175.7 14.9 %collective-permute-start.55 = (bf16[128,1024]{1,0:T(8,128)(2,1)S(1)}, bf16[128,1024]{1,0:T(8,128)(2,1)S(1)}, u32[]{:S(2)}, u32[]{:S(2)}) collective-permute-start(bf16[128,1024]{1,0:T(8,128)(2,1)S(1)} %get-tuple-element.150), channel_id=1, source_target_pairs={{0,3},{1,0},{2,1},{3,2},{4,7},{5,4},{6,5},{7,6},{8,11},{9,8},{10,9... | collective-permute-start | bytes 786440 | tf_op jit(solution)/shard_map/ppermute | solution.py:16
  180.2 31.1 %collective-permute-start.51 = (bf16[4,128,1024]{2,1,0:T(8,128)(2,1)S(1)}, bf16[4,128,1024]{2,1,0:T(8,128)(2,1)S(1)}, u32[]{:S(2)}, u32[]{:S(2)}) collective-permute-start(bf16[4,128,1024]{2,1,0:T(8,128)(2,1)S(1)} %get-tuple-element.128), channel_id=1, source_target_pairs={{0,16},{16,0},{1,17},{17,1},{2,18},{18,2},{3,19},{19,3},{4,20},{20... | collective-permute-start | bytes 3145736 | tf_op jit(solution)/shard_map/ppermute | solution.py:35
  191.8 19.5 %collective-permute-start.56 = (bf16[128,1024]{1,0:T(8,128)(2,1)S(1)}, bf16[128,1024]{1,0:T(8,128)(2,1)S(1)}, u32[]{:S(2)}, u32[]{:S(2)}) collective-permute-start(bf16[128,1024]{1,0:T(8,128)(2,1)S(1)} %get-tuple-element.162), channel_id=1, source_target_pairs={{0,16},{16,0},{1,17},{17,1},{2,18},{18,2},{3,19},{19,3},{4,20},{20... | collective-permute-start | bytes 786440 | tf_op jit(solution)/shard_map/ppermute | solution.py:35
  (46 other events, 492.9 us)
